TPU v7x, 128 devices: a whole 4x4x4 slice. The times are simulated.
128 devices in a mesh: seq: 8 (over x, core), res: 16 (over z, y).
Axes of the slice: x: 4, y: 4, z: 4, core: 2. Of those that a mesh axis runs over, the one named last changes fastest.
Arguments:
- normed: bfloat16 [512, 256, 768], P('seq', 'res'), may hold values from -8 to 8
- cotangent: bfloat16 [512, 256, 768], P('seq', 'res'), may hold values from -40 to 40
- w_query: bfloat16 [768, 768], replicated, may hold values from -0.16237976 to 0.16237976
- w_key: bfloat16 [768, 768], replicated, may hold values from -0.16237976 to 0.16237976
- w_value: bfloat16 [768, 768], replicated, may hold values from -0.21875 to 0.21875
- w_out: bfloat16 [768, 768], replicated, may hold values from -0.21875 to 0.21875
Outputs:
- input_grad: bfloat16 [512, 256, 768], P('seq', 'res')
All inputs are finite; a program needn't handle non-finite values.
Results may differ from a plain program's by a relative error of at most 0.0085.
Values may be sent and summed in bfloat16 or wider, within the bound.
No kernel may reach another device: no remote copies, remote signals or barrier semaphores. Data moves between devices by JAX's collectives and lax.ppermute only.
A program may use at most 64 MiB of HBM per device.

v0:
```python
import math

import jax
import jax.numpy as jnp
from jax import lax
from jax.sharding import PartitionSpec as P

HEADS = 12


def softmax_backward(tied_logit, prob_grad, scaling):
    row_max = jnp.max(tied_logit, axis=-1, keepdims=True)
    exponent = jnp.exp(tied_logit - row_max)
    attn_prob = (exponent / jnp.sum(exponent, axis=-1, keepdims=True)).astype(jnp.bfloat16)
    weights = attn_prob.astype(jnp.float32)
    row_dot = jnp.sum(weights * prob_grad, axis=-1, keepdims=True)
    logit_grad = (scaling * weights * (prob_grad - row_dot)).astype(jnp.bfloat16)
    return (attn_prob, logit_grad)


def body(normed, cotangent, w_query, w_key, w_value, w_out):
    row_input, row_cotangent = (
        lax.all_to_all(normed, "res", split_axis=0, concat_axis=1, tiled=True),
        lax.all_to_all(cotangent, "res", split_axis=0, concat_axis=1, tiled=True),
    )
    seq_count, res_len, model_width = row_input.shape
    head_size = model_width // HEADS
    devices_count = lax.axis_size("seq") * lax.axis_size("res")
    scaling = 1.0 / math.sqrt(head_size * seq_count * devices_count)
    flat_input = row_input.reshape(seq_count * res_len, model_width)

    def project(matrix):
        product = jnp.dot(flat_input, matrix, preferred_element_type=jnp.float32)
        return product.astype(jnp.bfloat16).reshape(seq_count, res_len, HEADS, head_size)

    query_rows = project(w_query)
    key_rows = project(w_key)
    value_rows = project(w_value)
    out_grad = jnp.einsum(
        "td,ed->te",
        row_cotangent.reshape(seq_count * res_len, model_width),
        w_out,
        preferred_element_type=jnp.float32,
    )
    out_grad = out_grad.astype(jnp.bfloat16).reshape(seq_count, res_len, HEADS, head_size)
    tied_logit = scaling * jnp.einsum(
        "sihe,sjhe->ihj", query_rows, key_rows, preferred_element_type=jnp.float32
    )
    prob_grad = jnp.einsum(
        "sihe,sjhe->ihj", out_grad, value_rows, preferred_element_type=jnp.float32
    )
    logit_term = tied_logit
    prob_term = prob_grad
    tied_logit, prob_grad = lax.psum((logit_term, prob_term), ("seq", "res"))
    attn_prob, logit_grad = softmax_backward(tied_logit, prob_grad, scaling)
    query_grad = jnp.einsum(
        "ihj,sjhe->sihe", logit_grad, key_rows, preferred_element_type=jnp.float32
    ).astype(jnp.bfloat16)
    key_grad = jnp.einsum(
        "ihj,sihe->sjhe", logit_grad, query_rows, preferred_element_type=jnp.float32
    ).astype(jnp.bfloat16)
    value_grad = jnp.einsum(
        "ihj,sihe->sjhe", attn_prob, out_grad, preferred_element_type=jnp.float32
    ).astype(jnp.bfloat16)
    token_count = seq_count * res_len
    total = jnp.einsum(
        "to,io->ti",
        query_grad.reshape(token_count, model_width),
        w_query,
        preferred_element_type=jnp.float32,
    )
    total = total + jnp.einsum(
        "to,io->ti",
        key_grad.reshape(token_count, model_width),
        w_key,
        preferred_element_type=jnp.float32,
    )
    total = total + jnp.einsum(
        "to,io->ti",
        value_grad.reshape(token_count, model_width),
        w_value,
        preferred_element_type=jnp.float32,
    )
    row_result = total.astype(jnp.bfloat16).reshape(seq_count, res_len, model_width)
    return lax.all_to_all(row_result, "res", split_axis=1, concat_axis=0, tiled=True)


def solution(mesh):
    in_specs = (P("seq", "res", None), P("seq", "res", None), P(), P(), P(), P())
    out_specs = P("seq", "res", None)
    return jax.shard_map(body, mesh=mesh, in_specs=in_specs, out_specs=out_specs, check_vma=False)
```

profile of v0, /device:TPU:2, one launch (start us, length us, event | category | flops | bytes accessed | tf_op | source)
XLA Modules:
  0.0 332.1 jit_solution(8406903469781259566)
XLA Ops:
  6.5 0.0 copy-start
  6.5 31.1 %all_to_all.48 = bf16[64,16,768]{2,1,0:T(8,128)(2,1)} all-to-all(bf16[64,16,768]{2,1,0:T(8,128)(2,1)} %param.6), channel_id=1, replica_groups=mesh['seq'=8,'res'=16] {'res'}, dimensions={0} | all-to-all | bytes 3145728 | tf_op jit(solution)/shard_map/all_to_all | solution.py:23
  37.6 3.7 %all-to-all-start.1 = ((bf16[64,16,768]{2,1,0:T(8,128)(2,1)}), bf16[64,16,768]{2,1,0:T(8,128)(2,1)S(1)}, u32[]{:S(2)}, u32[]{:S(2)}) async-start(bf16[64,16,768]{2,1,0:T(8,128)(2,1)} %param.7), calls=%async_computation.1 | async-start | bytes 3145728 | tf_op jit(solution)/shard_map/all_to_all | solution.py:24
  41.3 0.0 all-reduce.3.cloned.1.call-start
  41.4 2.7 copy.56
  44.1 19.7 %all-to-all-done.1 = bf16[64,16,768]{2,1,0:T(8,128)(2,1)S(1)} async-done(((bf16[64,16,768]{2,1,0:T(8,128)(2,1)}), bf16[64,16,768]{2,1,0:T(8,128)(2,1)S(1)}, u32[]{:S(2)}, u32[]{:S(2)}) %all-to-all-start.1) | async-done | bytes 1572896 | tf_op jit(solution)/shard_map/all_to_all | solution.py:24
  63.8 0.0 copy-start.7
  63.8 0.1 copy.62
  63.9 1.1 copy-done.7
  65.1 1.4 convolution_convert_fusion.3
  66.5 1.6 copy.63
  68.2 2.9 reshape.40
  71.0 4.3 %convolution_convert_fusion.4 = bf16[1024,768]{1,0:T(8,128)(2,1)} fusion(bf16[1024,768]{1,0:T(8,128)(2,1)} %bitcast.96, bf16[768,768]{1,0:T(8,128)(2,1)} %param.10), kind=kOutput, calls=%fused_computation.17 | convolution fusion | flops 1208745984 | bytes 4325376 | tf_op jit(solution)/shard_map/dot_general | solution.py:33
  75.4 2.6 copy.61
  77.9 3.9 %reshape.38 = bf16[4,256,12,64]{1,0,3,2:T(4,128)(2,1)} reshape(bf16[1024,768]{0,1:T(8,128)(2,1)} %copy.61) | data formatting | bytes 3145728 | tf_op jit(solution)/shard_map/reshape | solution.py:34
  81.8 0.0 copy-start.3
  81.8 4.4 %convolution_convert_fusion.5 = bf16[1024,768]{1,0:T(8,128)(2,1)} fusion(bf16[1024,768]{1,0:T(8,128)(2,1)} %bitcast.97, bf16[768,768]{1,0:T(8,128)(2,1)} %param.8), kind=kOutput, calls=%fused_computation.18 | convolution fusion | flops 1208745984 | bytes 4325376 | tf_op jit(solution)/shard_map/dot_general | solution.py:33
  86.2 0.0 copy-done
  86.2 0.0 copy-done.3
  86.2 2.5 convolution_convert_fusion.6
  88.8 2.6 copy.57
  91.4 3.9 %reshape.36 = bf16[4,256,12,64]{1,0,3,2:T(4,128)(2,1)} reshape(bf16[1024,768]{0,1:T(8,128)(2,1)} %copy.57) | data formatting | bytes 3145728 | tf_op jit(solution)/shard_map/reshape | solution.py:34
  95.2 2.6 copy.58
  97.8 3.8 %reshape.37 = bf16[4,256,12,64]{1,0,3,2:T(4,128)(2,1)} reshape(bf16[1024,768]{0,1:T(8,128)(2,1)} %copy.58) | data formatting | bytes 3145728 | tf_op jit(solution)/shard_map/reshape | solution.py:34
  101.6 0.0 copy-start.1
  101.7 0.0 copy-start.2
  101.7 3.9 %convolution_bitcast_fusion = f32[256,12,256]{0,2,1:T(8,128)} fusion(bf16[4,256,12,64]{1,0,3,2:T(4,128)(2,1)} %reshape.38, bf16[4,256,12,64]{1,0,3,2:T(4,128)(2,1)S(1)} %reshape.40), kind=kOutput, calls=%fused_computation.12 | convolution fusion | flops 402653184 | bytes 6291456 | tf_op jit(solution)/shard_map/sihe,sjhe->ihj/dot_general | solution.py:49
  105.5 0.0 copy-done.1
  105.6 0.0 copy-done.2
  105.6 2.4 fusion.4
  107.9 0.0 all-reduce.3.cloned.1.call-update
  108.0 155.4 %all-reduce.3.cloned.1.call-done = (f32[256,12,256]{0,2,1:T(8,128)}, f32[256,12,256]{0,2,1:T(8,128)}) async-done(((f32[256,12,256]{0,2,1:T(8,128)}, f32[256,12,256]{0,2,1:T(8,128)}), (f32[256,12,256]{0,2,1:T(8,128)}, f32[256,12,256]{0,2,1:T(8,128)})) %all-reduce.3.cloned.1.call-update) | async-done | bytes 6291472 | tf_op jit(solution)/shard_map/psum | solution.py:54
  263.3 3.4 %fusion.31 = (f32[256,12]{0,1:T(8,128)S(1)}, f32[256,12,256]{0,2,1:T(8,128)S(1)}) fusion(f32[256,12,256]{0,2,1:T(8,128)} %get-tuple-element.6), kind=kOutput, calls=%fused_computation.39 | output fusion | flops 1573119 | bytes 6303744 | tf_op jit(solution)/shard_map/sub | solution.py:13
  266.7 1.5 divide_convert_fusion
  268.2 6.5 %fusion.18 = bf16[4,256,12,64]{1,3,0,2:T(8,128)(2,1)} fusion(f32[256,12,256]{0,2,1:T(8,128)} %get-tuple-element.5, bf16[256,12,256]{0,2,1:T(8,128)(2,1)} %divide_convert_fusion, bf16[4,256,12,64]{1,0,3,2:T(4,128)(2,1)} %reshape.37), kind=kOutput, calls=%fused_computation.28 | convolution fusion | flops 408947968 | bytes 7864320 | tf_op jit(solution)/shard_map/ihj,sihe->sjhe/dot_general | solution.py:59
  274.7 6.5 %fusion.15 = bf16[4,256,12,64]{1,3,0,2:T(8,128)(2,1)} fusion(f32[256,12,256]{0,2,1:T(8,128)} %get-tuple-element.5, bf16[256,12,256]{0,2,1:T(8,128)(2,1)} %divide_convert_fusion, bf16[4,256,12,64]{1,0,3,2:T(4,128)(2,1)} %reshape.36), kind=kOutput, calls=%fused_computation.27 | convolution fusion | flops 408947968 | bytes 7864320 | tf_op jit(solution)/shard_map/ihj,sjhe->sihe/dot_general | solution.py:56
  281.2 2.0 fusion.12
  283.3 1.2 copy.74
  284.5 0.0 copy-start.5
  284.5 0.3 copy.90
  284.8 1.0 copy-done.5
  285.9 1.2 copy.68
  287.1 0.0 copy-start.4
  287.1 0.3 copy.88
  287.5 1.0 copy-done.4
  288.5 1.2 copy.71
  289.8 0.3 copy.89
  290.1 0.0 copy-start.8
  290.1 1.5 fusion.33
  291.6 0.0 copy-done.8
  291.6 0.0 copy-start.6
  291.6 1.7 fusion.32
  293.3 0.0 copy-done.6
  293.3 1.5 add_convert_fusion
  294.8 1.2 copy.75
  296.1 27.8 %all_to_all.49 = bf16[4,256,768]{2,0,1:T(4,128)(2,1)S(1)} all-to-all(bf16[4,256,768]{2,0,1:T(4,128)(2,1)S(1)} %copy.75), channel_id=1, replica_groups=mesh['seq'=8,'res'=16] {'res'}, dimensions={1} | all-to-all | bytes 3145728 | tf_op jit(solution)/shard_map/all_to_all | solution.py:85
  323.8 1.4 copy.76
Async XLA Ops:
  6.5 79.7 %copy-start = (bf16[768,768]{1,0:T(8,128)(2,1)S(1)}, bf16[768,768]{1,0:T(8,128)(2,1)}, u32[]{:S(2)}) copy-start(bf16[768,768]{1,0:T(8,128)(2,1)} %param.9) | copy-start | bytes 3538948
  37.6 26.2 %all-to-all-start.1 = ((bf16[64,16,768]{2,1,0:T(8,128)(2,1)}), bf16[64,16,768]{2,1,0:T(8,128)(2,1)S(1)}, u32[]{:S(2)}, u32[]{:S(2)}) async-start(bf16[64,16,768]{2,1,0:T(8,128)(2,1)} %param.7), calls=%async_computation.1 | async-start | bytes 3145728 | tf_op jit(solution)/shard_map/all_to_all | solution.py:24
  41.3 222.0 %all-reduce.3.cloned.1.call-start = ((), (), s32[]{:S(2)}) async-start(), calls=%async_computation.3 | async-start | bytes 12582912 | tf_op jit(solution)/shard_map/psum | solution.py:54
  63.8 1.3 copy-start.7
  81.8 4.4 %copy-start.3 = (bf16[4,16,16,768]{3,2,1,0:T(8,128)(2,1)S(1)}, bf16[4,16,16,768]{3,2,1,0:T(8,128)(2,1)}, u32[]{:S(2)}) copy-start(bf16[4,16,16,768]{3,2,1,0:T(8,128)(2,1)} %copy.56) | copy-start | bytes 4718596
  101.6 3.9 %copy-start.1 = (bf16[4,256,12,64]{1,0,3,2:T(4,128)(2,1)S(1)}, bf16[4,256,12,64]{1,0,3,2:T(4,128)(2,1)}, u32[]{:S(2)}) copy-start(bf16[4,256,12,64]{1,0,3,2:T(4,128)(2,1)} %reshape.36) | copy-start | bytes 4718596
  101.7 3.9 %copy-start.2 = (bf16[4,256,12,64]{1,0,3,2:T(4,128)(2,1)S(1)}, bf16[4,256,12,64]{1,0,3,2:T(4,128)(2,1)}, u32[]{:S(2)}) copy-start(bf16[4,256,12,64]{1,0,3,2:T(4,128)(2,1)} %reshape.37) | copy-start | bytes 4718596
  284.5 1.4 copy-start.5
  287.1 1.4 copy-start.4
  290.1 1.5 copy-start.8
  291.6 1.7 copy-start.6
Sparse Core Ops, SparseCore 0:
  108.1 155.1 all-reduce.2
where the time goes:
time: 334 us; the launch traced here: 332 us
  waiting for transfers between devices  175 us (52%)
  blocking collectives  58.8 us (18%)
  matrix products  38.6 us (12%)
  local copies, waits for them, and re-layouts  37.3 us (11%)
  between operations  13.6 us (4%)
  other arithmetic  4.92 us (1%)
  starting transfers between devices  3.75 us (1%)
    psum x1, waiting for transfers between devices, body(): tied_logit, prob_grad = lax.psum((logit_term, prob_term), ('seq', 'res'))  155 us
    all_to_all x1, blocking collectives, body(): lax.all_to_all(normed, 'res', split_axis=0, concat_axis=1, tiled=True)  31.1 us
    all_to_all x1, blocking collectives, body(): lax.all_to_all(row_result, 'res', split_axis=1, concat_axis=0, tiled=True)  27.8 us
    all_to_all x1, waiting for transfers between devices, body(): lax.all_to_all(cotangent, 'res', split_axis=0, concat_axis=1, tiled=True)  19.7 us
    reshape x3, local copies, waits for them, and re-layouts, project(): product.astype(jnp.bfloat16).reshape(seq_count, res_len, HEADS, head_size)  11.6 us
    dot_general x3, matrix products, project(): product = jnp.dot(flat_input, matrix, preferred_element_type=jnp.float32)  11.3 us
    convert_element_type x3, local copies, waits for them, and re-layouts, project(): product.astype(jnp.bfloat16).reshape(seq_count, res_len, HEADS, head_size)  7.76 us
  transfers between devices with their start and end apart: 2, of which 2 were waited for; matrix products, arithmetic and copies ran while one was open for 1% of the time, Pallas kernels for 0%

commit v1 on v0

v1 whole, which is shorter than its diff:
```python
import math

import jax
import jax.numpy as jnp
from jax import lax
from jax.experimental import pallas as pl
from jax.experimental.pallas import tpu as pltpu
from jax.sharding import Mesh, PartitionSpec as P

HEADS = 12
F32 = jnp.float32
BF16 = jnp.bfloat16
VMEM = pl.BlockSpec(memory_space=pltpu.VMEM)
SMEM = pl.BlockSpec(memory_space=pltpu.SMEM)
PARAMS = pltpu.CompilerParams(vmem_limit_bytes=40 * 1024 * 1024)
NT = (((1,), (1,)), ((), ()))
TN = (((0,), (0,)), ((), ()))


def dot(a, b, dims=(((1,), (0,)), ((), ()))):
    return lax.dot_general(a, b, dims, preferred_element_type=F32)


def rows_of(x_ref, s):
    blocks, _, block, width = x_ref.shape
    return x_ref[:, s].reshape(blocks * block, width)


def project(x_ref, pairs):
    seqs = x_ref.shape[1]
    for s in range(seqs):
        rows = rows_of(x_ref, s)
        for w_ref, o_ref in pairs:
            heads, packed, res = o_ref.shape
            head = packed // seqs
            out = dot(w_ref[...], rows, NT).astype(BF16)
            o_ref[:, s * head : (s + 1) * head, :] = out.reshape(heads, head, res)


def pair_products(core, scale, a_ref, b_ref, own_ref, other_ref):
    half = own_ref.shape[0]
    for h in range(half):
        for ref, base in ((own_ref, core * half), (other_ref, (1 - core) * half)):
            product = dot(a_ref[base + h], b_ref[base + h], TN)
            ref[h] = product if scale is None else scale * product


def rows_kernel(scale, core_ref, x_ref, wq_ref, wk_ref, wv_ref, q_ref, k_ref, v_ref, own_ref, other_ref):
    project(x_ref, ((wq_ref, q_ref), (wk_ref, k_ref), (wv_ref, v_ref)))
    pair_products(core_ref[0], scale, q_ref, k_ref, own_ref, other_ref)


def grad_rows_kernel(core_ref, c_ref, w_ref, v_ref, g_ref, own_ref, other_ref):
    project(c_ref, ((w_ref, g_ref),))
    pair_products(core_ref[0], None, g_ref, v_ref, own_ref, other_ref)


def pack_kernel(*refs):
    out_ref = refs[-1]
    blocks, terms, heads, rows, res = out_ref.shape
    for t in range(terms):
        a_ref, b_ref = refs[2 * t : 2 * t + 2]
        for h in range(heads):
            out_ref[:, t, h] = (a_ref[h] + b_ref[h]).astype(out_ref.dtype).reshape(blocks, rows, res)


def fold_kernel(x_ref, out_ref):
    total = x_ref[0].astype(F32)
    for k in range(1, x_ref.shape[0]):
        total = total + x_ref[k].astype(F32)
    out_ref[...] = total


def softmax_kernel(scaling, a_ref, b_ref, c_ref, d_ref, out_ref):
    total = (a_ref[...] + b_ref[...]) + (c_ref[...] + d_ref[...])
    logit, grad = total[0], total[1]
    exponent = jnp.exp(logit - jnp.max(logit, axis=-1, keepdims=True))
    prob = (exponent / jnp.sum(exponent, axis=-1, keepdims=True)).astype(BF16)
    weights = prob.astype(F32)
    row_dot = jnp.sum(weights * grad, axis=-1, keepdims=True)
    logit_grad = (scaling * weights * (grad - row_dot)).astype(BF16)
    for k in range(out_ref.shape[0]):
        out_ref[k, 0] = prob
        out_ref[k, 1] = logit_grad


def output_kernel(core_ref, own_ref, other_ref, q_ref, k_ref, g_ref, wq_ref, wk_ref, wv_ref, out_ref, qg_ref, kg_ref, vg_ref):
    core = core_ref[0]
    half = own_ref.shape[2]
    res = own_ref.shape[-1]
    seqs = out_ref.shape[1]
    for h in range(half):
        for ref, base in ((own_ref, core * half), (other_ref, (1 - core) * half)):
            prob = ref[:, 0, h].reshape(res, res)
            logit_grad = ref[:, 1, h].reshape(res, res)
            hh = base + h
            for o_ref, value in (
                (qg_ref, dot(k_ref[hh], logit_grad, NT)),
                (kg_ref, dot(q_ref[hh], logit_grad)),
                (vg_ref, dot(g_ref[hh], prob)),
            ):
                o_ref[:, hh] = value.astype(BF16).reshape(seqs, -1, res)
    for s in range(seqs):
        total = None
        for w_ref, o_ref in ((wq_ref, qg_ref), (wk_ref, kg_ref), (wv_ref, vg_ref)):
            part = dot(w_ref[...], o_ref[s].reshape(-1, res))
            total = part if total is None else total + part
        out_ref[:, s] = total.astype(BF16).T.reshape(out_ref.shape[0], -1, out_ref.shape[-1])


def call(kernel, outs, *args, smem=0, scratch=()):
    return pl.pallas_call(
        kernel,
        out_shape=outs,
        in_specs=[SMEM] * smem + [VMEM] * (len(args) - smem),
        out_specs=jax.tree.map(lambda _: VMEM, outs),
        scratch_shapes=scratch,
        compiler_params=PARAMS,
    )(*args)


def shape(dims, dtype=BF16):
    return jax.ShapeDtypeStruct(dims, dtype)


def ring(axis, step):
    n = lax.axis_size(axis)
    return [(i, (i + step) % n) for i in range(n)]


def body(normed, cotangent, w_query, w_key, w_value, w_out):
    blocks = lax.axis_size(("z", "y"))
    seq_count, block, width = normed.shape
    seqs, res = seq_count // blocks, block * blocks
    head = width // HEADS
    half = HEADS // 2
    scaling = 1.0 / math.sqrt(head * seqs * lax.axis_size(("x", "core", "z", "y")))
    core = lax.axis_index("core").reshape(1).astype(jnp.int32)

    def exchange(a, axes=("z", "y")):
        return lax.all_to_all(a, axes, split_axis=0, concat_axis=0, tiled=True)

    rows = exchange(normed.reshape(blocks, seqs, block, width))
    cot_rows = exchange(cotangent.reshape(blocks, seqs, block, width))
    packed = shape((HEADS, seqs * head, res))
    sums = shape((half, res, res), F32)

    def swap(a):
        return lax.ppermute(a, "core", ring("core", 1))

    q, k, v, logit_own, logit_other = call(
        lambda *refs: rows_kernel(scaling, *refs),
        (packed, packed, packed, sums, sums),
        core, rows, w_query.T, w_key.T, w_value.T, smem=1,
    )
    logit_recv = swap(logit_other)
    g, grad_own, grad_other = call(
        grad_rows_kernel, (packed, sums, sums), core, cot_rows, w_out, v, smem=1
    )
    grad_recv = swap(grad_other)
    split = lax.axis_size(("x", "z"))
    cut = (2, half, res // split, res)
    terms = call(pack_kernel, shape((split,) + cut), logit_own, logit_recv, grad_own, grad_recv)
    terms = exchange(terms, ("x", "z"))
    term = call(fold_kernel, shape(cut, F32), terms)
    others = [lax.ppermute(term, "y", ring("y", step)) for step in (1, 2, 3)]
    result = call(lambda *refs: softmax_kernel(scaling, *refs), shape((split,) + cut), term, *others)
    result = exchange(result, ("x", "z"))
    result_other = swap(result)
    grads = pltpu.VMEM((seqs, HEADS, head, res), BF16)
    out = call(
        output_kernel,
        shape((blocks, seqs, block, width)),
        core, result, result_other, q, k, g, w_query, w_key, w_value,
        smem=1, scratch=[grads, grads, grads],
    )
    return exchange(out).reshape(seq_count, block, width)


def solution(mesh):
    fine = Mesh(mesh.devices.reshape(4, 2, 4, 4), ("x", "core", "z", "y"))
    spec = P(("x", "core"), ("z", "y"), None)
    return jax.shard_map(
        body, mesh=fine, in_specs=(spec, spec, P(), P(), P(), P()), out_specs=spec, check_vma=False
    )
```

time: 334 us -> 172 us (0.51)
  waiting for transfers between devices: 175 us -> 16.1 us
  blocking collectives: 58.8 us -> 111 us
  matrix products: 38.6 us -> 0 us
  local copies, waits for them, and re-layouts: 37.3 us -> 20.6 us
  between operations: 13.6 us -> 0.13 us
  Pallas kernels: 0 us -> 12.6 us
  starting transfers between devices: 3.75 us -> 9.96 us
  other arithmetic: 4.92 us -> 0 us
    psum x1 -> x0, waiting for transfers between devices: 155 us -> none  [body(): tied_logit, prob_grad = lax.psum((logit_term, prob_term), ('seq', 'res'))]
    all_to_all x2 -> x4, blocking collectives: 58.8 us -> 111 us  [exchange(): return lax.all_to_all(a, axes, split_axis=0, concat_axis=0, tiled=True)]
    dot_general x12 -> x0, matrix products: 38.6 us -> none  [the longest x3 11.3 us: project(): product = jnp.dot(flat_input, matrix, preferred_element_type=jnp.float32)]
    all_to_all x1, waiting for transfers between devices: 19.7 us -> 1.2 us  [exchange(): return lax.all_to_all(a, axes, split_axis=0, concat_axis=0, tiled=True)]
    unnamed x21 -> x38, local copies, waits for them, and re-layouts: 4.29 us -> 20.6 us
    reshape x5 -> x0, local copies, waits for them, and re-layouts: 15.7 us -> none  [the longest x3 11.6 us: project(): product.astype(jnp.bfloat16).reshape(seq_count, res_len, HEADS, head_size)]
    ppermute x0 -> x6, waiting for transfers between devices: none -> 14.9 us  [the longest x3 8.55 us: swap(): return lax.ppermute(a, 'core', ring('core', 1))]
    convert_element_type x7 -> x0, local copies, waits for them, and re-layouts: 13.1 us -> none  [the longest x3 7.76 us: project(): product.astype(jnp.bfloat16).reshape(seq_count, res_len, HEADS, head_size)]
  transfers between devices with their start and end apart: 2 -> 7, of which waited for: 2 -> 6; matrix products, arithmetic and copies ran while one was open for 1% -> 4% of each run, Pallas kernels for 0% -> 3%
where the time goes in v1:
time: 172 us; the launch traced here: 170 us
  blocking collectives  111 us (65%)
  local copies, waits for them, and re-layouts  20.6 us (12%)
  waiting for transfers between devices  16.1 us (9%)
  Pallas kernels  12.6 us (7%)
  starting transfers between devices  9.96 us (6%)
    all_to_all x4, blocking collectives, exchange(): return lax.all_to_all(a, axes, split_axis=0, concat_axis=0, tiled=True)  111 us
    unnamed x38, local copies, waits for them, and re-layouts  20.6 us
    pallas_call x6, Pallas kernels, call(): pl.pallas_call(kernel, out_shape=outs, in_specs=[SMEM] * smem + [VMEM] *...  12.6 us
    ppermute x3, waiting for transfers between devices, swap(): return lax.ppermute(a, 'core', ring('core', 1))  8.55 us
    ppermute x3, waiting for transfers between devices, body(): others = [lax.ppermute(term, 'y', ring('y', step)) for step in (1, 2, 3)]  6.31 us
    ppermute x3, starting transfers between devices, body(): others = [lax.ppermute(term, 'y', ring('y', step)) for step in (1, 2, 3)]  5.68 us
    all_to_all x1, starting transfers between devices, exchange(): return lax.all_to_all(a, axes, split_axis=0, concat_axis=0, tiled=True)  3.71 us
  transfers between devices with their start and end apart: 7, of which 6 were waited for; matrix products, arithmetic and copies ran while one was open for 4% of the time, Pallas kernels for 3%

profile of v1, /device:TPU:2, one launch (start us, length us, event | category | flops | bytes accessed | tf_op | source)
XLA Modules:
  0.0 170.4 jit_solution(7215505260858922994)
XLA Ops:
  0.0 30.8 %all_to_all.25.refs_1_ = bf16[16,4,16,768]{3,2,1,0:T(8,128)(2,1)S(1)} all-to-all(bf16[16,4,16,768]{3,2,1,0:T(8,128)(2,1)} %bitcast.11), channel_id=1, replica_groups=mesh['x'=4,'core'=2,'z'=4,'y'=4] {'z','y'}, dimensions={0} | all-to-all | bytes 3145728 | tf_op jit(solution)/shard_map/all_to_all | solution.py:141
  30.8 3.7 %all-to-all-start.1 = ((bf16[16,4,16,768]{3,2,1,0:T(8,128)(2,1)}), bf16[16,4,16,768]{3,2,1,0:T(8,128)(2,1)S(1)}, u32[]{:S(2)}, u32[]{:S(2)}) async-start(bf16[16,4,16,768]{3,2,1,0:T(8,128)(2,1)} %bitcast.12), calls=%async_computation.1 | async-start | bytes 3145728 | tf_op jit(solution)/shard_map/all_to_all | solution.py:141
  34.5 2.4 %copy.7 = bf16[768,768]{0,1:T(8,128)(2,1)} copy(bf16[768,768]{1,0:T(8,128)(2,1)} %wq_ref.1) | data formatting | bytes 2359296 | tf_op args[2]
  36.9 2.4 %copy.8 = bf16[768,768]{0,1:T(8,128)(2,1)} copy(bf16[768,768]{1,0:T(8,128)(2,1)} %wk_ref.1) | data formatting | bytes 2359296 | tf_op args[3]
  39.3 2.4 %copy.9 = bf16[768,768]{0,1:T(8,128)(2,1)} copy(bf16[768,768]{1,0:T(8,128)(2,1)} %wv_ref.1) | data formatting | bytes 2359296 | tf_op args[4]
  41.7 0.0 copy-start.3
  41.7 1.3 copy-done.3
  43.0 0.0 copy-start.4
  43.0 1.3 copy-done.4
  44.2 0.0 copy-start.5
  44.2 1.3 copy-done.5
  45.5 4.5 %shard_map.64 = (bf16[12,256,256]{2,1,0:T(8,128)(2,1)S(1)}, bf16[12,256,256]{2,1,0:T(8,128)(2,1)S(1)}, bf16[12,256,256]{2,1,0:T(8,128)(2,1)S(1)}, f32[6,256,256]{2,1,0:T(8,128)S(1)}, f32[6,256,256]{2,1,0:T(8,128)S(1)}) custom-call(s32[1]{0:T(128)} %bitcast.refs_0_.core_ref, bf16[16,4,16,768]{3,2,1,0:T(8,128)(2,1)S(1)} %all_to_all.25.refs_1_, ...), custom_call_target="tpu_custom_call" | custom-call | tf_op jit(solution)/shard_map/pallas_call | solution.py:112
  50.0 0.0 copy-start.6
  50.0 1.2 copy-done.6
  51.2 0.0 copy-start.8
  51.2 1.1 copy-done.8
  52.3 0.0 copy-start.10
  52.3 1.2 copy-done.10
  53.5 0.0 copy-start.12
  53.5 1.1 copy-done.12
  54.6 0.0 copy-start.15
  54.6 1.2 copy-done.15
  55.8 1.2 all-to-all-done.1.c_ref
  57.0 0.0 copy-start.11
  57.0 1.4 copy-done.11
  58.4 0.0 copy-start.14
  58.4 1.3 copy-done.14
  59.7 0.0 copy-start.16
  59.7 0.0 copy-start.13
  59.7 2.0 %shard_map.65 = (bf16[12,256,256]{2,1,0:T(8,128)(2,1)S(1)}, f32[6,256,256]{2,1,0:T(8,128)S(1)}, f32[6,256,256]{2,1,0:T(8,128)S(1)}) custom-call(s32[1]{0:T(128)} %bitcast.refs_0_.core_ref, bf16[16,4,16,768]{3,2,1,0:T(8,128)(2,1)S(1)} %all-to-all-done.1.c_ref, bf16[768,768]{1,0:T(8,128)(2,1)S(1)} %copy-done.14, bf16[12,256,256]{2,1,0:T(8,128)(2,1)S(1)} %copy-done.11), custom_call_target="tpu_custom_call" | custom-call | tf_op jit(solution)/shard_map/pallas_call | solution.py:112
  61.7 0.1 collective-permute-start.1
  61.8 0.0 copy-done.16
  61.8 0.5 collective-permute-start
  62.3 2.9 %collective-permute-done.1.refs_3_ = f32[6,256,256]{2,1,0:T(8,128)S(1)} collective-permute-done((f32[6,256,256]{2,1,0:T(8,128)S(1)}, f32[6,256,256]{2,1,0:T(8,128)S(1)}, u32[]{:S(2)}, u32[]{:S(2)}) %collective-permute-start.1) | collective-permute-done | bytes 1572896 | tf_op jit(solution)/shard_map/ppermute | solution.py:149
  65.2 2.2 %collective-permute-done.refs_1_ = f32[6,256,256]{2,1,0:T(8,128)S(1)} collective-permute-done((f32[6,256,256]{2,1,0:T(8,128)S(1)}, f32[6,256,256]{2,1,0:T(8,128)S(1)}, u32[]{:S(2)}, u32[]{:S(2)}) %collective-permute-start) | collective-permute-done | bytes 1572896 | tf_op jit(solution)/shard_map/ppermute | solution.py:149
  67.5 0.0 copy-done.13
  67.5 0.3 shard_map.66
  67.8 27.0 %all_to_all.26.x_ref = bf16[16,2,6,16,256]{4,3,2,1,0:T(8,128)(2,1)S(1)} all-to-all(bf16[16,2,6,16,256]{4,3,2,1,0:T(8,128)(2,1)S(1)} %shard_map.66), channel_id=1, replica_groups=mesh['x'=4,'core'=2,'z'=4,'y'=4] {'x','z'}, dimensions={0} | all-to-all | bytes 3145728 | tf_op jit(solution)/shard_map/all_to_all | solution.py:141
  94.7 0.0 copy-start.9
  94.7 0.2 shard_map.67.refs_0_
  94.9 1.5 collective-permute-start.2
  96.5 2.7 %collective-permute-start.3 = (f32[2,6,16,256]{3,2,1,0:T(8,128)S(1)}, f32[2,6,16,256]{3,2,1,0:T(8,128)S(1)}, u32[]{:S(2)}, u32[]{:S(2)}) collective-permute-start(f32[2,6,16,256]{3,2,1,0:T(8,128)S(1)} %shard_map.67.refs_0_), channel_id=1, source_target_pairs={{0,2},{1,3},{2,0},{3,1},{4,6},{5,7},{6,4},{7,5},{8,10},{9,11},{10,... | collective-permute-start | bytes 589832 | tf_op jit(solution)/shard_map/ppermute | solution.py:166
  99.2 1.4 collective-permute-start.4
  100.6 2.7 %collective-permute-done.2.refs_1_ = f32[2,6,16,256]{3,2,1,0:T(8,128)S(1)} collective-permute-done((f32[2,6,16,256]{3,2,1,0:T(8,128)S(1)}, f32[2,6,16,256]{3,2,1,0:T(8,128)S(1)}, u32[]{:S(2)}, u32[]{:S(2)}) %collective-permute-start.2) | collective-permute-done | bytes 196640 | tf_op jit(solution)/shard_map/ppermute | solution.py:166
  103.3 3.6 %collective-permute-done.3.refs_2_ = f32[2,6,16,256]{3,2,1,0:T(8,128)S(1)} collective-permute-done((f32[2,6,16,256]{3,2,1,0:T(8,128)S(1)}, f32[2,6,16,256]{3,2,1,0:T(8,128)S(1)}, u32[]{:S(2)}, u32[]{:S(2)}) %collective-permute-start.3) | collective-permute-done | bytes 196640 | tf_op jit(solution)/shard_map/ppermute | solution.py:166
  106.9 0.0 collective-permute-done.4.refs_3_
  106.9 0.0 copy-start.2
  106.9 0.0 copy-start.7
  106.9 0.3 shard_map.68
  107.3 0.0 copy-start
  107.3 0.0 copy-start.1
  107.3 24.8 %all_to_all.27.own_ref = bf16[16,2,6,16,256]{4,3,2,1,0:T(8,128)(2,1)S(1)} all-to-all(bf16[16,2,6,16,256]{4,3,2,1,0:T(8,128)(2,1)S(1)} %shard_map.68), channel_id=1, replica_groups=mesh['x'=4,'core'=2,'z'=4,'y'=4] {'x','z'}, dimensions={0} | all-to-all | bytes 3145728 | tf_op jit(solution)/shard_map/all_to_all | solution.py:141
  132.1 0.0 collective-permute-start.5
  132.1 3.4 %collective-permute-done.5.other_ref = bf16[16,2,6,16,256]{4,3,2,1,0:T(8,128)(2,1)S(1)} collective-permute-done((bf16[16,2,6,16,256]{4,3,2,1,0:T(8,128)(2,1)S(1)}, bf16[16,2,6,16,256]{4,3,2,1,0:T(8,128)(2,1)S(1)}, u32[]{:S(2)}, u32[]{:S(2)}) %collective-permute-start.5) | collective-permute-done | bytes 1572896 | tf_op jit(solution)/shard_map/ppermute | solution.py:149
  135.5 0.0 copy-done.9
  135.5 0.0 copy-done.2
  135.5 0.0 copy-done.7
  135.5 0.0 copy-done
  135.5 0.0 copy-done.1
  135.5 5.3 %shard_map.69 = bf16[16,4,16,768]{3,2,1,0:T(8,128)(2,1)S(1)} custom-call(s32[1]{0:T(128)} %bitcast.refs_0_.core_ref, bf16[16,2,6,16,256]{4,3,2,1,0:T(8,128)(2,1)S(1)} %all_to_all.27.own_ref, bf16[16,2,6,16,256]{4,3,2,1,0:T(8,128)(2,1)S(1)} %collective-permute-done.5.other_ref, bf16[12,256,256]{2,1,0:T(8,128)(2,1)S(1)} %copy-done.7, ...), custom_call_target="tpu_custom_call" | custom-call | tf_op jit(solution)/shard_map/pallas_call | solution.py:112
  140.8 28.5 %all_to_all.28 = bf16[16,4,16,768]{3,2,1,0:T(8,128)(2,1)S(1)} all-to-all(bf16[16,4,16,768]{3,2,1,0:T(8,128)(2,1)S(1)} %shard_map.69), channel_id=1, replica_groups=mesh['x'=4,'core'=2,'z'=4,'y'=4] {'z','y'}, dimensions={0} | all-to-all | bytes 3145728 | tf_op jit(solution)/shard_map/all_to_all | solution.py:141
  169.3 1.1 copy.11
Async XLA Ops:
  30.8 26.2 %all-to-all-start.1 = ((bf16[16,4,16,768]{3,2,1,0:T(8,128)(2,1)}), bf16[16,4,16,768]{3,2,1,0:T(8,128)(2,1)S(1)}, u32[]{:S(2)}, u32[]{:S(2)}) async-start(bf16[16,4,16,768]{3,2,1,0:T(8,128)(2,1)} %bitcast.12), calls=%async_computation.1 | async-start | bytes 3145728 | tf_op jit(solution)/shard_map/all_to_all | solution.py:141
  41.7 1.3 copy-start.3
  43.0 1.3 copy-start.4
  44.2 1.3 copy-start.5
  50.0 1.2 copy-start.6
  51.2 1.1 copy-start.8
  52.3 1.2 copy-start.10
  53.5 1.1 copy-start.12
  54.6 1.2 copy-start.15
  57.0 1.4 copy-start.11
  58.4 1.3 copy-start.14
  59.7 2.1 %copy-start.16 = (f32[6,256,256]{2,1,0:T(8,128)S(1)}, f32[6,256,256]{2,1,0:T(8,128)}, u32[]{:S(2)}) copy-start(f32[6,256,256]{2,1,0:T(8,128)} %copy-done.15) | copy-start | bytes 4718596
  59.7 7.8 %copy-start.13 = (f32[6,256,256]{2,1,0:T(8,128)S(1)}, f32[6,256,256]{2,1,0:T(8,128)}, u32[]{:S(2)}) copy-start(f32[6,256,256]{2,1,0:T(8,128)} %copy-done.12) | copy-start | bytes 4718596
  61.7 3.5 %collective-permute-start.1 = (f32[6,256,256]{2,1,0:T(8,128)S(1)}, f32[6,256,256]{2,1,0:T(8,128)S(1)}, u32[]{:S(2)}, u32[]{:S(2)}) collective-permute-start(f32[6,256,256]{2,1,0:T(8,128)S(1)} %get-tuple-element.17), channel_id=1, source_target_pairs={{0,16},{16,0},{1,17},{17,1},{2,18},{18,2},{3,19},{19,3},{4,20},{20... | collective-permute-start | bytes 4718600 | tf_op jit(solution)/shard_map/ppermute | solution.py:149
  61.8 5.6 %collective-permute-start = (f32[6,256,256]{2,1,0:T(8,128)S(1)}, f32[6,256,256]{2,1,0:T(8,128)S(1)}, u32[]{:S(2)}, u32[]{:S(2)}) collective-permute-start(f32[6,256,256]{2,1,0:T(8,128)S(1)} %copy-done.16), channel_id=1, source_target_pairs={{0,16},{16,0},{1,17},{17,1},{2,18},{18,2},{3,19},{19,3},{4,20},{20... | collective-permute-start | bytes 4718600 | tf_op jit(solution)/shard_map/ppermute | solution.py:149
  94.7 40.8 %copy-start.9 = (bf16[12,256,256]{2,1,0:T(8,128)(2,1)S(1)}, bf16[12,256,256]{2,1,0:T(8,128)(2,1)}, u32[]{:S(2)}) copy-start(bf16[12,256,256]{2,1,0:T(8,128)(2,1)} %copy-done.8) | copy-start | bytes 4718596
  94.9 8.4 %collective-permute-start.2 = (f32[2,6,16,256]{3,2,1,0:T(8,128)S(1)}, f32[2,6,16,256]{3,2,1,0:T(8,128)S(1)}, u32[]{:S(2)}, u32[]{:S(2)}) collective-permute-start(f32[2,6,16,256]{3,2,1,0:T(8,128)S(1)} %shard_map.67.refs_0_), channel_id=1, source_target_pairs={{0,1},{1,2},{2,3},{3,0},{4,5},{5,6},{6,7},{7,4},{8,9},{9,10},{10,1... | collective-permute-start | bytes 589832 | tf_op jit(solution)/shard_map/ppermute | solution.py:166
  96.5 10.5 %collective-permute-start.3 = (f32[2,6,16,256]{3,2,1,0:T(8,128)S(1)}, f32[2,6,16,256]{3,2,1,0:T(8,128)S(1)}, u32[]{:S(2)}, u32[]{:S(2)}) collective-permute-start(f32[2,6,16,256]{3,2,1,0:T(8,128)S(1)} %shard_map.67.refs_0_), channel_id=1, source_target_pairs={{0,2},{1,3},{2,0},{3,1},{4,6},{5,7},{6,4},{7,5},{8,10},{9,11},{10,... | collective-permute-start | bytes 589832 | tf_op jit(solution)/shard_map/ppermute | solution.py:166
  99.2 7.8 %collective-permute-start.4 = (f32[2,6,16,256]{3,2,1,0:T(8,128)S(1)}, f32[2,6,16,256]{3,2,1,0:T(8,128)S(1)}, u32[]{:S(2)}, u32[]{:S(2)}) collective-permute-start(f32[2,6,16,256]{3,2,1,0:T(8,128)S(1)} %shard_map.67.refs_0_), channel_id=1, source_target_pairs={{0,3},{1,0},{2,1},{3,2},{4,7},{5,4},{6,5},{7,6},{8,11},{9,8},{10,9... | collective-permute-start | bytes 589832 | tf_op jit(solution)/shard_map/ppermute | solution.py:166
  106.9 28.6 %copy-start.2 = (bf16[768,768]{1,0:T(8,128)(2,1)S(1)}, bf16[768,768]{1,0:T(8,128)(2,1)}, u32[]{:S(2)}) copy-start(bf16[768,768]{1,0:T(8,128)(2,1)} %wv_ref.1) | copy-start | bytes 3538948
  106.9 28.6 %copy-start.7 = (bf16[12,256,256]{2,1,0:T(8,128)(2,1)S(1)}, bf16[12,256,256]{2,1,0:T(8,128)(2,1)}, u32[]{:S(2)}) copy-start(bf16[12,256,256]{2,1,0:T(8,128)(2,1)} %copy-done.6) | copy-start | bytes 4718596
  107.3 28.2 %copy-start = (bf16[768,768]{1,0:T(8,128)(2,1)S(1)}, bf16[768,768]{1,0:T(8,128)(2,1)}, u32[]{:S(2)}) copy-start(bf16[768,768]{1,0:T(8,128)(2,1)} %wq_ref.1) | copy-start | bytes 3538948
  107.3 28.2 %copy-start.1 = (bf16[768,768]{1,0:T(8,128)(2,1)S(1)}, bf16[768,768]{1,0:T(8,128)(2,1)}, u32[]{:S(2)}) copy-start(bf16[768,768]{1,0:T(8,128)(2,1)} %wk_ref.1) | copy-start | bytes 3538948
  132.1 3.4 %collective-permute-start.5 = (bf16[16,2,6,16,256]{4,3,2,1,0:T(8,128)(2,1)S(1)}, bf16[16,2,6,16,256]{4,3,2,1,0:T(8,128)(2,1)S(1)}, u32[]{:S(2)}, u32[]{:S(2)}) collective-permute-start(bf16[16,2,6,16,256]{4,3,2,1,0:T(8,128)(2,1)S(1)} %all_to_all.27.own_ref), channel_id=1, source_target_pairs={{0,16},{16,0},{1,17},{17,1},{2,18},{18,2},{3,19},{19,3},{4,20},{20... | collective-permute-start | bytes 4718600 | tf_op jit(solution)/shard_map/ppermute | solution.py:149

commit v2 on v1

v2 whole, which is shorter than its diff:
```python
import math

import jax
import jax.numpy as jnp
from jax import lax
from jax.experimental import pallas as pl
from jax.experimental.pallas import tpu as pltpu
from jax.sharding import Mesh, PartitionSpec as P

HEADS = 12
F32 = jnp.float32
BF16 = jnp.bfloat16
VMEM = pl.BlockSpec(memory_space=pltpu.VMEM)
SMEM = pl.BlockSpec(memory_space=pltpu.SMEM)
HBM = pl.BlockSpec(memory_space=pltpu.HBM)
NT = (((1,), (1,)), ((), ()))
TN = (((0,), (0,)), ((), ()))


def dot(a, b, dims=(((1,), (0,)), ((), ()))):
    return lax.dot_general(a, b, dims, preferred_element_type=F32)


def project(x_ref, pairs):
    blocks, seqs, block, width = x_ref.shape
    for s in range(seqs):
        rows = x_ref[:, s].reshape(blocks * block, width)
        for w_ref, o_ref in pairs:
            heads, packed, res = o_ref.shape
            head = packed // seqs
            out = dot(w_ref[...], rows, NT).astype(BF16)
            o_ref[:, s * head : (s + 1) * head, :] = out.reshape(heads, head, res)


def pair_products(core, scale, a_ref, b_ref, own_ref, other_ref):
    half = own_ref.shape[0]
    for h in range(half):
        for ref, base in ((own_ref, core * half), (other_ref, (1 - core) * half)):
            product = dot(a_ref[base + h], b_ref[base + h], TN)
            ref[h] = product if scale is None else scale * product


def start(pairs, sems):
    copies = [pltpu.make_async_copy(src, dst, sems.at[n]) for n, (src, dst) in enumerate(pairs)]
    for copy in copies:
        copy.start()
    return copies


def rows_kernel(scale, place_ref, x_ref, wq_in, wk_in, q_out, k_out, own_ref, other_ref, wq, wk, t_ref, q_ref, k_ref, in_sems, out_sems):
    loads = start(((wq_in, wq), (wk_in, wk)), in_sems)
    for load, w, o_ref in zip(loads, (wq, wk), (q_ref, k_ref)):
        load.wait()
        t_ref[...] = w[...].T
        project(x_ref, ((t_ref, o_ref),))
    stores = start(((q_ref, q_out), (k_ref, k_out)), out_sems)
    pair_products(place_ref[0], scale, q_ref, k_ref, own_ref, other_ref)
    for store in stores:
        store.wait()


def value_kernel(x_ref, w_ref, v_ref, t_ref):
    t_ref[...] = w_ref[...].T
    project(x_ref, ((t_ref, v_ref),))


def grad_rows_kernel(place_ref, c_ref, w_in, v_in, g_out, own_ref, other_ref, w, v_ref, g_ref, in_sems, out_sems):
    loads = start(((w_in, w), (v_in, v_ref)), in_sems)
    loads[0].wait()
    project(c_ref, ((w, g_ref),))
    stores = start(((g_ref, g_out),), out_sems)
    loads[1].wait()
    pair_products(place_ref[0], None, g_ref, v_ref, own_ref, other_ref)
    stores[0].wait()


def split_kernel(place_ref, a_ref, b_ref, *outs):
    rows = outs[0].shape[0]
    for d, ref in enumerate(outs):
        at = pl.ds(pl.multiple_of(lax.rem(place_ref[1] + d, len(outs)) * rows, rows), rows)
        ref[...] = (a_ref[at] + b_ref[at]).astype(ref.dtype)


def sum_kernel(*refs):
    a, b, c, d, out_ref = refs
    out_ref[...] = (a[...] + b[...]) + (c[...] + d[...])


def fold_kernel(place_ref, logit_ref, *refs):
    grads, outs = refs[:4], refs[4:]
    rows = outs[0].shape[0] // 2
    for d, ref in enumerate(outs):
        at = pl.ds(pl.multiple_of(lax.rem(place_ref[2] + d, len(outs)) * rows, rows), rows)
        a, b, c, e = (grad[at].astype(F32) for grad in grads)
        ref[pl.ds(0, rows)] = logit_ref[at]
        ref[pl.ds(rows, rows)] = (a + b) + (c + e)


def softmax_kernel(scaling, a_ref, b_ref, c_ref, d_ref, out_ref):
    total = (a_ref[...] + b_ref[...]) + (c_ref[...] + d_ref[...])
    rows = total.shape[0] // 2
    logit, grad = total[:rows], total[rows:]
    exponent = jnp.exp(logit - jnp.max(logit, axis=-1, keepdims=True))
    prob = (exponent / jnp.sum(exponent, axis=-1, keepdims=True)).astype(BF16)
    weights = prob.astype(F32)
    row_dot = jnp.sum(weights * grad, axis=-1, keepdims=True)
    out_ref[pl.ds(0, rows)] = prob
    out_ref[pl.ds(rows, rows)] = (scaling * weights * (grad - row_dot)).astype(BF16)


def join_kernel(place_ref, *refs):
    parts, out_ref = refs[:-1], refs[-1]
    rows = out_ref.shape[1] // len(parts)
    for d, part_ref in enumerate(parts):
        first = lax.rem(place_ref[2] + len(parts) - d, len(parts)) * rows
        at = pl.ds(pl.multiple_of(first, rows), rows)
        for term in range(2):
            out_ref[term, at] = part_ref[pl.ds(term * rows, rows)]


def head_grads(base, here, parts, q_ref, k_ref, g_ref, outs, stage_ref):
    rows = parts[0].shape[1]
    for d, part_ref in enumerate(parts):
        first = lax.rem(here + len(parts) - d, len(parts)) * rows
        stage_ref[:, pl.ds(pl.multiple_of(first, rows), rows)] = part_ref[...].astype(F32)
    res = stage_ref.shape[-1]
    for h in range(q_ref.shape[0] // 2):
        prob, logit_grad = (stage_ref[term, pl.ds(h * res, res)].astype(BF16) for term in range(2))
        hh = base + h
        for o_ref, value in zip(
            outs,
            (dot(k_ref[hh], logit_grad, NT), dot(q_ref[hh], logit_grad), dot(g_ref[hh], prob)),
        ):
            o_ref[:, hh] = value.astype(BF16).reshape(o_ref.shape[0], -1, res)


def output_kernel(place_ref, *refs):
    own, other, held_in, weights_in, out_ref = refs[:4], refs[4:8], refs[8:11], refs[11:14], refs[14]
    held, weights, outs, stage_ref, sems = refs[15:18], refs[18:21], refs[21:24], refs[24], refs[25]
    loads = start(list(zip((*held_in, *weights_in), (*held, *weights))), sems)
    for load in loads[:3]:
        load.wait()
    core = place_ref[0]
    half = held[0].shape[0] // 2
    head_grads(core * half, place_ref[1], own, *held, outs, stage_ref)
    head_grads((1 - core) * half, place_ref[3], other, *held, outs, stage_ref)
    for load in loads[3:]:
        load.wait()
    res = held[0].shape[-1]
    for s in range(out_ref.shape[1]):
        total = None
        for w_ref, o_ref in zip(weights, outs):
            part = dot(w_ref[...], o_ref[s].reshape(-1, res))
            total = part if total is None else total + part
        out_ref[:, s] = total.astype(BF16).T.reshape(out_ref.shape[0], -1, out_ref.shape[-1])


def call(kernel, outs, *args, specs=None, out_specs=None, scratch=(), mib=16):
    return pl.pallas_call(
        kernel,
        out_shape=outs,
        in_specs=list(specs or [VMEM] * len(args)),
        out_specs=out_specs or jax.tree.map(lambda _: VMEM, outs),
        scratch_shapes=scratch,
        compiler_params=pltpu.CompilerParams(vmem_limit_bytes=mib * 1024 * 1024),
    )(*args)


def shape(dims, dtype=BF16):
    return jax.ShapeDtypeStruct(dims, dtype)


def shift(a, axis, step):
    n = lax.axis_size(axis)
    return lax.ppermute(a, axis, [(i, (i + step) % n) for i in range(n)])


AXES = ("x", "core", "z", "y")


def number(x, core, z, y):
    return x * 32 + core * 16 + z * 4 + y


def turn(stage, step):
    pairs = []
    for core, axes in ((0, "xzy"), (1, "yxz")):
        for n in range(64):
            at = dict(x=n // 16, z=n // 4 % 4, y=n % 4)
            to = dict(at)
            to[axes[stage]] = (at[axes[stage]] + step) % 4
            pairs.append((number(core=core, **at), number(core=core, **to)))
    return pairs


def body(normed, cotangent, w_query, w_key, w_value, w_out):
    blocks = lax.axis_size(("z", "y"))
    seq_count, block, width = normed.shape
    seqs, res = seq_count // blocks, block * blocks
    head = width // HEADS
    half = HEADS // 2
    scaling = 1.0 / math.sqrt(head * seqs * lax.axis_size(AXES))
    core, x, z, y = (lax.axis_index(axis) for axis in ("core", "x", "z", "y"))
    place = jnp.stack(
        [core, jnp.where(core == 0, x, y), jnp.where(core == 0, z, x), jnp.where(core == 0, y, x)]
    ).astype(jnp.int32)

    def exchange(a):
        return lax.all_to_all(a, ("z", "y"), split_axis=0, concat_axis=0, tiled=True)

    def spread(parts, stage):
        sent = {d: lax.ppermute(parts[d], AXES, turn(stage, d)) for d in (1, 3, 2)}
        return [parts[0]] + [sent[d] for d in (1, 2, 3)]

    def flat(a):
        return a.reshape(half * res, res)

    rows = exchange(normed.reshape(blocks, seqs, block, width))
    cot_rows = exchange(cotangent.reshape(blocks, seqs, block, width))
    packed = shape((HEADS, seqs * head, res))
    sums = shape((half, res, res), F32)
    quarter = (half * res // 4, res)
    weight, held = pltpu.VMEM((width, width), BF16), pltpu.VMEM(packed.shape, BF16)
    sems = pltpu.SemaphoreType.DMA

    def split(dtype, own, other):
        return call(
            split_kernel, [shape(quarter, dtype)] * 4, place, flat(own), flat(shift(other, "core", 1)),
            specs=(SMEM, VMEM, VMEM),
        )

    def row_part(rows, *weights):
        q, k, own, other = call(
            lambda *refs: rows_kernel(scaling, *refs),
            (packed, packed, sums, sums),
            place, rows, *weights[:2],
            specs=(SMEM, VMEM, HBM, HBM), out_specs=(HBM, HBM, VMEM, VMEM),
            scratch=[weight] * 3 + [held] * 2 + [sems((2,)), sems((2,))], mib=24,
        )
        v = call(value_kernel, packed, rows, weights[2], scratch=[weight])
        return q, k, v, call(sum_kernel, shape(quarter, F32), *spread(split(F32, own, other), 0))

    def no_part(*_):
        return *(jnp.zeros(packed.shape, BF16) for _ in range(3)), jnp.zeros(quarter, F32)

    q, k, v, logit = lax.cond(core < 2, row_part, no_part, rows, w_query, w_key, w_value)
    g, grad_own, grad_other = call(
        grad_rows_kernel, (packed, sums, sums), place, cot_rows, w_out, v,
        specs=(SMEM, VMEM, HBM, HBM), out_specs=(HBM, VMEM, VMEM),
        scratch=[weight, held, held, sems((2,)), sems((1,))],
    )
    grads = spread(split(BF16, grad_own, grad_other), 0)
    both = (quarter[0] // 2, res)
    terms = call(
        fold_kernel, [shape(both, F32)] * 4, place, logit, *grads, specs=[SMEM] + [VMEM] * 5
    )
    term = call(sum_kernel, shape(both, F32), *spread(terms, 1))
    result = call(
        lambda *refs: softmax_kernel(scaling, *refs), shape(both), *spread([term] * 4, 2)
    )
    result = call(
        join_kernel, shape((2,) + quarter), place, *spread([result] * 4, 1), specs=[SMEM] + [VMEM] * 4
    )
    own = spread([result] * 4, 0)
    other = [shift(a, "core", 1) for a in own]
    grown = pltpu.VMEM((seqs, HEADS, head, res), BF16)
    out = call(
        output_kernel,
        shape((blocks, seqs, block, width)),
        place, *own, *other, q, k, g, w_query, w_key, w_value,
        specs=[SMEM] + [VMEM] * 8 + [HBM] * 6,
        scratch=[held] * 3 + [weight] * 3 + [grown] * 3
        + [pltpu.VMEM((2, half * res, res), F32), sems((6,))],
        mib=40,
    )
    return exchange(out).reshape(seq_count, block, width)


def solution(mesh):
    fine = Mesh(mesh.devices.reshape(4, 2, 4, 4), ("x", "core", "z", "y"))
    spec = P(("x", "core"), ("z", "y"), None)
    return jax.shard_map(
        body, mesh=fine, in_specs=(spec, spec, P(), P(), P(), P()), out_specs=spec, check_vma=False
    )
```

time: 172 us -> 166 us (0.965)
  blocking collectives: 111 us -> 59.6 us
  waiting for transfers between devices: 16.1 us -> 49.5 us
  starting transfers between devices: 9.96 us -> 31.2 us
  local copies, waits for them, and re-layouts: 20.6 us -> 1.17 us
  Pallas kernels: 12.6 us -> 23.6 us
    all_to_all x4 -> x2, blocking collectives: 111 us -> 59.6 us  [exchange(): lax.all_to_all(a, ('z', 'y'), split_axis=0, concat_axis=0, tiled=True)]
    ppermute x6 -> x24, waiting for transfers between devices: 14.9 us -> 49.5 us  [the longest x18 41.3 us: spread(): sent = {d: lax.ppermute(parts[d], AXES, turn(stage, d)) for d in (1, 3, 2)}]
    ppermute x6 -> x24, starting transfers between devices: 6.25 us -> 27.5 us  [the longest x18 25.1 us: spread(): sent = {d: lax.ppermute(parts[d], AXES, turn(stage, d)) for d in (1, 3, 2)}]
    unnamed x38 -> x9, local copies, waits for them, and re-layouts: 20.6 us -> 1.16 us
    pallas_call x6 -> x11, Pallas kernels: 12.6 us -> 23.6 us  [call(): pl.pallas_call(kernel, out_shape=outs, in_specs=list(specs or [VMEM] * le...]
  transfers between devices with their start and end apart: 7 -> 25, of which waited for: 6 -> 18; matrix products, arithmetic and copies ran while one was open for 4% -> 0% of each run, Pallas kernels for 3% -> 6%
where the time goes in v2:
time: 166 us; the launch traced here: 165 us
  blocking collectives  59.6 us (36%)
  waiting for transfers between devices  49.5 us (30%)
  starting transfers between devices  31.2 us (19%)
  Pallas kernels  23.6 us (14%)
    all_to_all x2, blocking collectives, exchange(): lax.all_to_all(a, ('z', 'y'), split_axis=0, concat_axis=0, tiled=True)  59.6 us
    ppermute x18, waiting for transfers between devices, spread(): sent = {d: lax.ppermute(parts[d], AXES, turn(stage, d)) for d in (1, 3, 2)}  41.3 us
    ppermute x18, starting transfers between devices, spread(): sent = {d: lax.ppermute(parts[d], AXES, turn(stage, d)) for d in (1, 3, 2)}  25.1 us
    pallas_call x11, Pallas kernels, call(): pl.pallas_call(kernel, out_shape=outs, in_specs=list(specs or [VMEM] * le...  23.6 us
    ppermute x6, waiting for transfers between devices, shift(): return lax.ppermute(a, axis, [(i, (i + step) % n) for i in range(n)])  8.14 us
    all_to_all x1, starting transfers between devices, exchange(): lax.all_to_all(a, ('z', 'y'), split_axis=0, concat_axis=0, tiled=True)  3.71 us
  transfers between devices with their start and end apart: 25, of which 18 were waited for; matrix products, arithmetic and copies ran while one was open for 0% of the time, Pallas kernels for 6%

profile of v2, /device:TPU:2, one launch (start us, length us, event | category | flops | bytes accessed | tf_op | source)
XLA Modules:
  0.0 165.3 jit_solution(6875913129443008823)
XLA Ops:
  0.0 30.9 %all_to_all.15 = bf16[16,4,16,768]{3,2,1,0:T(8,128)(2,1)} all-to-all(bf16[16,4,16,768]{3,2,1,0:T(8,128)(2,1)} %bitcast.16), channel_id=1, replica_groups=mesh['x'=4,'core'=2,'z'=4,'y'=4] {'z','y'}, dimensions={0} | all-to-all | bytes 3145728 | tf_op jit(solution)/shard_map/all_to_all | solution.py:209
  30.9 3.7 %all-to-all-start.1 = ((bf16[16,4,16,768]{3,2,1,0:T(8,128)(2,1)}), bf16[16,4,16,768]{3,2,1,0:T(8,128)(2,1)S(1)}, u32[]{:S(2)}, u32[]{:S(2)}) async-start(bf16[16,4,16,768]{3,2,1,0:T(8,128)(2,1)} %bitcast.7), calls=%async_computation.1 | async-start | bytes 3145728 | tf_op jit(solution)/shard_map/all_to_all | solution.py:209
  34.7 0.1 pad_add_fusion.place_ref
  34.7 25.8 %conditional.1 = (bf16[12,256,256]{2,1,0:T(8,128)(2,1)}, bf16[12,256,256]{2,1,0:T(8,128)(2,1)}, bf16[12,256,256]{2,1,0:T(8,128)(2,1)}, f32[384,256]{1,0:T(8,128)S(1)}) conditional(s32[]{:T(128)} %convert_element_type.3, () %tuple.13, (s32[4]{0:T(128)S(1)}, bf16[16,4,16,768]{3,2,1,0:T(8,128)(2,1)}, bf16[768,768]{1,0:T(8,128)(2,1)}, ...), branch_computations={%region_0.1_spmd, %region_1.2_spmd} | conditional | bytes 22020344 | solution.py:246
  34.7 6.8 %branch_1_fun.4 = (bf16[12,256,256]{2,1,0:T(8,128)(2,1)}, bf16[12,256,256]{2,1,0:T(8,128)(2,1)}, f32[6,256,256]{2,1,0:T(8,128)S(1)}, f32[6,256,256]{2,1,0:T(8,128)S(1)}) custom-call(s32[4]{0:T(128)S(1)} %get-tuple-element.15.refs_0_.place_ref, bf16[16,4,16,768]{3,2,1,0:T(8,128)(2,1)} %get-tuple-element.16.refs_1_.x_ref, ...), custom_call_target="tpu_custom_call" | custom-call | tf_op jit(solution)/shard_map/cond/branch_1_fun/pallas_call | solution.py:159
  41.6 0.1 collective-permute-start
  41.6 3.4 %collective-permute-done = f32[6,256,256]{2,1,0:T(8,128)S(1)} collective-permute-done((f32[6,256,256]{2,1,0:T(8,128)S(1)}, f32[6,256,256]{2,1,0:T(8,128)S(1)}, u32[]{:S(2)}, u32[]{:S(2)}) %collective-permute-start) | collective-permute-done | bytes 1572896 | tf_op jit(solution)/shard_map/cond/branch_1_fun/ppermute | solution.py:175
  45.0 0.7 branch_1_fun.6
  45.8 1.6 collective-permute-start.1
  47.3 1.1 collective-permute-start.2
  48.4 2.2 %collective-permute-start.3 = (f32[384,256]{1,0:T(8,128)S(1)}, f32[384,256]{1,0:T(8,128)S(1)}, u32[]{:S(2)}, u32[]{:S(2)}) collective-permute-start(f32[384,256]{1,0:T(8,128)S(1)} %get-tuple-element.27), channel_id=1, source_target_pairs={{0,96},{1,97},{2,98},{3,99},{4,100},{5,101},{6,102},{7,103},{8,104... | collective-permute-start | bytes 1179656 | tf_op jit(solution)/shard_map/cond/branch_1_fun/ppermute | solution.py:212
  50.6 2.6 %branch_1_fun.5 = bf16[12,256,256]{2,1,0:T(8,128)(2,1)} custom-call(bf16[16,4,16,768]{3,2,1,0:T(8,128)(2,1)S(1)} %copy-done.1, bf16[768,768]{1,0:T(8,128)(2,1)S(1)} %copy-done.5), custom_call_target="tpu_custom_call" | custom-call | tf_op jit(solution)/shard_map/cond/branch_1_fun/pallas_call | solution.py:159
  53.2 0.4 collective-permute-done.1.refs_1_
  53.6 3.1 %collective-permute-done.2.refs_2_ = f32[384,256]{1,0:T(8,128)S(1)} collective-permute-done((f32[384,256]{1,0:T(8,128)S(1)}, f32[384,256]{1,0:T(8,128)S(1)}, u32[]{:S(2)}, u32[]{:S(2)}) %collective-permute-start.2) | collective-permute-done | bytes 393248 | tf_op jit(solution)/shard_map/cond/branch_1_fun/ppermute | solution.py:212
  56.7 3.7 %collective-permute-done.3.refs_3_ = f32[384,256]{1,0:T(8,128)S(1)} collective-permute-done((f32[384,256]{1,0:T(8,128)S(1)}, f32[384,256]{1,0:T(8,128)S(1)}, u32[]{:S(2)}, u32[]{:S(2)}) %collective-permute-start.3) | collective-permute-done | bytes 393248 | tf_op jit(solution)/shard_map/cond/branch_1_fun/ppermute | solution.py:212
  60.4 0.1 branch_1_fun.7
  60.5 0.0 all-to-all-done.1.c_ref
  60.5 3.0 %shard_map.64 = (bf16[12,256,256]{2,1,0:T(8,128)(2,1)S(1)}, f32[6,256,256]{2,1,0:T(8,128)S(1)}, f32[6,256,256]{2,1,0:T(8,128)S(1)}) custom-call(s32[4]{0:T(128)S(1)} %pad_add_fusion.place_ref, bf16[16,4,16,768]{3,2,1,0:T(8,128)(2,1)S(1)} %all-to-all-done.1.c_ref, bf16[768,768]{1,0:T(8,128)(2,1)S(1)} %copy-done, bf16[12,256,256]{2,1,0:T(8,128)(2,1)} %get-tuple-element.44.v_in), custom_call_target="tpu_custom_call" | custom-call | tf_op jit(solution)/shard_map/pallas_call | solution.py:159
  63.5 2.2 %collective-permute-start.4 = (f32[6,256,256]{2,1,0:T(8,128)S(1)}, f32[6,256,256]{2,1,0:T(8,128)S(1)}, u32[]{:S(2)}, u32[]{:S(2)}) collective-permute-start(f32[6,256,256]{2,1,0:T(8,128)S(1)} %get-tuple-element.46), channel_id=1, source_target_pairs={{0,16},{16,0},{1,17},{17,1},{2,18},{18,2},{3,19},{19,3},{4,20},{20... | collective-permute-start | bytes 4718600 | tf_op jit(solution)/shard_map/ppermute | solution.py:175
  65.7 3.0 %collective-permute-done.4 = f32[6,256,256]{2,1,0:T(8,128)S(1)} collective-permute-done((f32[6,256,256]{2,1,0:T(8,128)S(1)}, f32[6,256,256]{2,1,0:T(8,128)S(1)}, u32[]{:S(2)}, u32[]{:S(2)}) %collective-permute-start.4) | collective-permute-done | bytes 1572896 | tf_op jit(solution)/shard_map/ppermute | solution.py:175
  68.8 0.7 shard_map.65
  69.5 1.6 collective-permute-start.5
  71.0 1.1 collective-permute-start.6
  72.1 2.2 %collective-permute-start.7 = (bf16[384,256]{1,0:T(8,128)(2,1)S(1)}, bf16[384,256]{1,0:T(8,128)(2,1)S(1)}, u32[]{:S(2)}, u32[]{:S(2)}) collective-permute-start(bf16[384,256]{1,0:T(8,128)(2,1)S(1)} %get-tuple-element.50), channel_id=1, source_target_pairs={{0,96},{1,97},{2,98},{3,99},{4,100},{5,101},{6,102},{7,103},{8,104... | collective-permute-start | bytes 589832 | tf_op jit(solution)/shard_map/ppermute | solution.py:212
  74.3 0.9 collective-permute-done.5.refs_1_
  75.2 3.1 %collective-permute-done.6.refs_2_ = bf16[384,256]{1,0:T(8,128)(2,1)S(1)} collective-permute-done((bf16[384,256]{1,0:T(8,128)(2,1)S(1)}, bf16[384,256]{1,0:T(8,128)(2,1)S(1)}, u32[]{:S(2)}, u32[]{:S(2)}) %collective-permute-start.6) | collective-permute-done | bytes 196640 | tf_op jit(solution)/shard_map/ppermute | solution.py:212
  78.3 1.6 collective-permute-done.7.refs_3_
  79.9 0.6 shard_map.66
  80.6 0.0 copy-start.2
  80.6 0.0 copy-start.3
  80.6 2.7 %collective-permute-start.10 = (f32[192,256]{1,0:T(8,128)S(1)}, f32[192,256]{1,0:T(8,128)S(1)}, u32[]{:S(2)}, u32[]{:S(2)}) collective-permute-start(f32[192,256]{1,0:T(8,128)S(1)} %get-tuple-element.54), channel_id=1, source_target_pairs={{0,12},{1,13},{2,14},{3,15},{4,0},{5,1},{6,2},{7,3},{8,4},{9,5},{1... | collective-permute-start | bytes 589832 | tf_op jit(solution)/shard_map/ppermute | solution.py:212
  83.3 0.0 collective-permute-start.8
  83.3 2.3 %collective-permute-start.9 = (f32[192,256]{1,0:T(8,128)S(1)}, f32[192,256]{1,0:T(8,128)S(1)}, u32[]{:S(2)}, u32[]{:S(2)}) collective-permute-start(f32[192,256]{1,0:T(8,128)S(1)} %get-tuple-element.53), channel_id=1, source_target_pairs={{0,8},{1,9},{2,10},{3,11},{4,12},{5,13},{6,14},{7,15},{8,0},{9,1},... | collective-permute-start | bytes 589832 | tf_op jit(solution)/shard_map/ppermute | solution.py:212
  85.5 0.9 collective-permute-done.10.refs_3_
  86.4 6.6 %collective-permute-done.8.refs_1_ = f32[192,256]{1,0:T(8,128)S(1)} collective-permute-done((f32[192,256]{1,0:T(8,128)S(1)}, f32[192,256]{1,0:T(8,128)S(1)}, u32[]{:S(2)}, u32[]{:S(2)}) %collective-permute-start.8) | collective-permute-done | bytes 196640 | tf_op jit(solution)/shard_map/ppermute | solution.py:212
  93.0 0.0 collective-permute-done.9.refs_2_
  93.1 0.9 collective-permute-start.11
  94.0 1.1 collective-permute-start.12
  95.1 1.7 %collective-permute-start.13 = (f32[192,256]{1,0:T(8,128)S(1)}, f32[192,256]{1,0:T(8,128)S(1)}, u32[]{:S(2)}, u32[]{:S(2)}) collective-permute-start(f32[192,256]{1,0:T(8,128)S(1)} %shard_map.67.refs_0_), channel_id=1, source_target_pairs={{0,3},{1,0},{2,1},{3,2},{4,7},{5,4},{6,5},{7,6},{8,11},{9,8},{10,9... | collective-permute-start | bytes 589832 | tf_op jit(solution)/shard_map/ppermute | solution.py:212
  96.7 5.4 %collective-permute-done.11.refs_1_ = f32[192,256]{1,0:T(8,128)S(1)} collective-permute-done((f32[192,256]{1,0:T(8,128)S(1)}, f32[192,256]{1,0:T(8,128)S(1)}, u32[]{:S(2)}, u32[]{:S(2)}) %collective-permute-start.11) | collective-permute-done | bytes 196640 | tf_op jit(solution)/shard_map/ppermute | solution.py:212
  102.1 0.0 collective-permute-done.12.refs_2_
  102.1 0.9 collective-permute-done.13.refs_3_
  103.0 0.3 shard_map.68.refs_0_
  103.3 0.1 collective-permute-start.14
  103.4 2.1 %collective-permute-start.15 = (bf16[192,256]{1,0:T(8,128)(2,1)S(1)}, bf16[192,256]{1,0:T(8,128)(2,1)S(1)}, u32[]{:S(2)}, u32[]{:S(2)}) collective-permute-start(bf16[192,256]{1,0:T(8,128)(2,1)S(1)} %shard_map.68.refs_0_), channel_id=1, source_target_pairs={{0,8},{1,9},{2,10},{3,11},{4,12},{5,13},{6,14},{7,15},{8,0},{9,1},... | collective-permute-start | bytes 294920 | tf_op jit(solution)/shard_map/ppermute | solution.py:212
  105.5 1.2 collective-permute-start.16
  106.6 3.6 %collective-permute-done.14.refs_1_ = bf16[192,256]{1,0:T(8,128)(2,1)S(1)} collective-permute-done((bf16[192,256]{1,0:T(8,128)(2,1)S(1)}, bf16[192,256]{1,0:T(8,128)(2,1)S(1)}, u32[]{:S(2)}, u32[]{:S(2)}) %collective-permute-start.14) | collective-permute-done | bytes 98336 | tf_op jit(solution)/shard_map/ppermute | solution.py:212
  110.3 0.9 collective-permute-done.16.refs_3_
  111.2 0.6 shard_map.69.refs_0_
  111.8 1.0 collective-permute-start.17
  112.7 0.7 collective-permute-start.18
  113.4 1.9 %collective-permute-start.19 = (bf16[2,384,256]{2,1,0:T(8,128)(2,1)S(1)}, bf16[2,384,256]{2,1,0:T(8,128)(2,1)S(1)}, u32[]{:S(2)}, u32[]{:S(2)}) collective-permute-start(bf16[2,384,256]{2,1,0:T(8,128)(2,1)S(1)} %shard_map.69.refs_0_), channel_id=1, source_target_pairs={{0,96},{1,97},{2,98},{3,99},{4,100},{5,101},{6,102},{7,103},{8,104... | collective-permute-start | bytes 1179656 | tf_op jit(solution)/shard_map/ppermute | solution.py:212
  115.3 0.0 collective-permute-start.20
  115.3 4.4 %collective-permute-done.17.refs_1_ = bf16[2,384,256]{2,1,0:T(8,128)(2,1)S(1)} collective-permute-done((bf16[2,384,256]{2,1,0:T(8,128)(2,1)S(1)}, bf16[2,384,256]{2,1,0:T(8,128)(2,1)S(1)}, u32[]{:S(2)}, u32[]{:S(2)}) %collective-permute-start.17) | collective-permute-done | bytes 393248 | tf_op jit(solution)/shard_map/ppermute | solution.py:212
  119.8 2.3 %collective-permute-done.18.refs_2_ = bf16[2,384,256]{2,1,0:T(8,128)(2,1)S(1)} collective-permute-done((bf16[2,384,256]{2,1,0:T(8,128)(2,1)S(1)}, bf16[2,384,256]{2,1,0:T(8,128)(2,1)S(1)}, u32[]{:S(2)}, u32[]{:S(2)}) %collective-permute-start.18) | collective-permute-done | bytes 393248 | tf_op jit(solution)/shard_map/ppermute | solution.py:212
  122.1 0.0 collective-permute-start.22
  122.1 3.3 %collective-permute-done.19.refs_3_ = bf16[2,384,256]{2,1,0:T(8,128)(2,1)S(1)} collective-permute-done((bf16[2,384,256]{2,1,0:T(8,128)(2,1)S(1)}, bf16[2,384,256]{2,1,0:T(8,128)(2,1)S(1)}, u32[]{:S(2)}, u32[]{:S(2)}) %collective-permute-start.19) | collective-permute-done | bytes 393248 | tf_op jit(solution)/shard_map/ppermute | solution.py:212
  125.5 0.0 collective-permute-start.23
  125.5 0.0 collective-permute-done.20.refs_4_
  125.5 0.0 collective-permute-done.21.refs_5_
  125.5 1.7 %collective-permute-done.23.refs_7_ = bf16[2,384,256]{2,1,0:T(8,128)(2,1)S(1)} collective-permute-done((bf16[2,384,256]{2,1,0:T(8,128)(2,1)S(1)}, bf16[2,384,256]{2,1,0:T(8,128)(2,1)S(1)}, u32[]{:S(2)}, u32[]{:S(2)}) %collective-permute-start.23) | collective-permute-done | bytes 393248 | tf_op jit(solution)/shard_map/ppermute | solution.py:175
  127.2 8.3 %shard_map.70 = bf16[16,4,16,768]{3,2,1,0:T(8,128)(2,1)S(1)} custom-call(s32[4]{0:T(128)S(1)} %pad_add_fusion.place_ref, bf16[2,384,256]{2,1,0:T(8,128)(2,1)S(1)} %shard_map.69.refs_0_, bf16[2,384,256]{2,1,0:T(8,128)(2,1)S(1)} %collective-permute-done.17.refs_1_, bf16[2,384,256]{2,1,0:T(8,128)(2,1)S(1)} %collective-permute-done.18.refs_2_, ...), custom_call_target="tpu_custom_call" | custom-call | tf_op jit(solution)/shard_map/pallas_call | solution.py:159
  135.5 28.7 %all_to_all.16 = bf16[16,4,16,768]{3,2,1,0:T(8,128)(2,1)S(1)} all-to-all(bf16[16,4,16,768]{3,2,1,0:T(8,128)(2,1)S(1)} %shard_map.70), channel_id=1, replica_groups=mesh['x'=4,'core'=2,'z'=4,'y'=4] {'z','y'}, dimensions={0} | all-to-all | bytes 3145728 | tf_op jit(solution)/shard_map/all_to_all | solution.py:209
  164.1 1.1 copy.16
  (14 shorter events, 0.1 us)
Async XLA Ops:
  30.9 29.6 %all-to-all-start.1 = ((bf16[16,4,16,768]{3,2,1,0:T(8,128)(2,1)}), bf16[16,4,16,768]{3,2,1,0:T(8,128)(2,1)S(1)}, u32[]{:S(2)}, u32[]{:S(2)}) async-start(bf16[16,4,16,768]{3,2,1,0:T(8,128)(2,1)} %bitcast.7), calls=%async_computation.1 | async-start | bytes 3145728 | tf_op jit(solution)/shard_map/all_to_all | solution.py:209
  34.7 25.8 %copy-start = (bf16[768,768]{1,0:T(8,128)(2,1)S(1)}, bf16[768,768]{1,0:T(8,128)(2,1)}, u32[]{:S(2)}) copy-start(bf16[768,768]{1,0:T(8,128)(2,1)} %w_in.1) | copy-start | bytes 3538948
  41.6 3.5 %collective-permute-start = (f32[6,256,256]{2,1,0:T(8,128)S(1)}, f32[6,256,256]{2,1,0:T(8,128)S(1)}, u32[]{:S(2)}, u32[]{:S(2)}) collective-permute-start(f32[6,256,256]{2,1,0:T(8,128)S(1)} %get-tuple-element.23), channel_id=1, source_target_pairs={{0,16},{16,0},{1,17},{17,1},{2,18},{18,2},{3,19},{19,3},{4,20},{20... | collective-permute-start | bytes 4718600 | tf_op jit(solution)/shard_map/cond/branch_1_fun/ppermute | solution.py:175
  45.0 5.6 %copy-start.1 = (bf16[16,4,16,768]{3,2,1,0:T(8,128)(2,1)S(1)}, bf16[16,4,16,768]{3,2,1,0:T(8,128)(2,1)}, u32[]{:S(2)}) copy-start(bf16[16,4,16,768]{3,2,1,0:T(8,128)(2,1)} %get-tuple-element.16.refs_1_.x_ref) | copy-start | bytes 4718596 | tf_op jit(solution)/shard_map/cond
  45.0 5.6 %copy-start.5 = (bf16[768,768]{1,0:T(8,128)(2,1)S(1)}, bf16[768,768]{1,0:T(8,128)(2,1)}, u32[]{:S(2)}) copy-start(bf16[768,768]{1,0:T(8,128)(2,1)} %get-tuple-element.21.w_ref) | copy-start | bytes 3538948 | tf_op jit(solution)/shard_map/cond
  45.8 7.8 %collective-permute-start.1 = (f32[384,256]{1,0:T(8,128)S(1)}, f32[384,256]{1,0:T(8,128)S(1)}, u32[]{:S(2)}, u32[]{:S(2)}) collective-permute-start(f32[384,256]{1,0:T(8,128)S(1)} %get-tuple-element.25), channel_id=1, source_target_pairs={{0,32},{1,33},{2,34},{3,35},{4,36},{5,37},{6,38},{7,39},{8,40},{9,... | collective-permute-start | bytes 1179656 | tf_op jit(solution)/shard_map/cond/branch_1_fun/ppermute | solution.py:212
  47.3 9.4 %collective-permute-start.2 = (f32[384,256]{1,0:T(8,128)S(1)}, f32[384,256]{1,0:T(8,128)S(1)}, u32[]{:S(2)}, u32[]{:S(2)}) collective-permute-start(f32[384,256]{1,0:T(8,128)S(1)} %get-tuple-element.26), channel_id=1, source_target_pairs={{0,64},{1,65},{2,66},{3,67},{4,68},{5,69},{6,70},{7,71},{8,72},{9,... | collective-permute-start | bytes 1179656 | tf_op jit(solution)/shard_map/cond/branch_1_fun/ppermute | solution.py:212
  48.4 12.0 %collective-permute-start.3 = (f32[384,256]{1,0:T(8,128)S(1)}, f32[384,256]{1,0:T(8,128)S(1)}, u32[]{:S(2)}, u32[]{:S(2)}) collective-permute-start(f32[384,256]{1,0:T(8,128)S(1)} %get-tuple-element.27), channel_id=1, source_target_pairs={{0,96},{1,97},{2,98},{3,99},{4,100},{5,101},{6,102},{7,103},{8,104... | collective-permute-start | bytes 1179656 | tf_op jit(solution)/shard_map/cond/branch_1_fun/ppermute | solution.py:212
  63.5 5.3 %collective-permute-start.4 = (f32[6,256,256]{2,1,0:T(8,128)S(1)}, f32[6,256,256]{2,1,0:T(8,128)S(1)}, u32[]{:S(2)}, u32[]{:S(2)}) collective-permute-start(f32[6,256,256]{2,1,0:T(8,128)S(1)} %get-tuple-element.46), channel_id=1, source_target_pairs={{0,16},{16,0},{1,17},{17,1},{2,18},{18,2},{3,19},{19,3},{4,20},{20... | collective-permute-start | bytes 4718600 | tf_op jit(solution)/shard_map/ppermute | solution.py:175
  69.5 5.7 %collective-permute-start.5 = (bf16[384,256]{1,0:T(8,128)(2,1)S(1)}, bf16[384,256]{1,0:T(8,128)(2,1)S(1)}, u32[]{:S(2)}, u32[]{:S(2)}) collective-permute-start(bf16[384,256]{1,0:T(8,128)(2,1)S(1)} %get-tuple-element.48), channel_id=1, source_target_pairs={{0,32},{1,33},{2,34},{3,35},{4,36},{5,37},{6,38},{7,39},{8,40},{9,... | collective-permute-start | bytes 589832 | tf_op jit(solution)/shard_map/ppermute | solution.py:212
  71.0 7.3 %collective-permute-start.6 = (bf16[384,256]{1,0:T(8,128)(2,1)S(1)}, bf16[384,256]{1,0:T(8,128)(2,1)S(1)}, u32[]{:S(2)}, u32[]{:S(2)}) collective-permute-start(bf16[384,256]{1,0:T(8,128)(2,1)S(1)} %get-tuple-element.49), channel_id=1, source_target_pairs={{0,64},{1,65},{2,66},{3,67},{4,68},{5,69},{6,70},{7,71},{8,72},{9,... | collective-permute-start | bytes 589832 | tf_op jit(solution)/shard_map/ppermute | solution.py:212
  72.1 7.8 %collective-permute-start.7 = (bf16[384,256]{1,0:T(8,128)(2,1)S(1)}, bf16[384,256]{1,0:T(8,128)(2,1)S(1)}, u32[]{:S(2)}, u32[]{:S(2)}) collective-permute-start(bf16[384,256]{1,0:T(8,128)(2,1)S(1)} %get-tuple-element.50), channel_id=1, source_target_pairs={{0,96},{1,97},{2,98},{3,99},{4,100},{5,101},{6,102},{7,103},{8,104... | collective-permute-start | bytes 589832 | tf_op jit(solution)/shard_map/ppermute | solution.py:212
  79.9 47.3 %copy-start.4 = (bf16[768,768]{1,0:T(8,128)(2,1)S(1)}, bf16[768,768]{1,0:T(8,128)(2,1)}, u32[]{:S(2)}) copy-start(bf16[768,768]{1,0:T(8,128)(2,1)} %refs_13_.1) | copy-start | bytes 3538948
  80.6 46.6 %copy-start.2 = (bf16[768,768]{1,0:T(8,128)(2,1)S(1)}, bf16[768,768]{1,0:T(8,128)(2,1)}, u32[]{:S(2)}) copy-start(bf16[768,768]{1,0:T(8,128)(2,1)} %refs_11_.1) | copy-start | bytes 3538948
  80.6 46.6 %copy-start.3 = (bf16[768,768]{1,0:T(8,128)(2,1)S(1)}, bf16[768,768]{1,0:T(8,128)(2,1)}, u32[]{:S(2)}) copy-start(bf16[768,768]{1,0:T(8,128)(2,1)} %refs_12_.1) | copy-start | bytes 3538948
  80.6 5.9 %collective-permute-start.10 = (f32[192,256]{1,0:T(8,128)S(1)}, f32[192,256]{1,0:T(8,128)S(1)}, u32[]{:S(2)}, u32[]{:S(2)}) collective-permute-start(f32[192,256]{1,0:T(8,128)S(1)} %get-tuple-element.54), channel_id=1, source_target_pairs={{0,12},{1,13},{2,14},{3,15},{4,0},{5,1},{6,2},{7,3},{8,4},{9,5},{1... | collective-permute-start | bytes 589832 | tf_op jit(solution)/shard_map/ppermute | solution.py:212
  83.3 9.8 %collective-permute-start.8 = (f32[192,256]{1,0:T(8,128)S(1)}, f32[192,256]{1,0:T(8,128)S(1)}, u32[]{:S(2)}, u32[]{:S(2)}) collective-permute-start(f32[192,256]{1,0:T(8,128)S(1)} %get-tuple-element.52), channel_id=1, source_target_pairs={{0,4},{1,5},{2,6},{3,7},{4,8},{5,9},{6,10},{7,11},{8,12},{9,13},{1... | collective-permute-start | bytes 589832 | tf_op jit(solution)/shard_map/ppermute | solution.py:212
  83.3 9.8 %collective-permute-start.9 = (f32[192,256]{1,0:T(8,128)S(1)}, f32[192,256]{1,0:T(8,128)S(1)}, u32[]{:S(2)}, u32[]{:S(2)}) collective-permute-start(f32[192,256]{1,0:T(8,128)S(1)} %get-tuple-element.53), channel_id=1, source_target_pairs={{0,8},{1,9},{2,10},{3,11},{4,12},{5,13},{6,14},{7,15},{8,0},{9,1},... | collective-permute-start | bytes 589832 | tf_op jit(solution)/shard_map/ppermute | solution.py:212
  93.1 9.1 %collective-permute-start.11 = (f32[192,256]{1,0:T(8,128)S(1)}, f32[192,256]{1,0:T(8,128)S(1)}, u32[]{:S(2)}, u32[]{:S(2)}) collective-permute-start(f32[192,256]{1,0:T(8,128)S(1)} %shard_map.67.refs_0_), channel_id=1, source_target_pairs={{0,1},{1,2},{2,3},{3,0},{4,5},{5,6},{6,7},{7,4},{8,9},{9,10},{10,1... | collective-permute-start | bytes 589832 | tf_op jit(solution)/shard_map/ppermute | solution.py:212
  94.0 8.2 %collective-permute-start.12 = (f32[192,256]{1,0:T(8,128)S(1)}, f32[192,256]{1,0:T(8,128)S(1)}, u32[]{:S(2)}, u32[]{:S(2)}) collective-permute-start(f32[192,256]{1,0:T(8,128)S(1)} %shard_map.67.refs_0_), channel_id=1, source_target_pairs={{0,2},{1,3},{2,0},{3,1},{4,6},{5,7},{6,4},{7,5},{8,10},{9,11},{10,... | collective-permute-start | bytes 589832 | tf_op jit(solution)/shard_map/ppermute | solution.py:212
  95.1 8.0 %collective-permute-start.13 = (f32[192,256]{1,0:T(8,128)S(1)}, f32[192,256]{1,0:T(8,128)S(1)}, u32[]{:S(2)}, u32[]{:S(2)}) collective-permute-start(f32[192,256]{1,0:T(8,128)S(1)} %shard_map.67.refs_0_), channel_id=1, source_target_pairs={{0,3},{1,0},{2,1},{3,2},{4,7},{5,4},{6,5},{7,6},{8,11},{9,8},{10,9... | collective-permute-start | bytes 589832 | tf_op jit(solution)/shard_map/ppermute | solution.py:212
  103.3 7.0 %collective-permute-start.14 = (bf16[192,256]{1,0:T(8,128)(2,1)S(1)}, bf16[192,256]{1,0:T(8,128)(2,1)S(1)}, u32[]{:S(2)}, u32[]{:S(2)}) collective-permute-start(bf16[192,256]{1,0:T(8,128)(2,1)S(1)} %shard_map.68.refs_0_), channel_id=1, source_target_pairs={{0,4},{1,5},{2,6},{3,7},{4,8},{5,9},{6,10},{7,11},{8,12},{9,13},{1... | collective-permute-start | bytes 294920 | tf_op jit(solution)/shard_map/ppermute | solution.py:212
  103.4 6.9 %collective-permute-start.15 = (bf16[192,256]{1,0:T(8,128)(2,1)S(1)}, bf16[192,256]{1,0:T(8,128)(2,1)S(1)}, u32[]{:S(2)}, u32[]{:S(2)}) collective-permute-start(bf16[192,256]{1,0:T(8,128)(2,1)S(1)} %shard_map.68.refs_0_), channel_id=1, source_target_pairs={{0,8},{1,9},{2,10},{3,11},{4,12},{5,13},{6,14},{7,15},{8,0},{9,1},... | collective-permute-start | bytes 294920 | tf_op jit(solution)/shard_map/ppermute | solution.py:212
  105.5 5.7 %collective-permute-start.16 = (bf16[192,256]{1,0:T(8,128)(2,1)S(1)}, bf16[192,256]{1,0:T(8,128)(2,1)S(1)}, u32[]{:S(2)}, u32[]{:S(2)}) collective-permute-start(bf16[192,256]{1,0:T(8,128)(2,1)S(1)} %shard_map.68.refs_0_), channel_id=1, source_target_pairs={{0,12},{1,13},{2,14},{3,15},{4,0},{5,1},{6,2},{7,3},{8,4},{9,5},{1... | collective-permute-start | bytes 294920 | tf_op jit(solution)/shard_map/ppermute | solution.py:212
  111.8 8.0 %collective-permute-start.17 = (bf16[2,384,256]{2,1,0:T(8,128)(2,1)S(1)}, bf16[2,384,256]{2,1,0:T(8,128)(2,1)S(1)}, u32[]{:S(2)}, u32[]{:S(2)}) collective-permute-start(bf16[2,384,256]{2,1,0:T(8,128)(2,1)S(1)} %shard_map.69.refs_0_), channel_id=1, source_target_pairs={{0,32},{1,33},{2,34},{3,35},{4,36},{5,37},{6,38},{7,39},{8,40},{9,... | collective-permute-start | bytes 1179656 | tf_op jit(solution)/shard_map/ppermute | solution.py:212
  112.7 9.4 %collective-permute-start.18 = (bf16[2,384,256]{2,1,0:T(8,128)(2,1)S(1)}, bf16[2,384,256]{2,1,0:T(8,128)(2,1)S(1)}, u32[]{:S(2)}, u32[]{:S(2)}) collective-permute-start(bf16[2,384,256]{2,1,0:T(8,128)(2,1)S(1)} %shard_map.69.refs_0_), channel_id=1, source_target_pairs={{0,64},{1,65},{2,66},{3,67},{4,68},{5,69},{6,70},{7,71},{8,72},{9,... | collective-permute-start | bytes 1179656 | tf_op jit(solution)/shard_map/ppermute | solution.py:212
  113.4 12.1 %collective-permute-start.19 = (bf16[2,384,256]{2,1,0:T(8,128)(2,1)S(1)}, bf16[2,384,256]{2,1,0:T(8,128)(2,1)S(1)}, u32[]{:S(2)}, u32[]{:S(2)}) collective-permute-start(bf16[2,384,256]{2,1,0:T(8,128)(2,1)S(1)} %shard_map.69.refs_0_), channel_id=1, source_target_pairs={{0,96},{1,97},{2,98},{3,99},{4,100},{5,101},{6,102},{7,103},{8,104... | collective-permute-start | bytes 1179656 | tf_op jit(solution)/shard_map/ppermute | solution.py:212
  115.3 10.1 %collective-permute-start.20 = (bf16[2,384,256]{2,1,0:T(8,128)(2,1)S(1)}, bf16[2,384,256]{2,1,0:T(8,128)(2,1)S(1)}, u32[]{:S(2)}, u32[]{:S(2)}) collective-permute-start(bf16[2,384,256]{2,1,0:T(8,128)(2,1)S(1)} %shard_map.69.refs_0_), channel_id=1, source_target_pairs={{0,16},{16,0},{1,17},{17,1},{2,18},{18,2},{3,19},{19,3},{4,20},{20... | collective-permute-start | bytes 1179656 | tf_op jit(solution)/shard_map/ppermute | solution.py:175
  119.8 5.7 %collective-permute-start.21 = (bf16[2,384,256]{2,1,0:T(8,128)(2,1)S(1)}, bf16[2,384,256]{2,1,0:T(8,128)(2,1)S(1)}, u32[]{:S(2)}, u32[]{:S(2)}) collective-permute-start(bf16[2,384,256]{2,1,0:T(8,128)(2,1)S(1)} %collective-permute-done.17.refs_1_), channel_id=1, source_target_pairs={{0,16},{16,0},{1,17},{17,1},{2,18},{18,2},{3,19},{19,3},{4,20},{20... | collective-permute-start | bytes 1179656 | tf_op jit(solution)/shard_map/ppermute | solution.py:175
  122.1 3.3 %collective-permute-start.22 = (bf16[2,384,256]{2,1,0:T(8,128)(2,1)S(1)}, bf16[2,384,256]{2,1,0:T(8,128)(2,1)S(1)}, u32[]{:S(2)}, u32[]{:S(2)}) collective-permute-start(bf16[2,384,256]{2,1,0:T(8,128)(2,1)S(1)} %collective-permute-done.18.refs_2_), channel_id=1, source_target_pairs={{0,16},{16,0},{1,17},{17,1},{2,18},{18,2},{3,19},{19,3},{4,20},{20... | collective-permute-start | bytes 1179656 | tf_op jit(solution)/shard_map/ppermute | solution.py:175
  125.5 1.7 %collective-permute-start.23 = (bf16[2,384,256]{2,1,0:T(8,128)(2,1)S(1)}, bf16[2,384,256]{2,1,0:T(8,128)(2,1)S(1)}, u32[]{:S(2)}, u32[]{:S(2)}) collective-permute-start(bf16[2,384,256]{2,1,0:T(8,128)(2,1)S(1)} %collective-permute-done.19.refs_3_), channel_id=1, source_target_pairs={{0,16},{16,0},{1,17},{17,1},{2,18},{18,2},{3,19},{19,3},{4,20},{20... | collective-permute-start | bytes 1179656 | tf_op jit(solution)/shard_map/ppermute | solution.py:175

commit v3 on v2

--- a/solution.py
+++ b/solution.py
@@ -12,6 +12,7 @@
 BF16 = jnp.bfloat16
 VMEM = pl.BlockSpec(memory_space=pltpu.VMEM)
 SMEM = pl.BlockSpec(memory_space=pltpu.SMEM)
+ANY = pl.BlockSpec(memory_space=pl.ANY)
 HBM = pl.BlockSpec(memory_space=pltpu.HBM)
 NT = (((1,), (1,)), ((), ()))
 TN = (((0,), (0,)), ((), ()))
@@ -37,7 +38,7 @@
     for h in range(half):
         for ref, base in ((own_ref, core * half), (other_ref, (1 - core) * half)):
             product = dot(a_ref[base + h], b_ref[base + h], TN)
-            ref[h] = product if scale is None else scale * product
+            ref[h] = (product if scale is None else scale * product).astype(ref.dtype)
 
 
 def start(pairs, sems):
@@ -47,13 +48,17 @@
     return copies
 
 
-def rows_kernel(scale, place_ref, x_ref, wq_in, wk_in, q_out, k_out, own_ref, other_ref, wq, wk, t_ref, q_ref, k_ref, in_sems, out_sems):
-    loads = start(((wq_in, wq), (wk_in, wk)), in_sems)
-    for load, w, o_ref in zip(loads, (wq, wk), (q_ref, k_ref)):
-        load.wait()
-        t_ref[...] = w[...].T
-        project(x_ref, ((t_ref, o_ref),))
-    stores = start(((q_ref, q_out), (k_ref, k_out)), out_sems)
+def rows_kernel(scale, place_ref, x_in, wq_in, wk_in, q_out, k_out, own_ref, other_ref, wq, wk, t_ref, x_ref, q_ref, k_ref, in_sems, out_sems):
+    loads = start(((wq_in, wq), (x_in, x_ref), (wk_in, wk)), in_sems)
+    loads[0].wait()
+    t_ref[...] = wq[...].T
+    loads[1].wait()
+    project(x_ref, ((t_ref, q_ref),))
+    stores = start(((q_ref, q_out),), out_sems.at[pl.ds(0, 1)])
+    loads[2].wait()
+    t_ref[...] = wk[...].T
+    project(x_ref, ((t_ref, k_ref),))
+    stores += start(((k_ref, k_out),), out_sems.at[pl.ds(1, 1)])
     pair_products(place_ref[0], scale, q_ref, k_ref, own_ref, other_ref)
     for store in stores:
         store.wait()
@@ -108,8 +113,14 @@
     out_ref[pl.ds(rows, rows)] = (scaling * weights * (grad - row_dot)).astype(BF16)
 
 
+def fetch_kernel(*refs):
+    count = (len(refs) - 1) // 2
+    for copy in start(list(zip(refs[:count], refs[count:-1])), refs[-1]):
+        copy.wait()
+
+
 def join_kernel(place_ref, *refs):
-    parts, out_ref = refs[:-1], refs[-1]
+    parts, out_ref = refs[:4], refs[-1]
     rows = out_ref.shape[1] // len(parts)
     for d, part_ref in enumerate(parts):
         first = lax.rem(place_ref[2] + len(parts) - d, len(parts)) * rows
@@ -118,14 +129,17 @@
             out_ref[term, at] = part_ref[pl.ds(term * rows, rows)]
 
 
-def head_grads(base, here, parts, q_ref, k_ref, g_ref, outs, stage_ref):
+def place_rows(here, parts, stage_ref):
     rows = parts[0].shape[1]
     for d, part_ref in enumerate(parts):
         first = lax.rem(here + len(parts) - d, len(parts)) * rows
-        stage_ref[:, pl.ds(pl.multiple_of(first, rows), rows)] = part_ref[...].astype(F32)
+        stage_ref[:, pl.ds(pl.multiple_of(first, rows), rows)] = part_ref[...]
+
+
+def head_grads(base, q_ref, k_ref, g_ref, outs, stage_ref):
     res = stage_ref.shape[-1]
     for h in range(q_ref.shape[0] // 2):
-        prob, logit_grad = (stage_ref[term, pl.ds(h * res, res)].astype(BF16) for term in range(2))
+        prob, logit_grad = (stage_ref[term, pl.ds(h * res, res)] for term in range(2))
         hh = base + h
         for o_ref, value in zip(
             outs,
@@ -135,17 +149,14 @@
 
 
 def output_kernel(place_ref, *refs):
-    own, other, held_in, weights_in, out_ref = refs[:4], refs[4:8], refs[8:11], refs[11:14], refs[14]
-    held, weights, outs, stage_ref, sems = refs[15:18], refs[18:21], refs[21:24], refs[24], refs[25]
-    loads = start(list(zip((*held_in, *weights_in), (*held, *weights))), sems)
-    for load in loads[:3]:
-        load.wait()
+    own, other, held, weights, out_ref = refs[:4], refs[4:8], refs[8:11], refs[11:14], refs[14]
+    outs, own_stage, other_stage = refs[15:18], refs[18], refs[19]
     core = place_ref[0]
     half = held[0].shape[0] // 2
-    head_grads(core * half, place_ref[1], own, *held, outs, stage_ref)
-    head_grads((1 - core) * half, place_ref[3], other, *held, outs, stage_ref)
-    for load in loads[3:]:
-        load.wait()
+    place_rows(place_ref[1], own, own_stage)
+    head_grads(core * half, *held, outs, own_stage)
+    place_rows(place_ref[3], other, other_stage)
+    head_grads((1 - core) * half, *held, outs, other_stage)
     res = held[0].shape[-1]
     for s in range(out_ref.shape[1]):
         total = None
@@ -234,8 +245,12 @@
             lambda *refs: rows_kernel(scaling, *refs),
             (packed, packed, sums, sums),
             place, rows, *weights[:2],
-            specs=(SMEM, VMEM, HBM, HBM), out_specs=(HBM, HBM, VMEM, VMEM),
-            scratch=[weight] * 3 + [held] * 2 + [sems((2,)), sems((2,))], mib=24,
+            specs=(SMEM, HBM, HBM, HBM), out_specs=(HBM, HBM, VMEM, VMEM),
+            scratch=[weight] * 3
+            + [pltpu.VMEM((blocks, seqs, block, width), BF16)]
+            + [held] * 2
+            + [sems((3,)), sems((2,))],
+            mib=24,
         )
         v = call(value_kernel, packed, rows, weights[2], scratch=[weight])
         return q, k, v, call(sum_kernel, shape(quarter, F32), *spread(split(F32, own, other), 0))
@@ -245,7 +260,7 @@
 
     q, k, v, logit = lax.cond(core < 2, row_part, no_part, rows, w_query, w_key, w_value)
     g, grad_own, grad_other = call(
-        grad_rows_kernel, (packed, sums, sums), place, cot_rows, w_out, v,
+        grad_rows_kernel, (packed, sums, shape(sums.shape)), place, cot_rows, w_out, v,
         specs=(SMEM, VMEM, HBM, HBM), out_specs=(HBM, VMEM, VMEM),
         scratch=[weight, held, held, sems((2,)), sems((1,))],
     )
@@ -258,8 +273,12 @@
     result = call(
         lambda *refs: softmax_kernel(scaling, *refs), shape(both), *spread([term] * 4, 2)
     )
+    q, k, g = call(
+        fetch_kernel, [packed] * 3, q, k, g, specs=[HBM] * 3, scratch=[sems((3,))]
+    )
     result = call(
-        join_kernel, shape((2,) + quarter), place, *spread([result] * 4, 1), specs=[SMEM] + [VMEM] * 4
+        join_kernel, shape((2,) + quarter), place, *spread([result] * 4, 1), q,
+        specs=[SMEM] + [VMEM] * 4 + [ANY],
     )
     own = spread([result] * 4, 0)
     other = [shift(a, "core", 1) for a in own]
@@ -268,10 +287,9 @@
         output_kernel,
         shape((blocks, seqs, block, width)),
         place, *own, *other, q, k, g, w_query, w_key, w_value,
-        specs=[SMEM] + [VMEM] * 8 + [HBM] * 6,
-        scratch=[held] * 3 + [weight] * 3 + [grown] * 3
-        + [pltpu.VMEM((2, half * res, res), F32), sems((6,))],
-        mib=40,
+        specs=[SMEM] + [VMEM] * 14,
+        scratch=[grown] * 3 + [pltpu.VMEM((2, half * res, res), BF16)] * 2,
+        mib=24,
     )
     return exchange(out).reshape(seq_count, block, width)
 

time: 166 us -> 162 us (0.976)
  waiting for transfers between devices: 49.5 us -> 40.5 us
  starting transfers between devices: 31.2 us -> 36.5 us
    ppermute x18, waiting for transfers between devices: 41.3 us -> 33.5 us  [spread(): sent = {d: lax.ppermute(parts[d], AXES, turn(stage, d)) for d in (1, 3, 2)}]
    ppermute x18, starting transfers between devices: 25.1 us -> 30.1 us  [spread(): sent = {d: lax.ppermute(parts[d], AXES, turn(stage, d)) for d in (1, 3, 2)}]
    pallas_call x11 -> x12, Pallas kernels: 23.6 us -> 22.9 us  [call(): pl.pallas_call(kernel, out_shape=outs, in_specs=list(specs or [VMEM] * le...]
  transfers between devices with their start and end apart: 25 -> 25, of which waited for: 18 -> 18; matrix products, arithmetic and copies ran while one was open for 0% -> 0% of each run, Pallas kernels for 6% -> 7%
where the time goes in v3:
time: 162 us; the launch traced here: 161 us
  blocking collectives  60 us (37%)
  waiting for transfers between devices  40.5 us (25%)
  starting transfers between devices  36.5 us (23%)
  Pallas kernels  22.9 us (14%)
    all_to_all x2, blocking collectives, exchange(): lax.all_to_all(a, ('z', 'y'), split_axis=0, concat_axis=0, tiled=True)  60 us
    ppermute x18, waiting for transfers between devices, spread(): sent = {d: lax.ppermute(parts[d], AXES, turn(stage, d)) for d in (1, 3, 2)}  33.5 us
    ppermute x18, starting transfers between devices, spread(): sent = {d: lax.ppermute(parts[d], AXES, turn(stage, d)) for d in (1, 3, 2)}  30.1 us
    pallas_call x12, Pallas kernels, call(): pl.pallas_call(kernel, out_shape=outs, in_specs=list(specs or [VMEM] * le...  22.9 us
    ppermute x6, waiting for transfers between devices, shift(): return lax.ppermute(a, axis, [(i, (i + step) % n) for i in range(n)])  7.02 us
    all_to_all x1, starting transfers between devices, exchange(): lax.all_to_all(a, ('z', 'y'), split_axis=0, concat_axis=0, tiled=True)  3.71 us
  transfers between devices with their start and end apart: 25, of which 18 were waited for; matrix products, arithmetic and copies ran while one was open for 0% of the time, Pallas kernels for 7%

profile of v3, /device:TPU:2, one launch (start us, length us, event | category | flops | bytes accessed | tf_op | source)
XLA Modules:
  0.0 161.3 jit_solution(14417901200449016878)
XLA Ops:
  0.0 30.9 %all_to_all.15 = bf16[16,4,16,768]{3,2,1,0:T(8,128)(2,1)} all-to-all(bf16[16,4,16,768]{3,2,1,0:T(8,128)(2,1)} %bitcast.16), channel_id=1, replica_groups=mesh['x'=4,'core'=2,'z'=4,'y'=4] {'z','y'}, dimensions={0} | all-to-all | bytes 3145728 | tf_op jit(solution)/shard_map/all_to_all | solution.py:220
  30.9 3.7 %all-to-all-start.1 = ((bf16[16,4,16,768]{3,2,1,0:T(8,128)(2,1)}), bf16[16,4,16,768]{3,2,1,0:T(8,128)(2,1)S(1)}, u32[]{:S(2)}, u32[]{:S(2)}) async-start(bf16[16,4,16,768]{3,2,1,0:T(8,128)(2,1)} %bitcast.7), calls=%async_computation.1 | async-start | bytes 3145728 | tf_op jit(solution)/shard_map/all_to_all | solution.py:220
  34.7 0.1 pad_add_fusion.place_ref
  34.7 25.3 %conditional.1 = (bf16[12,256,256]{2,1,0:T(8,128)(2,1)}, bf16[12,256,256]{2,1,0:T(8,128)(2,1)}, bf16[12,256,256]{2,1,0:T(8,128)(2,1)}, f32[384,256]{1,0:T(8,128)S(1)}) conditional(s32[]{:T(128)} %convert_element_type.3, () %tuple.13, (s32[4]{0:T(128)S(1)}, bf16[16,4,16,768]{3,2,1,0:T(8,128)(2,1)}, bf16[768,768]{1,0:T(8,128)(2,1)}, ...), branch_computations={%region_0.1_spmd, %region_1.2_spmd} | conditional | bytes 22020344 | solution.py:261
  34.7 6.3 %branch_1_fun.4 = (bf16[12,256,256]{2,1,0:T(8,128)(2,1)}, bf16[12,256,256]{2,1,0:T(8,128)(2,1)}, f32[6,256,256]{2,1,0:T(8,128)S(1)}, f32[6,256,256]{2,1,0:T(8,128)S(1)}) custom-call(s32[4]{0:T(128)S(1)} %get-tuple-element.15.refs_0_.place_ref, bf16[16,4,16,768]{3,2,1,0:T(8,128)(2,1)} %get-tuple-element.16.refs_1_.x_ref, ...), custom_call_target="tpu_custom_call" | custom-call | tf_op jit(solution)/shard_map/cond/branch_1_fun/pallas_call | solution.py:170
  41.1 0.1 collective-permute-start
  41.2 3.4 %collective-permute-done = f32[6,256,256]{2,1,0:T(8,128)S(1)} collective-permute-done((f32[6,256,256]{2,1,0:T(8,128)S(1)}, f32[6,256,256]{2,1,0:T(8,128)S(1)}, u32[]{:S(2)}, u32[]{:S(2)}) %collective-permute-start) | collective-permute-done | bytes 1572896 | tf_op jit(solution)/shard_map/cond/branch_1_fun/ppermute | solution.py:186
  44.6 0.7 branch_1_fun.6
  45.3 1.6 collective-permute-start.1
  46.9 1.1 collective-permute-start.2
  48.0 2.2 %collective-permute-start.3 = (f32[384,256]{1,0:T(8,128)S(1)}, f32[384,256]{1,0:T(8,128)S(1)}, u32[]{:S(2)}, u32[]{:S(2)}) collective-permute-start(f32[384,256]{1,0:T(8,128)S(1)} %get-tuple-element.27), channel_id=1, source_target_pairs={{0,96},{1,97},{2,98},{3,99},{4,100},{5,101},{6,102},{7,103},{8,104... | collective-permute-start | bytes 1179656 | tf_op jit(solution)/shard_map/cond/branch_1_fun/ppermute | solution.py:223
  50.1 2.6 %branch_1_fun.5 = bf16[12,256,256]{2,1,0:T(8,128)(2,1)} custom-call(bf16[16,4,16,768]{3,2,1,0:T(8,128)(2,1)S(1)} %copy-done.1, bf16[768,768]{1,0:T(8,128)(2,1)S(1)} %copy-done.5), custom_call_target="tpu_custom_call" | custom-call | tf_op jit(solution)/shard_map/cond/branch_1_fun/pallas_call | solution.py:170
  52.7 0.5 collective-permute-done.1.refs_1_
  53.1 3.1 %collective-permute-done.2.refs_2_ = f32[384,256]{1,0:T(8,128)S(1)} collective-permute-done((f32[384,256]{1,0:T(8,128)S(1)}, f32[384,256]{1,0:T(8,128)S(1)}, u32[]{:S(2)}, u32[]{:S(2)}) %collective-permute-start.2) | collective-permute-done | bytes 393248 | tf_op jit(solution)/shard_map/cond/branch_1_fun/ppermute | solution.py:223
  56.2 3.7 %collective-permute-done.3.refs_3_ = f32[384,256]{1,0:T(8,128)S(1)} collective-permute-done((f32[384,256]{1,0:T(8,128)S(1)}, f32[384,256]{1,0:T(8,128)S(1)}, u32[]{:S(2)}, u32[]{:S(2)}) %collective-permute-start.3) | collective-permute-done | bytes 393248 | tf_op jit(solution)/shard_map/cond/branch_1_fun/ppermute | solution.py:223
  59.9 0.1 branch_1_fun.7
  60.0 0.0 all-to-all-done.1.c_ref
  60.0 3.0 %shard_map.64 = (bf16[12,256,256]{2,1,0:T(8,128)(2,1)S(1)}, f32[6,256,256]{2,1,0:T(8,128)S(1)}, bf16[6,256,256]{2,1,0:T(8,128)(2,1)S(1)}) custom-call(s32[4]{0:T(128)S(1)} %pad_add_fusion.place_ref, bf16[16,4,16,768]{3,2,1,0:T(8,128)(2,1)S(1)} %all-to-all-done.1.c_ref, bf16[768,768]{1,0:T(8,128)(2,1)S(1)} %copy-done, ...), custom_call_target="tpu_custom_call" | custom-call | tf_op jit(solution)/shard_map/pallas_call | solution.py:170
  63.0 2.6 %collective-permute-start.4 = (bf16[6,256,256]{2,1,0:T(8,128)(2,1)S(1)}, bf16[6,256,256]{2,1,0:T(8,128)(2,1)S(1)}, u32[]{:S(2)}, u32[]{:S(2)}) collective-permute-start(bf16[6,256,256]{2,1,0:T(8,128)(2,1)S(1)} %get-tuple-element.49), channel_id=1, source_target_pairs={{0,16},{16,0},{1,17},{17,1},{2,18},{18,2},{3,19},{19,3},{4,20},{20... | collective-permute-start | bytes 2359304 | tf_op jit(solution)/shard_map/ppermute | solution.py:186
  65.6 1.9 %collective-permute-done.4 = bf16[6,256,256]{2,1,0:T(8,128)(2,1)S(1)} collective-permute-done((bf16[6,256,256]{2,1,0:T(8,128)(2,1)S(1)}, bf16[6,256,256]{2,1,0:T(8,128)(2,1)S(1)}, u32[]{:S(2)}, u32[]{:S(2)}) %collective-permute-start.4) | collective-permute-done | bytes 786464 | tf_op jit(solution)/shard_map/ppermute | solution.py:186
  67.5 0.7 shard_map.65
  68.2 1.6 collective-permute-start.5
  69.7 1.1 collective-permute-start.6
  70.8 2.2 %collective-permute-start.7 = (bf16[384,256]{1,0:T(8,128)(2,1)S(1)}, bf16[384,256]{1,0:T(8,128)(2,1)S(1)}, u32[]{:S(2)}, u32[]{:S(2)}) collective-permute-start(bf16[384,256]{1,0:T(8,128)(2,1)S(1)} %get-tuple-element.53), channel_id=1, source_target_pairs={{0,96},{1,97},{2,98},{3,99},{4,100},{5,101},{6,102},{7,103},{8,104... | collective-permute-start | bytes 589832 | tf_op jit(solution)/shard_map/ppermute | solution.py:223
  73.0 0.9 collective-permute-done.5.refs_1_
  73.9 3.1 %collective-permute-done.6.refs_2_ = bf16[384,256]{1,0:T(8,128)(2,1)S(1)} collective-permute-done((bf16[384,256]{1,0:T(8,128)(2,1)S(1)}, bf16[384,256]{1,0:T(8,128)(2,1)S(1)}, u32[]{:S(2)}, u32[]{:S(2)}) %collective-permute-start.6) | collective-permute-done | bytes 196640 | tf_op jit(solution)/shard_map/ppermute | solution.py:223
  77.0 1.6 %collective-permute-done.7.refs_3_ = bf16[384,256]{1,0:T(8,128)(2,1)S(1)} collective-permute-done((bf16[384,256]{1,0:T(8,128)(2,1)S(1)}, bf16[384,256]{1,0:T(8,128)(2,1)S(1)}, u32[]{:S(2)}, u32[]{:S(2)}) %collective-permute-start.7) | collective-permute-done | bytes 196640 | tf_op jit(solution)/shard_map/ppermute | solution.py:223
  78.6 0.6 shard_map.66
  79.3 1.5 collective-permute-start.8
  80.8 2.7 %collective-permute-start.9 = (f32[192,256]{1,0:T(8,128)S(1)}, f32[192,256]{1,0:T(8,128)S(1)}, u32[]{:S(2)}, u32[]{:S(2)}) collective-permute-start(f32[192,256]{1,0:T(8,128)S(1)} %get-tuple-element.56), channel_id=1, source_target_pairs={{0,8},{1,9},{2,10},{3,11},{4,12},{5,13},{6,14},{7,15},{8,0},{9,1},... | collective-permute-start | bytes 589832 | tf_op jit(solution)/shard_map/ppermute | solution.py:223
  83.6 1.4 collective-permute-start.10
  85.0 1.2 collective-permute-done.8.refs_1_
  86.2 3.1 %collective-permute-done.9.refs_2_ = f32[192,256]{1,0:T(8,128)S(1)} collective-permute-done((f32[192,256]{1,0:T(8,128)S(1)}, f32[192,256]{1,0:T(8,128)S(1)}, u32[]{:S(2)}, u32[]{:S(2)}) %collective-permute-start.9) | collective-permute-done | bytes 196640 | tf_op jit(solution)/shard_map/ppermute | solution.py:223
  89.3 0.0 collective-permute-done.10.refs_3_
  89.4 0.8 collective-permute-start.11
  90.2 1.5 collective-permute-start.12
  91.7 2.4 %collective-permute-start.13 = (f32[192,256]{1,0:T(8,128)S(1)}, f32[192,256]{1,0:T(8,128)S(1)}, u32[]{:S(2)}, u32[]{:S(2)}) collective-permute-start(f32[192,256]{1,0:T(8,128)S(1)} %shard_map.67.refs_0_), channel_id=1, source_target_pairs={{0,3},{1,0},{2,1},{3,2},{4,7},{5,4},{6,5},{7,6},{8,11},{9,8},{10,9... | collective-permute-start | bytes 589832 | tf_op jit(solution)/shard_map/ppermute | solution.py:223
  94.0 4.4 %collective-permute-done.11.refs_1_ = f32[192,256]{1,0:T(8,128)S(1)} collective-permute-done((f32[192,256]{1,0:T(8,128)S(1)}, f32[192,256]{1,0:T(8,128)S(1)}, u32[]{:S(2)}, u32[]{:S(2)}) %collective-permute-start.11) | collective-permute-done | bytes 196640 | tf_op jit(solution)/shard_map/ppermute | solution.py:223
  98.4 0.0 collective-permute-done.12.refs_2_
  98.4 0.9 collective-permute-done.13.refs_3_
  99.3 0.3 shard_map.68.refs_0_
  99.5 2.0 %collective-permute-start.14 = (bf16[192,256]{1,0:T(8,128)(2,1)S(1)}, bf16[192,256]{1,0:T(8,128)(2,1)S(1)}, u32[]{:S(2)}, u32[]{:S(2)}) collective-permute-start(bf16[192,256]{1,0:T(8,128)(2,1)S(1)} %shard_map.68.refs_0_), channel_id=1, source_target_pairs={{0,4},{1,5},{2,6},{3,7},{4,8},{5,9},{6,10},{7,11},{8,12},{9,13},{1... | collective-permute-start | bytes 294920 | tf_op jit(solution)/shard_map/ppermute | solution.py:223
  101.5 2.1 %collective-permute-start.15 = (bf16[192,256]{1,0:T(8,128)(2,1)S(1)}, bf16[192,256]{1,0:T(8,128)(2,1)S(1)}, u32[]{:S(2)}, u32[]{:S(2)}) collective-permute-start(bf16[192,256]{1,0:T(8,128)(2,1)S(1)} %shard_map.68.refs_0_), channel_id=1, source_target_pairs={{0,8},{1,9},{2,10},{3,11},{4,12},{5,13},{6,14},{7,15},{8,0},{9,1},... | collective-permute-start | bytes 294920 | tf_op jit(solution)/shard_map/ppermute | solution.py:223
  103.6 1.5 collective-permute-start.16
  105.2 2.0 %shard_map.69 = (bf16[12,256,256]{2,1,0:T(8,128)(2,1)S(1)}, bf16[12,256,256]{2,1,0:T(8,128)(2,1)S(1)}, bf16[12,256,256]{2,1,0:T(8,128)(2,1)S(1)}) custom-call(bf16[12,256,256]{2,1,0:T(8,128)(2,1)} %get-tuple-element.58.refs_0_, bf16[12,256,256]{2,1,0:T(8,128)(2,1)} %get-tuple-element.59.refs_1_, bf16[12,256,256]{2,1,0:T(8,128)(2,1)S(1)} %get-tuple-element.60.refs_2_), custom_call_target="tpu_custom_call" | custom-call | tf_op jit(solution)/shard_map/pallas_call | solution.py:170
  107.2 0.0 copy-start.2
  107.2 0.0 copy-start.3
  107.2 0.0 collective-permute-done.14.refs_1_
  107.2 0.4 collective-permute-done.15.refs_2_
  107.6 0.6 collective-permute-done.16.refs_3_
  108.3 0.6 shard_map.70.refs_0_
  108.8 1.2 collective-permute-start.17
  110.1 1.2 collective-permute-start.18
  111.3 1.9 %collective-permute-start.19 = (bf16[2,384,256]{2,1,0:T(8,128)(2,1)S(1)}, bf16[2,384,256]{2,1,0:T(8,128)(2,1)S(1)}, u32[]{:S(2)}, u32[]{:S(2)}) collective-permute-start(bf16[2,384,256]{2,1,0:T(8,128)(2,1)S(1)} %shard_map.70.refs_0_), channel_id=1, source_target_pairs={{0,96},{1,97},{2,98},{3,99},{4,100},{5,101},{6,102},{7,103},{8,104... | collective-permute-start | bytes 1179656 | tf_op jit(solution)/shard_map/ppermute | solution.py:223
  113.2 0.0 collective-permute-start.20
  113.2 3.6 %collective-permute-done.17.refs_1_ = bf16[2,384,256]{2,1,0:T(8,128)(2,1)S(1)} collective-permute-done((bf16[2,384,256]{2,1,0:T(8,128)(2,1)S(1)}, bf16[2,384,256]{2,1,0:T(8,128)(2,1)S(1)}, u32[]{:S(2)}, u32[]{:S(2)}) %collective-permute-start.17) | collective-permute-done | bytes 393248 | tf_op jit(solution)/shard_map/ppermute | solution.py:223
  116.9 2.6 %collective-permute-done.18.refs_2_ = bf16[2,384,256]{2,1,0:T(8,128)(2,1)S(1)} collective-permute-done((bf16[2,384,256]{2,1,0:T(8,128)(2,1)S(1)}, bf16[2,384,256]{2,1,0:T(8,128)(2,1)S(1)}, u32[]{:S(2)}, u32[]{:S(2)}) %collective-permute-start.18) | collective-permute-done | bytes 393248 | tf_op jit(solution)/shard_map/ppermute | solution.py:223
  119.5 0.0 collective-permute-start.22
  119.5 3.8 %collective-permute-done.19.refs_3_ = bf16[2,384,256]{2,1,0:T(8,128)(2,1)S(1)} collective-permute-done((bf16[2,384,256]{2,1,0:T(8,128)(2,1)S(1)}, bf16[2,384,256]{2,1,0:T(8,128)(2,1)S(1)}, u32[]{:S(2)}, u32[]{:S(2)}) %collective-permute-start.19) | collective-permute-done | bytes 393248 | tf_op jit(solution)/shard_map/ppermute | solution.py:223
  123.3 0.0 collective-permute-done.22.refs_6_
  123.3 1.7 %collective-permute-done.23.refs_7_ = bf16[2,384,256]{2,1,0:T(8,128)(2,1)S(1)} collective-permute-done((bf16[2,384,256]{2,1,0:T(8,128)(2,1)S(1)}, bf16[2,384,256]{2,1,0:T(8,128)(2,1)S(1)}, u32[]{:S(2)}, u32[]{:S(2)}) %collective-permute-start.23) | collective-permute-done | bytes 393248 | tf_op jit(solution)/shard_map/ppermute | solution.py:186
  125.0 6.0 %shard_map.71 = bf16[16,4,16,768]{3,2,1,0:T(8,128)(2,1)S(1)} custom-call(s32[4]{0:T(128)S(1)} %pad_add_fusion.place_ref, bf16[2,384,256]{2,1,0:T(8,128)(2,1)S(1)} %shard_map.70.refs_0_, bf16[2,384,256]{2,1,0:T(8,128)(2,1)S(1)} %collective-permute-done.17.refs_1_, bf16[2,384,256]{2,1,0:T(8,128)(2,1)S(1)} %collective-permute-done.18.refs_2_, ...), custom_call_target="tpu_custom_call" | custom-call | tf_op jit(solution)/shard_map/pallas_call | solution.py:170
  131.0 29.1 %all_to_all.16 = bf16[16,4,16,768]{3,2,1,0:T(8,128)(2,1)S(1)} all-to-all(bf16[16,4,16,768]{3,2,1,0:T(8,128)(2,1)S(1)} %shard_map.71), channel_id=1, replica_groups=mesh['x'=4,'core'=2,'z'=4,'y'=4] {'z','y'}, dimensions={0} | all-to-all | bytes 3145728 | tf_op jit(solution)/shard_map/all_to_all | solution.py:220
  160.1 1.1 copy.16
  (15 shorter events, 0.1 us)
Async XLA Ops:
  30.9 29.1 %all-to-all-start.1 = ((bf16[16,4,16,768]{3,2,1,0:T(8,128)(2,1)}), bf16[16,4,16,768]{3,2,1,0:T(8,128)(2,1)S(1)}, u32[]{:S(2)}, u32[]{:S(2)}) async-start(bf16[16,4,16,768]{3,2,1,0:T(8,128)(2,1)} %bitcast.7), calls=%async_computation.1 | async-start | bytes 3145728 | tf_op jit(solution)/shard_map/all_to_all | solution.py:220
  34.7 25.3 %copy-start = (bf16[768,768]{1,0:T(8,128)(2,1)S(1)}, bf16[768,768]{1,0:T(8,128)(2,1)}, u32[]{:S(2)}) copy-start(bf16[768,768]{1,0:T(8,128)(2,1)} %w_in.1) | copy-start | bytes 3538948
  41.1 3.5 %collective-permute-start = (f32[6,256,256]{2,1,0:T(8,128)S(1)}, f32[6,256,256]{2,1,0:T(8,128)S(1)}, u32[]{:S(2)}, u32[]{:S(2)}) collective-permute-start(f32[6,256,256]{2,1,0:T(8,128)S(1)} %get-tuple-element.23), channel_id=1, source_target_pairs={{0,16},{16,0},{1,17},{17,1},{2,18},{18,2},{3,19},{19,3},{4,20},{20... | collective-permute-start | bytes 4718600 | tf_op jit(solution)/shard_map/cond/branch_1_fun/ppermute | solution.py:186
  44.6 5.5 %copy-start.1 = (bf16[16,4,16,768]{3,2,1,0:T(8,128)(2,1)S(1)}, bf16[16,4,16,768]{3,2,1,0:T(8,128)(2,1)}, u32[]{:S(2)}) copy-start(bf16[16,4,16,768]{3,2,1,0:T(8,128)(2,1)} %get-tuple-element.16.refs_1_.x_ref) | copy-start | bytes 4718596 | tf_op jit(solution)/shard_map/cond
  44.6 5.5 %copy-start.5 = (bf16[768,768]{1,0:T(8,128)(2,1)S(1)}, bf16[768,768]{1,0:T(8,128)(2,1)}, u32[]{:S(2)}) copy-start(bf16[768,768]{1,0:T(8,128)(2,1)} %get-tuple-element.21.w_ref) | copy-start | bytes 3538948 | tf_op jit(solution)/shard_map/cond
  45.3 7.8 %collective-permute-start.1 = (f32[384,256]{1,0:T(8,128)S(1)}, f32[384,256]{1,0:T(8,128)S(1)}, u32[]{:S(2)}, u32[]{:S(2)}) collective-permute-start(f32[384,256]{1,0:T(8,128)S(1)} %get-tuple-element.25), channel_id=1, source_target_pairs={{0,32},{1,33},{2,34},{3,35},{4,36},{5,37},{6,38},{7,39},{8,40},{9,... | collective-permute-start | bytes 1179656 | tf_op jit(solution)/shard_map/cond/branch_1_fun/ppermute | solution.py:223
  46.9 9.4 %collective-permute-start.2 = (f32[384,256]{1,0:T(8,128)S(1)}, f32[384,256]{1,0:T(8,128)S(1)}, u32[]{:S(2)}, u32[]{:S(2)}) collective-permute-start(f32[384,256]{1,0:T(8,128)S(1)} %get-tuple-element.26), channel_id=1, source_target_pairs={{0,64},{1,65},{2,66},{3,67},{4,68},{5,69},{6,70},{7,71},{8,72},{9,... | collective-permute-start | bytes 1179656 | tf_op jit(solution)/shard_map/cond/branch_1_fun/ppermute | solution.py:223
  48.0 12.0 %collective-permute-start.3 = (f32[384,256]{1,0:T(8,128)S(1)}, f32[384,256]{1,0:T(8,128)S(1)}, u32[]{:S(2)}, u32[]{:S(2)}) collective-permute-start(f32[384,256]{1,0:T(8,128)S(1)} %get-tuple-element.27), channel_id=1, source_target_pairs={{0,96},{1,97},{2,98},{3,99},{4,100},{5,101},{6,102},{7,103},{8,104... | collective-permute-start | bytes 1179656 | tf_op jit(solution)/shard_map/cond/branch_1_fun/ppermute | solution.py:223
  63.0 4.5 %collective-permute-start.4 = (bf16[6,256,256]{2,1,0:T(8,128)(2,1)S(1)}, bf16[6,256,256]{2,1,0:T(8,128)(2,1)S(1)}, u32[]{:S(2)}, u32[]{:S(2)}) collective-permute-start(bf16[6,256,256]{2,1,0:T(8,128)(2,1)S(1)} %get-tuple-element.49), channel_id=1, source_target_pairs={{0,16},{16,0},{1,17},{17,1},{2,18},{18,2},{3,19},{19,3},{4,20},{20... | collective-permute-start | bytes 2359304 | tf_op jit(solution)/shard_map/ppermute | solution.py:186
  68.2 5.7 %collective-permute-start.5 = (bf16[384,256]{1,0:T(8,128)(2,1)S(1)}, bf16[384,256]{1,0:T(8,128)(2,1)S(1)}, u32[]{:S(2)}, u32[]{:S(2)}) collective-permute-start(bf16[384,256]{1,0:T(8,128)(2,1)S(1)} %get-tuple-element.51), channel_id=1, source_target_pairs={{0,32},{1,33},{2,34},{3,35},{4,36},{5,37},{6,38},{7,39},{8,40},{9,... | collective-permute-start | bytes 589832 | tf_op jit(solution)/shard_map/ppermute | solution.py:223
  69.7 7.3 %collective-permute-start.6 = (bf16[384,256]{1,0:T(8,128)(2,1)S(1)}, bf16[384,256]{1,0:T(8,128)(2,1)S(1)}, u32[]{:S(2)}, u32[]{:S(2)}) collective-permute-start(bf16[384,256]{1,0:T(8,128)(2,1)S(1)} %get-tuple-element.52), channel_id=1, source_target_pairs={{0,64},{1,65},{2,66},{3,67},{4,68},{5,69},{6,70},{7,71},{8,72},{9,... | collective-permute-start | bytes 589832 | tf_op jit(solution)/shard_map/ppermute | solution.py:223
  70.8 7.8 %collective-permute-start.7 = (bf16[384,256]{1,0:T(8,128)(2,1)S(1)}, bf16[384,256]{1,0:T(8,128)(2,1)S(1)}, u32[]{:S(2)}, u32[]{:S(2)}) collective-permute-start(bf16[384,256]{1,0:T(8,128)(2,1)S(1)} %get-tuple-element.53), channel_id=1, source_target_pairs={{0,96},{1,97},{2,98},{3,99},{4,100},{5,101},{6,102},{7,103},{8,104... | collective-permute-start | bytes 589832 | tf_op jit(solution)/shard_map/ppermute | solution.py:223
  79.3 7.0 %collective-permute-start.8 = (f32[192,256]{1,0:T(8,128)S(1)}, f32[192,256]{1,0:T(8,128)S(1)}, u32[]{:S(2)}, u32[]{:S(2)}) collective-permute-start(f32[192,256]{1,0:T(8,128)S(1)} %get-tuple-element.55), channel_id=1, source_target_pairs={{0,4},{1,5},{2,6},{3,7},{4,8},{5,9},{6,10},{7,11},{8,12},{9,13},{1... | collective-permute-start | bytes 589832 | tf_op jit(solution)/shard_map/ppermute | solution.py:223
  80.8 8.5 %collective-permute-start.9 = (f32[192,256]{1,0:T(8,128)S(1)}, f32[192,256]{1,0:T(8,128)S(1)}, u32[]{:S(2)}, u32[]{:S(2)}) collective-permute-start(f32[192,256]{1,0:T(8,128)S(1)} %get-tuple-element.56), channel_id=1, source_target_pairs={{0,8},{1,9},{2,10},{3,11},{4,12},{5,13},{6,14},{7,15},{8,0},{9,1},... | collective-permute-start | bytes 589832 | tf_op jit(solution)/shard_map/ppermute | solution.py:223
  83.6 5.8 %collective-permute-start.10 = (f32[192,256]{1,0:T(8,128)S(1)}, f32[192,256]{1,0:T(8,128)S(1)}, u32[]{:S(2)}, u32[]{:S(2)}) collective-permute-start(f32[192,256]{1,0:T(8,128)S(1)} %get-tuple-element.57), channel_id=1, source_target_pairs={{0,12},{1,13},{2,14},{3,15},{4,0},{5,1},{6,2},{7,3},{8,4},{9,5},{1... | collective-permute-start | bytes 589832 | tf_op jit(solution)/shard_map/ppermute | solution.py:223
  89.4 9.1 %collective-permute-start.11 = (f32[192,256]{1,0:T(8,128)S(1)}, f32[192,256]{1,0:T(8,128)S(1)}, u32[]{:S(2)}, u32[]{:S(2)}) collective-permute-start(f32[192,256]{1,0:T(8,128)S(1)} %shard_map.67.refs_0_), channel_id=1, source_target_pairs={{0,1},{1,2},{2,3},{3,0},{4,5},{5,6},{6,7},{7,4},{8,9},{9,10},{10,1... | collective-permute-start | bytes 589832 | tf_op jit(solution)/shard_map/ppermute | solution.py:223
  90.2 8.2 %collective-permute-start.12 = (f32[192,256]{1,0:T(8,128)S(1)}, f32[192,256]{1,0:T(8,128)S(1)}, u32[]{:S(2)}, u32[]{:S(2)}) collective-permute-start(f32[192,256]{1,0:T(8,128)S(1)} %shard_map.67.refs_0_), channel_id=1, source_target_pairs={{0,2},{1,3},{2,0},{3,1},{4,6},{5,7},{6,4},{7,5},{8,10},{9,11},{10,... | collective-permute-start | bytes 589832 | tf_op jit(solution)/shard_map/ppermute | solution.py:223
  91.7 7.6 %collective-permute-start.13 = (f32[192,256]{1,0:T(8,128)S(1)}, f32[192,256]{1,0:T(8,128)S(1)}, u32[]{:S(2)}, u32[]{:S(2)}) collective-permute-start(f32[192,256]{1,0:T(8,128)S(1)} %shard_map.67.refs_0_), channel_id=1, source_target_pairs={{0,3},{1,0},{2,1},{3,2},{4,7},{5,4},{6,5},{7,6},{8,11},{9,8},{10,9... | collective-permute-start | bytes 589832 | tf_op jit(solution)/shard_map/ppermute | solution.py:223
  99.5 7.7 %collective-permute-start.14 = (bf16[192,256]{1,0:T(8,128)(2,1)S(1)}, bf16[192,256]{1,0:T(8,128)(2,1)S(1)}, u32[]{:S(2)}, u32[]{:S(2)}) collective-permute-start(bf16[192,256]{1,0:T(8,128)(2,1)S(1)} %shard_map.68.refs_0_), channel_id=1, source_target_pairs={{0,4},{1,5},{2,6},{3,7},{4,8},{5,9},{6,10},{7,11},{8,12},{9,13},{1... | collective-permute-start | bytes 294920 | tf_op jit(solution)/shard_map/ppermute | solution.py:223
  101.5 6.1 %collective-permute-start.15 = (bf16[192,256]{1,0:T(8,128)(2,1)S(1)}, bf16[192,256]{1,0:T(8,128)(2,1)S(1)}, u32[]{:S(2)}, u32[]{:S(2)}) collective-permute-start(bf16[192,256]{1,0:T(8,128)(2,1)S(1)} %shard_map.68.refs_0_), channel_id=1, source_target_pairs={{0,8},{1,9},{2,10},{3,11},{4,12},{5,13},{6,14},{7,15},{8,0},{9,1},... | collective-permute-start | bytes 294920 | tf_op jit(solution)/shard_map/ppermute | solution.py:223
  103.6 4.6 %collective-permute-start.16 = (bf16[192,256]{1,0:T(8,128)(2,1)S(1)}, bf16[192,256]{1,0:T(8,128)(2,1)S(1)}, u32[]{:S(2)}, u32[]{:S(2)}) collective-permute-start(bf16[192,256]{1,0:T(8,128)(2,1)S(1)} %shard_map.68.refs_0_), channel_id=1, source_target_pairs={{0,12},{1,13},{2,14},{3,15},{4,0},{5,1},{6,2},{7,3},{8,4},{9,5},{1... | collective-permute-start | bytes 294920 | tf_op jit(solution)/shard_map/ppermute | solution.py:223
  105.2 19.8 %copy-start.4 = (bf16[768,768]{1,0:T(8,128)(2,1)S(1)}, bf16[768,768]{1,0:T(8,128)(2,1)}, u32[]{:S(2)}) copy-start(bf16[768,768]{1,0:T(8,128)(2,1)} %refs_13_.1) | copy-start | bytes 3538948
  107.2 17.8 %copy-start.2 = (bf16[768,768]{1,0:T(8,128)(2,1)S(1)}, bf16[768,768]{1,0:T(8,128)(2,1)}, u32[]{:S(2)}) copy-start(bf16[768,768]{1,0:T(8,128)(2,1)} %refs_11_.1) | copy-start | bytes 3538948
  107.2 17.8 %copy-start.3 = (bf16[768,768]{1,0:T(8,128)(2,1)S(1)}, bf16[768,768]{1,0:T(8,128)(2,1)}, u32[]{:S(2)}) copy-start(bf16[768,768]{1,0:T(8,128)(2,1)} %refs_12_.1) | copy-start | bytes 3538948
  108.8 8.0 %collective-permute-start.17 = (bf16[2,384,256]{2,1,0:T(8,128)(2,1)S(1)}, bf16[2,384,256]{2,1,0:T(8,128)(2,1)S(1)}, u32[]{:S(2)}, u32[]{:S(2)}) collective-permute-start(bf16[2,384,256]{2,1,0:T(8,128)(2,1)S(1)} %shard_map.70.refs_0_), channel_id=1, source_target_pairs={{0,32},{1,33},{2,34},{3,35},{4,36},{5,37},{6,38},{7,39},{8,40},{9,... | collective-permute-start | bytes 1179656 | tf_op jit(solution)/shard_map/ppermute | solution.py:223
  110.1 9.4 %collective-permute-start.18 = (bf16[2,384,256]{2,1,0:T(8,128)(2,1)S(1)}, bf16[2,384,256]{2,1,0:T(8,128)(2,1)S(1)}, u32[]{:S(2)}, u32[]{:S(2)}) collective-permute-start(bf16[2,384,256]{2,1,0:T(8,128)(2,1)S(1)} %shard_map.70.refs_0_), channel_id=1, source_target_pairs={{0,64},{1,65},{2,66},{3,67},{4,68},{5,69},{6,70},{7,71},{8,72},{9,... | collective-permute-start | bytes 1179656 | tf_op jit(solution)/shard_map/ppermute | solution.py:223
  111.3 12.0 %collective-permute-start.19 = (bf16[2,384,256]{2,1,0:T(8,128)(2,1)S(1)}, bf16[2,384,256]{2,1,0:T(8,128)(2,1)S(1)}, u32[]{:S(2)}, u32[]{:S(2)}) collective-permute-start(bf16[2,384,256]{2,1,0:T(8,128)(2,1)S(1)} %shard_map.70.refs_0_), channel_id=1, source_target_pairs={{0,96},{1,97},{2,98},{3,99},{4,100},{5,101},{6,102},{7,103},{8,104... | collective-permute-start | bytes 1179656 | tf_op jit(solution)/shard_map/ppermute | solution.py:223
  113.2 10.0 %collective-permute-start.20 = (bf16[2,384,256]{2,1,0:T(8,128)(2,1)S(1)}, bf16[2,384,256]{2,1,0:T(8,128)(2,1)S(1)}, u32[]{:S(2)}, u32[]{:S(2)}) collective-permute-start(bf16[2,384,256]{2,1,0:T(8,128)(2,1)S(1)} %shard_map.70.refs_0_), channel_id=1, source_target_pairs={{0,16},{16,0},{1,17},{17,1},{2,18},{18,2},{3,19},{19,3},{4,20},{20... | collective-permute-start | bytes 1179656 | tf_op jit(solution)/shard_map/ppermute | solution.py:186
  116.9 6.4 %collective-permute-start.21 = (bf16[2,384,256]{2,1,0:T(8,128)(2,1)S(1)}, bf16[2,384,256]{2,1,0:T(8,128)(2,1)S(1)}, u32[]{:S(2)}, u32[]{:S(2)}) collective-permute-start(bf16[2,384,256]{2,1,0:T(8,128)(2,1)S(1)} %collective-permute-done.17.refs_1_), channel_id=1, source_target_pairs={{0,16},{16,0},{1,17},{17,1},{2,18},{18,2},{3,19},{19,3},{4,20},{20... | collective-permute-start | bytes 1179656 | tf_op jit(solution)/shard_map/ppermute | solution.py:186
  119.5 3.8 %collective-permute-start.22 = (bf16[2,384,256]{2,1,0:T(8,128)(2,1)S(1)}, bf16[2,384,256]{2,1,0:T(8,128)(2,1)S(1)}, u32[]{:S(2)}, u32[]{:S(2)}) collective-permute-start(bf16[2,384,256]{2,1,0:T(8,128)(2,1)S(1)} %collective-permute-done.18.refs_2_), channel_id=1, source_target_pairs={{0,16},{16,0},{1,17},{17,1},{2,18},{18,2},{3,19},{19,3},{4,20},{20... | collective-permute-start | bytes 1179656 | tf_op jit(solution)/shard_map/ppermute | solution.py:186
  123.3 1.7 %collective-permute-start.23 = (bf16[2,384,256]{2,1,0:T(8,128)(2,1)S(1)}, bf16[2,384,256]{2,1,0:T(8,128)(2,1)S(1)}, u32[]{:S(2)}, u32[]{:S(2)}) collective-permute-start(bf16[2,384,256]{2,1,0:T(8,128)(2,1)S(1)} %collective-permute-done.19.refs_3_), channel_id=1, source_target_pairs={{0,16},{16,0},{1,17},{17,1},{2,18},{18,2},{3,19},{19,3},{4,20},{20... | collective-permute-start | bytes 1179656 | tf_op jit(solution)/shard_map/ppermute | solution.py:186

commit v4 on v3

--- a/solution.py
+++ b/solution.py
@@ -136,7 +136,7 @@
         stage_ref[:, pl.ds(pl.multiple_of(first, rows), rows)] = part_ref[...]
 
 
-def head_grads(base, q_ref, k_ref, g_ref, outs, stage_ref):
+def head_grads(base, first, q_ref, k_ref, g_ref, outs, stage_ref):
     res = stage_ref.shape[-1]
     for h in range(q_ref.shape[0] // 2):
         prob, logit_grad = (stage_ref[term, pl.ds(h * res, res)] for term in range(2))
@@ -145,18 +145,24 @@
             outs,
             (dot(k_ref[hh], logit_grad, NT), dot(q_ref[hh], logit_grad), dot(g_ref[hh], prob)),
         ):
-            o_ref[:, hh] = value.astype(BF16).reshape(o_ref.shape[0], -1, res)
+            o_ref[:, first + h] = value.astype(BF16).reshape(o_ref.shape[0], -1, res)
+
+
+def own_grads_kernel(place_ref, *refs):
+    own, held, outs, stage_ref = refs[:4], refs[4:7], refs[7:10], refs[10]
+    place_rows(place_ref[1], own, stage_ref)
+    head_grads(place_ref[0] * outs[0].shape[1], 0, *held, outs, stage_ref)
 
 
 def output_kernel(place_ref, *refs):
-    own, other, held, weights, out_ref = refs[:4], refs[4:8], refs[8:11], refs[11:14], refs[14]
-    outs, own_stage, other_stage = refs[15:18], refs[18], refs[19]
+    other, own_outs, held, weights, out_ref = refs[:4], refs[4:7], refs[7:10], refs[10:13], refs[13]
+    outs, stage_ref = refs[14:17], refs[17]
     core = place_ref[0]
     half = held[0].shape[0] // 2
-    place_rows(place_ref[1], own, own_stage)
-    head_grads(core * half, *held, outs, own_stage)
-    place_rows(place_ref[3], other, other_stage)
-    head_grads((1 - core) * half, *held, outs, other_stage)
+    for own_ref, o_ref in zip(own_outs, outs):
+        o_ref[:, pl.ds(core * half, half)] = own_ref[...]
+    place_rows(place_ref[3], other, stage_ref)
+    head_grads((1 - core) * half, (1 - core) * half, *held, outs, stage_ref)
     res = held[0].shape[-1]
     for s in range(out_ref.shape[1]):
         total = None
@@ -282,13 +288,17 @@
     )
     own = spread([result] * 4, 0)
     other = [shift(a, "core", 1) for a in own]
-    grown = pltpu.VMEM((seqs, HEADS, head, res), BF16)
+    stage = pltpu.VMEM((2, half * res, res), BF16)
+    own_grown = call(
+        own_grads_kernel, [shape((seqs, half, head, res))] * 3, place, *own, q, k, g,
+        specs=[SMEM] + [VMEM] * 7, scratch=[stage],
+    )
     out = call(
         output_kernel,
         shape((blocks, seqs, block, width)),
-        place, *own, *other, q, k, g, w_query, w_key, w_value,
-        specs=[SMEM] + [VMEM] * 14,
-        scratch=[grown] * 3 + [pltpu.VMEM((2, half * res, res), BF16)] * 2,
+        place, *other, *own_grown, q, k, g, w_query, w_key, w_value,
+        specs=[SMEM] + [VMEM] * 13,
+        scratch=[pltpu.VMEM((seqs, HEADS, head, res), BF16)] * 3 + [stage],
         mib=24,
     )
     return exchange(out).reshape(seq_count, block, width)

time: 162 us -> 162 us (level)
    pallas_call x12 -> x13, Pallas kernels: 22.9 us -> 23.8 us  [call(): pl.pallas_call(kernel, out_shape=outs, in_specs=list(specs or [VMEM] * le...]
  transfers between devices with their start and end apart: 25 -> 25, of which waited for: 18 -> 18; matrix products, arithmetic and copies ran while one was open for 0% -> 0% of each run, Pallas kernels for 7% -> 8%
where the time goes in v4:
time: 162 us
  blocking collectives  60.5 us (37%)
  waiting for transfers between devices  39.1 us (24%)
  starting transfers between devices  36.4 us (22%)
  Pallas kernels  23.8 us (15%)
    all_to_all x2, blocking collectives, exchange(): lax.all_to_all(a, ('z', 'y'), split_axis=0, concat_axis=0, tiled=True)  60.5 us
    ppermute x18, waiting for transfers between devices, spread(): sent = {d: lax.ppermute(parts[d], AXES, turn(stage, d)) for d in (1, 3, 2)}  33.6 us
    ppermute x18, starting transfers between devices, spread(): sent = {d: lax.ppermute(parts[d], AXES, turn(stage, d)) for d in (1, 3, 2)}  30.1 us
    pallas_call x13, Pallas kernels, call(): pl.pallas_call(kernel, out_shape=outs, in_specs=list(specs or [VMEM] * le...  23.8 us
    ppermute x6, waiting for transfers between devices, shift(): return lax.ppermute(a, axis, [(i, (i + step) % n) for i in range(n)])  5.52 us
    all_to_all x1, starting transfers between devices, exchange(): lax.all_to_all(a, ('z', 'y'), split_axis=0, concat_axis=0, tiled=True)  3.71 us
  transfers between devices with their start and end apart: 25, of which 18 were waited for; matrix products, arithmetic and copies ran while one was open for 0% of the time, Pallas kernels for 8%

profile of v4, /device:TPU:2, one launch (start us, length us, event | category | flops | bytes accessed | tf_op | source)
XLA Modules:
  0.0 161.5 jit_solution(5193968753022779977)
XLA Ops:
  0.0 30.9 %all_to_all.15 = bf16[16,4,16,768]{3,2,1,0:T(8,128)(2,1)} all-to-all(bf16[16,4,16,768]{3,2,1,0:T(8,128)(2,1)} %bitcast.16), channel_id=1, replica_groups=mesh['x'=4,'core'=2,'z'=4,'y'=4] {'z','y'}, dimensions={0} | all-to-all | bytes 3145728 | tf_op jit(solution)/shard_map/all_to_all | solution.py:226
  30.9 3.7 %all-to-all-start.1 = ((bf16[16,4,16,768]{3,2,1,0:T(8,128)(2,1)}), bf16[16,4,16,768]{3,2,1,0:T(8,128)(2,1)S(1)}, u32[]{:S(2)}, u32[]{:S(2)}) async-start(bf16[16,4,16,768]{3,2,1,0:T(8,128)(2,1)} %bitcast.7), calls=%async_computation.1 | async-start | bytes 3145728 | tf_op jit(solution)/shard_map/all_to_all | solution.py:226
  34.7 0.1 pad_add_fusion.place_ref
  34.7 25.3 %conditional.1 = (bf16[12,256,256]{2,1,0:T(8,128)(2,1)}, bf16[12,256,256]{2,1,0:T(8,128)(2,1)}, bf16[12,256,256]{2,1,0:T(8,128)(2,1)}, f32[384,256]{1,0:T(8,128)S(1)}) conditional(s32[]{:T(128)} %convert_element_type.3, () %tuple.13, (s32[4]{0:T(128)S(1)}, bf16[16,4,16,768]{3,2,1,0:T(8,128)(2,1)}, bf16[768,768]{1,0:T(8,128)(2,1)}, ...), branch_computations={%region_0.1_spmd, %region_1.2_spmd} | conditional | bytes 22020344 | solution.py:267
  34.7 6.3 %branch_1_fun.4 = (bf16[12,256,256]{2,1,0:T(8,128)(2,1)}, bf16[12,256,256]{2,1,0:T(8,128)(2,1)}, f32[6,256,256]{2,1,0:T(8,128)S(1)}, f32[6,256,256]{2,1,0:T(8,128)S(1)}) custom-call(s32[4]{0:T(128)S(1)} %get-tuple-element.15.refs_0_.place_ref, bf16[16,4,16,768]{3,2,1,0:T(8,128)(2,1)} %get-tuple-element.16.refs_1_.x_ref, ...), custom_call_target="tpu_custom_call" | custom-call | tf_op jit(solution)/shard_map/cond/branch_1_fun/pallas_call | solution.py:176
  41.1 0.1 collective-permute-start
  41.2 3.4 %collective-permute-done = f32[6,256,256]{2,1,0:T(8,128)S(1)} collective-permute-done((f32[6,256,256]{2,1,0:T(8,128)S(1)}, f32[6,256,256]{2,1,0:T(8,128)S(1)}, u32[]{:S(2)}, u32[]{:S(2)}) %collective-permute-start) | collective-permute-done | bytes 1572896 | tf_op jit(solution)/shard_map/cond/branch_1_fun/ppermute | solution.py:192
  44.6 0.7 branch_1_fun.6
  45.3 1.6 collective-permute-start.1
  46.9 1.1 collective-permute-start.2
  48.0 2.2 %collective-permute-start.3 = (f32[384,256]{1,0:T(8,128)S(1)}, f32[384,256]{1,0:T(8,128)S(1)}, u32[]{:S(2)}, u32[]{:S(2)}) collective-permute-start(f32[384,256]{1,0:T(8,128)S(1)} %get-tuple-element.27), channel_id=1, source_target_pairs={{0,96},{1,97},{2,98},{3,99},{4,100},{5,101},{6,102},{7,103},{8,104... | collective-permute-start | bytes 1179656 | tf_op jit(solution)/shard_map/cond/branch_1_fun/ppermute | solution.py:229
  50.1 2.6 %branch_1_fun.5 = bf16[12,256,256]{2,1,0:T(8,128)(2,1)} custom-call(bf16[16,4,16,768]{3,2,1,0:T(8,128)(2,1)S(1)} %copy-done.1, bf16[768,768]{1,0:T(8,128)(2,1)S(1)} %copy-done.5), custom_call_target="tpu_custom_call" | custom-call | tf_op jit(solution)/shard_map/cond/branch_1_fun/pallas_call | solution.py:176
  52.7 0.4 collective-permute-done.1.refs_1_
  53.1 3.1 %collective-permute-done.2.refs_2_ = f32[384,256]{1,0:T(8,128)S(1)} collective-permute-done((f32[384,256]{1,0:T(8,128)S(1)}, f32[384,256]{1,0:T(8,128)S(1)}, u32[]{:S(2)}, u32[]{:S(2)}) %collective-permute-start.2) | collective-permute-done | bytes 393248 | tf_op jit(solution)/shard_map/cond/branch_1_fun/ppermute | solution.py:229
  56.2 3.7 %collective-permute-done.3.refs_3_ = f32[384,256]{1,0:T(8,128)S(1)} collective-permute-done((f32[384,256]{1,0:T(8,128)S(1)}, f32[384,256]{1,0:T(8,128)S(1)}, u32[]{:S(2)}, u32[]{:S(2)}) %collective-permute-start.3) | collective-permute-done | bytes 393248 | tf_op jit(solution)/shard_map/cond/branch_1_fun/ppermute | solution.py:229
  59.9 0.1 branch_1_fun.7
  60.0 0.0 all-to-all-done.1.c_ref
  60.0 3.0 %shard_map.64 = (bf16[12,256,256]{2,1,0:T(8,128)(2,1)S(1)}, f32[6,256,256]{2,1,0:T(8,128)S(1)}, bf16[6,256,256]{2,1,0:T(8,128)(2,1)S(1)}) custom-call(s32[4]{0:T(128)S(1)} %pad_add_fusion.place_ref, bf16[16,4,16,768]{3,2,1,0:T(8,128)(2,1)S(1)} %all-to-all-done.1.c_ref, bf16[768,768]{1,0:T(8,128)(2,1)S(1)} %copy-done, ...), custom_call_target="tpu_custom_call" | custom-call | tf_op jit(solution)/shard_map/pallas_call | solution.py:176
  63.0 2.5 %collective-permute-start.4 = (bf16[6,256,256]{2,1,0:T(8,128)(2,1)S(1)}, bf16[6,256,256]{2,1,0:T(8,128)(2,1)S(1)}, u32[]{:S(2)}, u32[]{:S(2)}) collective-permute-start(bf16[6,256,256]{2,1,0:T(8,128)(2,1)S(1)} %get-tuple-element.52), channel_id=1, source_target_pairs={{0,16},{16,0},{1,17},{17,1},{2,18},{18,2},{3,19},{19,3},{4,20},{20... | collective-permute-start | bytes 2359304 | tf_op jit(solution)/shard_map/ppermute | solution.py:192
  65.6 1.9 %collective-permute-done.4 = bf16[6,256,256]{2,1,0:T(8,128)(2,1)S(1)} collective-permute-done((bf16[6,256,256]{2,1,0:T(8,128)(2,1)S(1)}, bf16[6,256,256]{2,1,0:T(8,128)(2,1)S(1)}, u32[]{:S(2)}, u32[]{:S(2)}) %collective-permute-start.4) | collective-permute-done | bytes 786464 | tf_op jit(solution)/shard_map/ppermute | solution.py:192
  67.5 0.7 shard_map.65
  68.2 1.6 collective-permute-start.5
  69.7 1.1 collective-permute-start.6
  70.8 2.2 %collective-permute-start.7 = (bf16[384,256]{1,0:T(8,128)(2,1)S(1)}, bf16[384,256]{1,0:T(8,128)(2,1)S(1)}, u32[]{:S(2)}, u32[]{:S(2)}) collective-permute-start(bf16[384,256]{1,0:T(8,128)(2,1)S(1)} %get-tuple-element.56), channel_id=1, source_target_pairs={{0,96},{1,97},{2,98},{3,99},{4,100},{5,101},{6,102},{7,103},{8,104... | collective-permute-start | bytes 589832 | tf_op jit(solution)/shard_map/ppermute | solution.py:229
  73.0 0.9 collective-permute-done.5.refs_1_
  73.9 3.1 %collective-permute-done.6.refs_2_ = bf16[384,256]{1,0:T(8,128)(2,1)S(1)} collective-permute-done((bf16[384,256]{1,0:T(8,128)(2,1)S(1)}, bf16[384,256]{1,0:T(8,128)(2,1)S(1)}, u32[]{:S(2)}, u32[]{:S(2)}) %collective-permute-start.6) | collective-permute-done | bytes 196640 | tf_op jit(solution)/shard_map/ppermute | solution.py:229
  77.0 1.6 %collective-permute-done.7.refs_3_ = bf16[384,256]{1,0:T(8,128)(2,1)S(1)} collective-permute-done((bf16[384,256]{1,0:T(8,128)(2,1)S(1)}, bf16[384,256]{1,0:T(8,128)(2,1)S(1)}, u32[]{:S(2)}, u32[]{:S(2)}) %collective-permute-start.7) | collective-permute-done | bytes 196640 | tf_op jit(solution)/shard_map/ppermute | solution.py:229
  78.6 0.6 shard_map.66
  79.3 1.5 collective-permute-start.8
  80.8 2.7 %collective-permute-start.9 = (f32[192,256]{1,0:T(8,128)S(1)}, f32[192,256]{1,0:T(8,128)S(1)}, u32[]{:S(2)}, u32[]{:S(2)}) collective-permute-start(f32[192,256]{1,0:T(8,128)S(1)} %get-tuple-element.59), channel_id=1, source_target_pairs={{0,8},{1,9},{2,10},{3,11},{4,12},{5,13},{6,14},{7,15},{8,0},{9,1},... | collective-permute-start | bytes 589832 | tf_op jit(solution)/shard_map/ppermute | solution.py:229
  83.6 1.4 collective-permute-start.10
  85.0 1.2 collective-permute-done.8.refs_1_
  86.2 3.1 %collective-permute-done.9.refs_2_ = f32[192,256]{1,0:T(8,128)S(1)} collective-permute-done((f32[192,256]{1,0:T(8,128)S(1)}, f32[192,256]{1,0:T(8,128)S(1)}, u32[]{:S(2)}, u32[]{:S(2)}) %collective-permute-start.9) | collective-permute-done | bytes 196640 | tf_op jit(solution)/shard_map/ppermute | solution.py:229
  89.4 0.8 collective-permute-start.11
  90.2 1.5 collective-permute-start.12
  91.7 2.4 %collective-permute-start.13 = (f32[192,256]{1,0:T(8,128)S(1)}, f32[192,256]{1,0:T(8,128)S(1)}, u32[]{:S(2)}, u32[]{:S(2)}) collective-permute-start(f32[192,256]{1,0:T(8,128)S(1)} %shard_map.67.refs_0_), channel_id=1, source_target_pairs={{0,3},{1,0},{2,1},{3,2},{4,7},{5,4},{6,5},{7,6},{8,11},{9,8},{10,9... | collective-permute-start | bytes 589832 | tf_op jit(solution)/shard_map/ppermute | solution.py:229
  94.0 4.4 %collective-permute-done.11.refs_1_ = f32[192,256]{1,0:T(8,128)S(1)} collective-permute-done((f32[192,256]{1,0:T(8,128)S(1)}, f32[192,256]{1,0:T(8,128)S(1)}, u32[]{:S(2)}, u32[]{:S(2)}) %collective-permute-start.11) | collective-permute-done | bytes 196640 | tf_op jit(solution)/shard_map/ppermute | solution.py:229
  98.4 0.0 collective-permute-done.12.refs_2_
  98.4 0.9 collective-permute-done.13.refs_3_
  99.3 0.3 shard_map.68.refs_0_
  99.5 2.0 %collective-permute-start.14 = (bf16[192,256]{1,0:T(8,128)(2,1)S(1)}, bf16[192,256]{1,0:T(8,128)(2,1)S(1)}, u32[]{:S(2)}, u32[]{:S(2)}) collective-permute-start(bf16[192,256]{1,0:T(8,128)(2,1)S(1)} %shard_map.68.refs_0_), channel_id=1, source_target_pairs={{0,4},{1,5},{2,6},{3,7},{4,8},{5,9},{6,10},{7,11},{8,12},{9,13},{1... | collective-permute-start | bytes 294920 | tf_op jit(solution)/shard_map/ppermute | solution.py:229
  101.5 2.1 %collective-permute-start.15 = (bf16[192,256]{1,0:T(8,128)(2,1)S(1)}, bf16[192,256]{1,0:T(8,128)(2,1)S(1)}, u32[]{:S(2)}, u32[]{:S(2)}) collective-permute-start(bf16[192,256]{1,0:T(8,128)(2,1)S(1)} %shard_map.68.refs_0_), channel_id=1, source_target_pairs={{0,8},{1,9},{2,10},{3,11},{4,12},{5,13},{6,14},{7,15},{8,0},{9,1},... | collective-permute-start | bytes 294920 | tf_op jit(solution)/shard_map/ppermute | solution.py:229
  103.6 1.5 collective-permute-start.16
  105.2 1.9 %shard_map.69 = (bf16[12,256,256]{2,1,0:T(8,128)(2,1)S(1)}, bf16[12,256,256]{2,1,0:T(8,128)(2,1)S(1)}, bf16[12,256,256]{2,1,0:T(8,128)(2,1)S(1)}) custom-call(bf16[12,256,256]{2,1,0:T(8,128)(2,1)} %get-tuple-element.61.refs_0_, bf16[12,256,256]{2,1,0:T(8,128)(2,1)} %get-tuple-element.62.refs_1_, bf16[12,256,256]{2,1,0:T(8,128)(2,1)S(1)} %get-tuple-element.63.refs_2_), custom_call_target="tpu_custom_call" | custom-call | tf_op jit(solution)/shard_map/pallas_call | solution.py:176
  107.1 0.0 collective-permute-done.14.refs_1_
  107.1 0.5 collective-permute-done.15.refs_2_
  107.6 0.6 collective-permute-done.16.refs_3_
  108.3 0.6 shard_map.70.refs_0_
  108.8 1.2 collective-permute-start.18
  110.1 1.2 collective-permute-start.20
  111.3 1.9 %collective-permute-start.22 = (bf16[2,384,256]{2,1,0:T(8,128)(2,1)S(1)}, bf16[2,384,256]{2,1,0:T(8,128)(2,1)S(1)}, u32[]{:S(2)}, u32[]{:S(2)}) collective-permute-start(bf16[2,384,256]{2,1,0:T(8,128)(2,1)S(1)} %shard_map.70.refs_0_), channel_id=1, source_target_pairs={{0,96},{1,97},{2,98},{3,99},{4,100},{5,101},{6,102},{7,103},{8,104... | collective-permute-start | bytes 1179656 | tf_op jit(solution)/shard_map/ppermute | solution.py:229
  113.2 0.0 collective-permute-start.17
  113.2 3.6 %collective-permute-done.18.refs_1_ = bf16[2,384,256]{2,1,0:T(8,128)(2,1)S(1)} collective-permute-done((bf16[2,384,256]{2,1,0:T(8,128)(2,1)S(1)}, bf16[2,384,256]{2,1,0:T(8,128)(2,1)S(1)}, u32[]{:S(2)}, u32[]{:S(2)}) %collective-permute-start.18) | collective-permute-done | bytes 393248 | tf_op jit(solution)/shard_map/ppermute | solution.py:229
  116.9 0.0 collective-permute-start.19
  116.9 2.6 %collective-permute-done.20.refs_2_ = bf16[2,384,256]{2,1,0:T(8,128)(2,1)S(1)} collective-permute-done((bf16[2,384,256]{2,1,0:T(8,128)(2,1)S(1)}, bf16[2,384,256]{2,1,0:T(8,128)(2,1)S(1)}, u32[]{:S(2)}, u32[]{:S(2)}) %collective-permute-start.20) | collective-permute-done | bytes 393248 | tf_op jit(solution)/shard_map/ppermute | solution.py:229
  119.5 3.8 %collective-permute-done.22.refs_3_ = bf16[2,384,256]{2,1,0:T(8,128)(2,1)S(1)} collective-permute-done((bf16[2,384,256]{2,1,0:T(8,128)(2,1)S(1)}, bf16[2,384,256]{2,1,0:T(8,128)(2,1)S(1)}, u32[]{:S(2)}, u32[]{:S(2)}) %collective-permute-start.22) | collective-permute-done | bytes 393248 | tf_op jit(solution)/shard_map/ppermute | solution.py:229
  123.3 0.0 collective-permute-start.23
  123.3 1.5 shard_map.71
  124.8 0.0 collective-permute-done.17.refs_0_
  124.8 0.2 collective-permute-done.23.refs_3_
  125.0 0.3 copy-done.4
  125.3 5.5 %shard_map.72 = bf16[16,4,16,768]{3,2,1,0:T(8,128)(2,1)S(1)} custom-call(s32[4]{0:T(128)S(1)} %pad_add_fusion.place_ref, bf16[2,384,256]{2,1,0:T(8,128)(2,1)S(1)} %collective-permute-done.17.refs_0_, bf16[2,384,256]{2,1,0:T(8,128)(2,1)S(1)} %collective-permute-done.19.refs_1_, bf16[2,384,256]{2,1,0:T(8,128)(2,1)S(1)} %collective-permute-done.21.refs_2_, ...), custom_call_target="tpu_custom_call" | custom-call | tf_op jit(solution)/shard_map/pallas_call | solution.py:176
  130.8 29.6 %all_to_all.16 = bf16[16,4,16,768]{3,2,1,0:T(8,128)(2,1)S(1)} all-to-all(bf16[16,4,16,768]{3,2,1,0:T(8,128)(2,1)S(1)} %shard_map.72), channel_id=1, replica_groups=mesh['x'=4,'core'=2,'z'=4,'y'=4] {'z','y'}, dimensions={0} | all-to-all | bytes 3145728 | tf_op jit(solution)/shard_map/all_to_all | solution.py:226
  160.4 1.1 copy.16
  (16 shorter events, 0.1 us)
Async XLA Ops:
  30.9 29.1 %all-to-all-start.1 = ((bf16[16,4,16,768]{3,2,1,0:T(8,128)(2,1)}), bf16[16,4,16,768]{3,2,1,0:T(8,128)(2,1)S(1)}, u32[]{:S(2)}, u32[]{:S(2)}) async-start(bf16[16,4,16,768]{3,2,1,0:T(8,128)(2,1)} %bitcast.7), calls=%async_computation.1 | async-start | bytes 3145728 | tf_op jit(solution)/shard_map/all_to_all | solution.py:226
  34.7 25.3 %copy-start = (bf16[768,768]{1,0:T(8,128)(2,1)S(1)}, bf16[768,768]{1,0:T(8,128)(2,1)}, u32[]{:S(2)}) copy-start(bf16[768,768]{1,0:T(8,128)(2,1)} %w_in.1) | copy-start | bytes 3538948
  41.1 3.5 %collective-permute-start = (f32[6,256,256]{2,1,0:T(8,128)S(1)}, f32[6,256,256]{2,1,0:T(8,128)S(1)}, u32[]{:S(2)}, u32[]{:S(2)}) collective-permute-start(f32[6,256,256]{2,1,0:T(8,128)S(1)} %get-tuple-element.23), channel_id=1, source_target_pairs={{0,16},{16,0},{1,17},{17,1},{2,18},{18,2},{3,19},{19,3},{4,20},{20... | collective-permute-start | bytes 4718600 | tf_op jit(solution)/shard_map/cond/branch_1_fun/ppermute | solution.py:192
  44.6 5.5 %copy-start.1 = (bf16[16,4,16,768]{3,2,1,0:T(8,128)(2,1)S(1)}, bf16[16,4,16,768]{3,2,1,0:T(8,128)(2,1)}, u32[]{:S(2)}) copy-start(bf16[16,4,16,768]{3,2,1,0:T(8,128)(2,1)} %get-tuple-element.16.refs_1_.x_ref) | copy-start | bytes 4718596 | tf_op jit(solution)/shard_map/cond
  44.6 5.5 %copy-start.5 = (bf16[768,768]{1,0:T(8,128)(2,1)S(1)}, bf16[768,768]{1,0:T(8,128)(2,1)}, u32[]{:S(2)}) copy-start(bf16[768,768]{1,0:T(8,128)(2,1)} %get-tuple-element.21.w_ref) | copy-start | bytes 3538948 | tf_op jit(solution)/shard_map/cond
  45.3 7.8 %collective-permute-start.1 = (f32[384,256]{1,0:T(8,128)S(1)}, f32[384,256]{1,0:T(8,128)S(1)}, u32[]{:S(2)}, u32[]{:S(2)}) collective-permute-start(f32[384,256]{1,0:T(8,128)S(1)} %get-tuple-element.25), channel_id=1, source_target_pairs={{0,32},{1,33},{2,34},{3,35},{4,36},{5,37},{6,38},{7,39},{8,40},{9,... | collective-permute-start | bytes 1179656 | tf_op jit(solution)/shard_map/cond/branch_1_fun/ppermute | solution.py:229
  46.9 9.4 %collective-permute-start.2 = (f32[384,256]{1,0:T(8,128)S(1)}, f32[384,256]{1,0:T(8,128)S(1)}, u32[]{:S(2)}, u32[]{:S(2)}) collective-permute-start(f32[384,256]{1,0:T(8,128)S(1)} %get-tuple-element.26), channel_id=1, source_target_pairs={{0,64},{1,65},{2,66},{3,67},{4,68},{5,69},{6,70},{7,71},{8,72},{9,... | collective-permute-start | bytes 1179656 | tf_op jit(solution)/shard_map/cond/branch_1_fun/ppermute | solution.py:229
  48.0 12.0 %collective-permute-start.3 = (f32[384,256]{1,0:T(8,128)S(1)}, f32[384,256]{1,0:T(8,128)S(1)}, u32[]{:S(2)}, u32[]{:S(2)}) collective-permute-start(f32[384,256]{1,0:T(8,128)S(1)} %get-tuple-element.27), channel_id=1, source_target_pairs={{0,96},{1,97},{2,98},{3,99},{4,100},{5,101},{6,102},{7,103},{8,104... | collective-permute-start | bytes 1179656 | tf_op jit(solution)/shard_map/cond/branch_1_fun/ppermute | solution.py:229
  63.0 4.5 %collective-permute-start.4 = (bf16[6,256,256]{2,1,0:T(8,128)(2,1)S(1)}, bf16[6,256,256]{2,1,0:T(8,128)(2,1)S(1)}, u32[]{:S(2)}, u32[]{:S(2)}) collective-permute-start(bf16[6,256,256]{2,1,0:T(8,128)(2,1)S(1)} %get-tuple-element.52), channel_id=1, source_target_pairs={{0,16},{16,0},{1,17},{17,1},{2,18},{18,2},{3,19},{19,3},{4,20},{20... | collective-permute-start | bytes 2359304 | tf_op jit(solution)/shard_map/ppermute | solution.py:192
  68.2 5.7 %collective-permute-start.5 = (bf16[384,256]{1,0:T(8,128)(2,1)S(1)}, bf16[384,256]{1,0:T(8,128)(2,1)S(1)}, u32[]{:S(2)}, u32[]{:S(2)}) collective-permute-start(bf16[384,256]{1,0:T(8,128)(2,1)S(1)} %get-tuple-element.54), channel_id=1, source_target_pairs={{0,32},{1,33},{2,34},{3,35},{4,36},{5,37},{6,38},{7,39},{8,40},{9,... | collective-permute-start | bytes 589832 | tf_op jit(solution)/shard_map/ppermute | solution.py:229
  69.7 7.3 %collective-permute-start.6 = (bf16[384,256]{1,0:T(8,128)(2,1)S(1)}, bf16[384,256]{1,0:T(8,128)(2,1)S(1)}, u32[]{:S(2)}, u32[]{:S(2)}) collective-permute-start(bf16[384,256]{1,0:T(8,128)(2,1)S(1)} %get-tuple-element.55), channel_id=1, source_target_pairs={{0,64},{1,65},{2,66},{3,67},{4,68},{5,69},{6,70},{7,71},{8,72},{9,... | collective-permute-start | bytes 589832 | tf_op jit(solution)/shard_map/ppermute | solution.py:229
  70.8 7.8 %collective-permute-start.7 = (bf16[384,256]{1,0:T(8,128)(2,1)S(1)}, bf16[384,256]{1,0:T(8,128)(2,1)S(1)}, u32[]{:S(2)}, u32[]{:S(2)}) collective-permute-start(bf16[384,256]{1,0:T(8,128)(2,1)S(1)} %get-tuple-element.56), channel_id=1, source_target_pairs={{0,96},{1,97},{2,98},{3,99},{4,100},{5,101},{6,102},{7,103},{8,104... | collective-permute-start | bytes 589832 | tf_op jit(solution)/shard_map/ppermute | solution.py:229
  79.3 7.0 %collective-permute-start.8 = (f32[192,256]{1,0:T(8,128)S(1)}, f32[192,256]{1,0:T(8,128)S(1)}, u32[]{:S(2)}, u32[]{:S(2)}) collective-permute-start(f32[192,256]{1,0:T(8,128)S(1)} %get-tuple-element.58), channel_id=1, source_target_pairs={{0,4},{1,5},{2,6},{3,7},{4,8},{5,9},{6,10},{7,11},{8,12},{9,13},{1... | collective-permute-start | bytes 589832 | tf_op jit(solution)/shard_map/ppermute | solution.py:229
  80.8 8.5 %collective-permute-start.9 = (f32[192,256]{1,0:T(8,128)S(1)}, f32[192,256]{1,0:T(8,128)S(1)}, u32[]{:S(2)}, u32[]{:S(2)}) collective-permute-start(f32[192,256]{1,0:T(8,128)S(1)} %get-tuple-element.59), channel_id=1, source_target_pairs={{0,8},{1,9},{2,10},{3,11},{4,12},{5,13},{6,14},{7,15},{8,0},{9,1},... | collective-permute-start | bytes 589832 | tf_op jit(solution)/shard_map/ppermute | solution.py:229
  83.6 5.8 %collective-permute-start.10 = (f32[192,256]{1,0:T(8,128)S(1)}, f32[192,256]{1,0:T(8,128)S(1)}, u32[]{:S(2)}, u32[]{:S(2)}) collective-permute-start(f32[192,256]{1,0:T(8,128)S(1)} %get-tuple-element.60), channel_id=1, source_target_pairs={{0,12},{1,13},{2,14},{3,15},{4,0},{5,1},{6,2},{7,3},{8,4},{9,5},{1... | collective-permute-start | bytes 589832 | tf_op jit(solution)/shard_map/ppermute | solution.py:229
  89.4 9.1 %collective-permute-start.11 = (f32[192,256]{1,0:T(8,128)S(1)}, f32[192,256]{1,0:T(8,128)S(1)}, u32[]{:S(2)}, u32[]{:S(2)}) collective-permute-start(f32[192,256]{1,0:T(8,128)S(1)} %shard_map.67.refs_0_), channel_id=1, source_target_pairs={{0,1},{1,2},{2,3},{3,0},{4,5},{5,6},{6,7},{7,4},{8,9},{9,10},{10,1... | collective-permute-start | bytes 589832 | tf_op jit(solution)/shard_map/ppermute | solution.py:229
  90.2 8.2 %collective-permute-start.12 = (f32[192,256]{1,0:T(8,128)S(1)}, f32[192,256]{1,0:T(8,128)S(1)}, u32[]{:S(2)}, u32[]{:S(2)}) collective-permute-start(f32[192,256]{1,0:T(8,128)S(1)} %shard_map.67.refs_0_), channel_id=1, source_target_pairs={{0,2},{1,3},{2,0},{3,1},{4,6},{5,7},{6,4},{7,5},{8,10},{9,11},{10,... | collective-permute-start | bytes 589832 | tf_op jit(solution)/shard_map/ppermute | solution.py:229
  91.7 7.6 %collective-permute-start.13 = (f32[192,256]{1,0:T(8,128)S(1)}, f32[192,256]{1,0:T(8,128)S(1)}, u32[]{:S(2)}, u32[]{:S(2)}) collective-permute-start(f32[192,256]{1,0:T(8,128)S(1)} %shard_map.67.refs_0_), channel_id=1, source_target_pairs={{0,3},{1,0},{2,1},{3,2},{4,7},{5,4},{6,5},{7,6},{8,11},{9,8},{10,9... | collective-permute-start | bytes 589832 | tf_op jit(solution)/shard_map/ppermute | solution.py:229
  99.5 7.6 %collective-permute-start.14 = (bf16[192,256]{1,0:T(8,128)(2,1)S(1)}, bf16[192,256]{1,0:T(8,128)(2,1)S(1)}, u32[]{:S(2)}, u32[]{:S(2)}) collective-permute-start(bf16[192,256]{1,0:T(8,128)(2,1)S(1)} %shard_map.68.refs_0_), channel_id=1, source_target_pairs={{0,4},{1,5},{2,6},{3,7},{4,8},{5,9},{6,10},{7,11},{8,12},{9,13},{1... | collective-permute-start | bytes 294920 | tf_op jit(solution)/shard_map/ppermute | solution.py:229
  101.5 6.1 %collective-permute-start.15 = (bf16[192,256]{1,0:T(8,128)(2,1)S(1)}, bf16[192,256]{1,0:T(8,128)(2,1)S(1)}, u32[]{:S(2)}, u32[]{:S(2)}) collective-permute-start(bf16[192,256]{1,0:T(8,128)(2,1)S(1)} %shard_map.68.refs_0_), channel_id=1, source_target_pairs={{0,8},{1,9},{2,10},{3,11},{4,12},{5,13},{6,14},{7,15},{8,0},{9,1},... | collective-permute-start | bytes 294920 | tf_op jit(solution)/shard_map/ppermute | solution.py:229
  103.6 4.6 %collective-permute-start.16 = (bf16[192,256]{1,0:T(8,128)(2,1)S(1)}, bf16[192,256]{1,0:T(8,128)(2,1)S(1)}, u32[]{:S(2)}, u32[]{:S(2)}) collective-permute-start(bf16[192,256]{1,0:T(8,128)(2,1)S(1)} %shard_map.68.refs_0_), channel_id=1, source_target_pairs={{0,12},{1,13},{2,14},{3,15},{4,0},{5,1},{6,2},{7,3},{8,4},{9,5},{1... | collective-permute-start | bytes 294920 | tf_op jit(solution)/shard_map/ppermute | solution.py:229
  108.8 8.0 %collective-permute-start.18 = (bf16[2,384,256]{2,1,0:T(8,128)(2,1)S(1)}, bf16[2,384,256]{2,1,0:T(8,128)(2,1)S(1)}, u32[]{:S(2)}, u32[]{:S(2)}) collective-permute-start(bf16[2,384,256]{2,1,0:T(8,128)(2,1)S(1)} %shard_map.70.refs_0_), channel_id=1, source_target_pairs={{0,32},{1,33},{2,34},{3,35},{4,36},{5,37},{6,38},{7,39},{8,40},{9,... | collective-permute-start | bytes 1179656 | tf_op jit(solution)/shard_map/ppermute | solution.py:229
  110.1 9.4 %collective-permute-start.20 = (bf16[2,384,256]{2,1,0:T(8,128)(2,1)S(1)}, bf16[2,384,256]{2,1,0:T(8,128)(2,1)S(1)}, u32[]{:S(2)}, u32[]{:S(2)}) collective-permute-start(bf16[2,384,256]{2,1,0:T(8,128)(2,1)S(1)} %shard_map.70.refs_0_), channel_id=1, source_target_pairs={{0,64},{1,65},{2,66},{3,67},{4,68},{5,69},{6,70},{7,71},{8,72},{9,... | collective-permute-start | bytes 1179656 | tf_op jit(solution)/shard_map/ppermute | solution.py:229
  111.3 12.0 %collective-permute-start.22 = (bf16[2,384,256]{2,1,0:T(8,128)(2,1)S(1)}, bf16[2,384,256]{2,1,0:T(8,128)(2,1)S(1)}, u32[]{:S(2)}, u32[]{:S(2)}) collective-permute-start(bf16[2,384,256]{2,1,0:T(8,128)(2,1)S(1)} %shard_map.70.refs_0_), channel_id=1, source_target_pairs={{0,96},{1,97},{2,98},{3,99},{4,100},{5,101},{6,102},{7,103},{8,104... | collective-permute-start | bytes 1179656 | tf_op jit(solution)/shard_map/ppermute | solution.py:229
  113.2 11.5 %collective-permute-start.17 = (bf16[2,384,256]{2,1,0:T(8,128)(2,1)S(1)}, bf16[2,384,256]{2,1,0:T(8,128)(2,1)S(1)}, u32[]{:S(2)}, u32[]{:S(2)}) collective-permute-start(bf16[2,384,256]{2,1,0:T(8,128)(2,1)S(1)} %shard_map.70.refs_0_), channel_id=1, source_target_pairs={{0,16},{16,0},{1,17},{17,1},{2,18},{18,2},{3,19},{19,3},{4,20},{20... | collective-permute-start | bytes 1179656 | tf_op jit(solution)/shard_map/ppermute | solution.py:192
  116.9 7.9 %collective-permute-start.19 = (bf16[2,384,256]{2,1,0:T(8,128)(2,1)S(1)}, bf16[2,384,256]{2,1,0:T(8,128)(2,1)S(1)}, u32[]{:S(2)}, u32[]{:S(2)}) collective-permute-start(bf16[2,384,256]{2,1,0:T(8,128)(2,1)S(1)} %collective-permute-done.18.refs_1_), channel_id=1, source_target_pairs={{0,16},{16,0},{1,17},{17,1},{2,18},{18,2},{3,19},{19,3},{4,20},{20... | collective-permute-start | bytes 1179656 | tf_op jit(solution)/shard_map/ppermute | solution.py:192
  119.5 5.3 %collective-permute-start.21 = (bf16[2,384,256]{2,1,0:T(8,128)(2,1)S(1)}, bf16[2,384,256]{2,1,0:T(8,128)(2,1)S(1)}, u32[]{:S(2)}, u32[]{:S(2)}) collective-permute-start(bf16[2,384,256]{2,1,0:T(8,128)(2,1)S(1)} %collective-permute-done.20.refs_2_), channel_id=1, source_target_pairs={{0,16},{16,0},{1,17},{17,1},{2,18},{18,2},{3,19},{19,3},{4,20},{20... | collective-permute-start | bytes 1179656 | tf_op jit(solution)/shard_map/ppermute | solution.py:192
  123.3 1.7 %collective-permute-start.23 = (bf16[2,384,256]{2,1,0:T(8,128)(2,1)S(1)}, bf16[2,384,256]{2,1,0:T(8,128)(2,1)S(1)}, u32[]{:S(2)}, u32[]{:S(2)}) collective-permute-start(bf16[2,384,256]{2,1,0:T(8,128)(2,1)S(1)} %collective-permute-done.22.refs_3_), channel_id=1, source_target_pairs={{0,16},{16,0},{1,17},{17,1},{2,18},{18,2},{3,19},{19,3},{4,20},{20... | collective-permute-start | bytes 1179656 | tf_op jit(solution)/shard_map/ppermute | solution.py:192
  123.3 1.7 %copy-start.2 = (bf16[768,768]{1,0:T(8,128)(2,1)S(1)}, bf16[768,768]{1,0:T(8,128)(2,1)}, u32[]{:S(2)}) copy-start(bf16[768,768]{1,0:T(8,128)(2,1)} %refs_10_.1) | copy-start | bytes 3538948
  123.3 1.7 %copy-start.3 = (bf16[768,768]{1,0:T(8,128)(2,1)S(1)}, bf16[768,768]{1,0:T(8,128)(2,1)}, u32[]{:S(2)}) copy-start(bf16[768,768]{1,0:T(8,128)(2,1)} %refs_11_.1) | copy-start | bytes 3538948
  123.3 2.0 %copy-start.4 = (bf16[768,768]{1,0:T(8,128)(2,1)S(1)}, bf16[768,768]{1,0:T(8,128)(2,1)}, u32[]{:S(2)}) copy-start(bf16[768,768]{1,0:T(8,128)(2,1)} %refs_12_.1) | copy-start | bytes 3538948

commit v5 on v3

--- a/solution.py
+++ b/solution.py
@@ -33,12 +33,10 @@
             o_ref[:, s * head : (s + 1) * head, :] = out.reshape(heads, head, res)
 
 
-def pair_products(core, scale, a_ref, b_ref, own_ref, other_ref):
-    half = own_ref.shape[0]
-    for h in range(half):
-        for ref, base in ((own_ref, core * half), (other_ref, (1 - core) * half)):
-            product = dot(a_ref[base + h], b_ref[base + h], TN)
-            ref[h] = (product if scale is None else scale * product).astype(ref.dtype)
+def half_products(base, scale, a_ref, b_ref, out_ref):
+    for h in range(out_ref.shape[0]):
+        product = dot(a_ref[base + h], b_ref[base + h], TN)
+        out_ref[h] = (product if scale is None else scale * product).astype(out_ref.dtype)
 
 
 def start(pairs, sems):
@@ -48,18 +46,21 @@
     return copies
 
 
-def rows_kernel(scale, place_ref, x_in, wq_in, wk_in, q_out, k_out, own_ref, other_ref, wq, wk, t_ref, x_ref, q_ref, k_ref, in_sems, out_sems):
-    loads = start(((wq_in, wq), (x_in, x_ref), (wk_in, wk)), in_sems)
+def rows_kernel(scale, place_ref, x_in, wq_in, wk_in, q_ref, k_ref, other_ref, wq, wk, t_ref, x_ref, sems):
+    loads = start(((wq_in, wq), (x_in, x_ref), (wk_in, wk)), sems)
     loads[0].wait()
     t_ref[...] = wq[...].T
     loads[1].wait()
     project(x_ref, ((t_ref, q_ref),))
-    stores = start(((q_ref, q_out),), out_sems.at[pl.ds(0, 1)])
     loads[2].wait()
     t_ref[...] = wk[...].T
     project(x_ref, ((t_ref, k_ref),))
-    stores += start(((k_ref, k_out),), out_sems.at[pl.ds(1, 1)])
-    pair_products(place_ref[0], scale, q_ref, k_ref, own_ref, other_ref)
+    half_products((1 - place_ref[0]) * other_ref.shape[0], scale, q_ref, k_ref, other_ref)
+
+
+def own_rows_kernel(scale, place_ref, q_ref, k_ref, q_out, k_out, own_ref, sems):
+    stores = start(((q_ref, q_out), (k_ref, k_out)), sems)
+    half_products(place_ref[0] * own_ref.shape[0], scale, q_ref, k_ref, own_ref)
     for store in stores:
         store.wait()
 
@@ -69,14 +70,16 @@
     project(x_ref, ((t_ref, v_ref),))
 
 
-def grad_rows_kernel(place_ref, c_ref, w_in, v_in, g_out, own_ref, other_ref, w, v_ref, g_ref, in_sems, out_sems):
-    loads = start(((w_in, w), (v_in, v_ref)), in_sems)
+def grad_rows_kernel(place_ref, c_ref, w_in, v_in, g_ref, v_ref, other_ref, w, sems):
+    loads = start(((w_in, w), (v_in, v_ref)), sems)
     loads[0].wait()
     project(c_ref, ((w, g_ref),))
-    stores = start(((g_ref, g_out),), out_sems)
     loads[1].wait()
-    pair_products(place_ref[0], None, g_ref, v_ref, own_ref, other_ref)
-    stores[0].wait()
+    half_products((1 - place_ref[0]) * other_ref.shape[0], None, g_ref, v_ref, other_ref)
+
+
+def own_grad_kernel(place_ref, g_ref, v_ref, own_ref):
+    half_products(place_ref[0] * own_ref.shape[0], None, g_ref, v_ref, own_ref)
 
 
 def split_kernel(place_ref, a_ref, b_ref, *outs):
@@ -241,16 +244,19 @@
         )
 
     def row_part(rows, *weights):
-        q, k, own, other = call(
+        q, k, other = call(
             lambda *refs: rows_kernel(scaling, *refs),
-            (packed, packed, sums, sums),
+            (packed, packed, sums),
             place, rows, *weights[:2],
-            specs=(SMEM, HBM, HBM, HBM), out_specs=(HBM, HBM, VMEM, VMEM),
-            scratch=[weight] * 3
-            + [pltpu.VMEM((blocks, seqs, block, width), BF16)]
-            + [held] * 2
-            + [sems((3,)), sems((2,))],
+            specs=(SMEM, HBM, HBM, HBM),
+            scratch=[weight] * 3 + [pltpu.VMEM((blocks, seqs, block, width), BF16), sems((3,))],
             mib=24,
+        )
+        q, k, own = call(
+            lambda *refs: own_rows_kernel(scaling, *refs),
+            (packed, packed, sums),
+            place, q, k,
+            specs=(SMEM, VMEM, VMEM), out_specs=(HBM, HBM, VMEM), scratch=[sems((2,))],
         )
         v = call(value_kernel, packed, rows, weights[2], scratch=[weight])
         return q, k, v, call(sum_kernel, shape(quarter, F32), *spread(split(F32, own, other), 0))
@@ -259,11 +265,11 @@
         return *(jnp.zeros(packed.shape, BF16) for _ in range(3)), jnp.zeros(quarter, F32)
 
     q, k, v, logit = lax.cond(core < 2, row_part, no_part, rows, w_query, w_key, w_value)
-    g, grad_own, grad_other = call(
-        grad_rows_kernel, (packed, sums, shape(sums.shape)), place, cot_rows, w_out, v,
-        specs=(SMEM, VMEM, HBM, HBM), out_specs=(HBM, VMEM, VMEM),
-        scratch=[weight, held, held, sems((2,)), sems((1,))],
-    )
+    g, v, grad_other = call(
+        grad_rows_kernel, (packed, packed, shape(sums.shape)), place, cot_rows, w_out, v,
+        specs=(SMEM, VMEM, HBM, HBM), scratch=[weight, sems((2,))],
+    )
+    grad_own = call(own_grad_kernel, sums, place, g, v, specs=(SMEM, VMEM, VMEM))
     grads = spread(split(BF16, grad_own, grad_other), 0)
     both = (quarter[0] // 2, res)
     terms = call(
@@ -273,9 +279,7 @@
     result = call(
         lambda *refs: softmax_kernel(scaling, *refs), shape(both), *spread([term] * 4, 2)
     )
-    q, k, g = call(
-        fetch_kernel, [packed] * 3, q, k, g, specs=[HBM] * 3, scratch=[sems((3,))]
-    )
+    q, k = call(fetch_kernel, [packed] * 2, q, k, specs=[HBM] * 2, scratch=[sems((2,))])
     result = call(
         join_kernel, shape((2,) + quarter), place, *spread([result] * 4, 1), q,
         specs=[SMEM] + [VMEM] * 4 + [ANY],

time: 162 us -> 162 us (level)
  starting transfers between devices: 36.5 us -> 32.3 us
  waiting for transfers between devices: 40.5 us -> 42.9 us
  Pallas kernels: 22.9 us -> 25.2 us
    ppermute x18, waiting for transfers between devices: 33.5 us -> 39.3 us  [spread(): sent = {d: lax.ppermute(parts[d], AXES, turn(stage, d)) for d in (1, 3, 2)}]
    ppermute x18, starting transfers between devices: 30.1 us -> 25.1 us  [spread(): sent = {d: lax.ppermute(parts[d], AXES, turn(stage, d)) for d in (1, 3, 2)}]
    ppermute x6, waiting for transfers between devices: 7.02 us -> 3.6 us  [shift(): return lax.ppermute(a, axis, [(i, (i + step) % n) for i in range(n)])]
    pallas_call x12 -> x14, Pallas kernels: 22.9 us -> 25.2 us  [call(): pl.pallas_call(kernel, out_shape=outs, in_specs=list(specs or [VMEM] * le...]
  transfers between devices with their start and end apart: 25 -> 25, of which waited for: 18 -> 18; matrix products, arithmetic and copies ran while one was open for 0% -> 0% of each run, Pallas kernels for 7% -> 9%
where the time goes in v5:
time: 162 us; the launch traced here: 161 us
  blocking collectives  59.6 us (37%)
  waiting for transfers between devices  42.9 us (26%)
  starting transfers between devices  32.3 us (20%)
  Pallas kernels  25.2 us (16%)
    all_to_all x2, blocking collectives, exchange(): lax.all_to_all(a, ('z', 'y'), split_axis=0, concat_axis=0, tiled=True)  59.6 us
    ppermute x18, waiting for transfers between devices, spread(): sent = {d: lax.ppermute(parts[d], AXES, turn(stage, d)) for d in (1, 3, 2)}  39.3 us
    pallas_call x14, Pallas kernels, call(): pl.pallas_call(kernel, out_shape=outs, in_specs=list(specs or [VMEM] * le...  25.2 us
    ppermute x18, starting transfers between devices, spread(): sent = {d: lax.ppermute(parts[d], AXES, turn(stage, d)) for d in (1, 3, 2)}  25.1 us
    all_to_all x1, starting transfers between devices, exchange(): lax.all_to_all(a, ('z', 'y'), split_axis=0, concat_axis=0, tiled=True)  3.71 us
    ppermute x6, waiting for transfers between devices, shift(): return lax.ppermute(a, axis, [(i, (i + step) % n) for i in range(n)])  3.6 us
    ppermute x6, starting transfers between devices, shift(): return lax.ppermute(a, axis, [(i, (i + step) % n) for i in range(n)])  3.42 us
  transfers between devices with their start and end apart: 25, of which 18 were waited for; matrix products, arithmetic and copies ran while one was open for 0% of the time, Pallas kernels for 9%

profile of v5, /device:TPU:2, one launch (start us, length us, event | category | flops | bytes accessed | tf_op | source)
XLA Modules:
  0.0 161.3 jit_solution(666969034073793886)
XLA Ops:
  0.0 30.9 %all_to_all.15 = bf16[16,4,16,768]{3,2,1,0:T(8,128)(2,1)} all-to-all(bf16[16,4,16,768]{3,2,1,0:T(8,128)(2,1)} %bitcast.16), channel_id=1, replica_groups=mesh['x'=4,'core'=2,'z'=4,'y'=4] {'z','y'}, dimensions={0} | all-to-all | bytes 3145728 | tf_op jit(solution)/shard_map/all_to_all | solution.py:223
  30.9 3.7 %all-to-all-start.1 = ((bf16[16,4,16,768]{3,2,1,0:T(8,128)(2,1)}), bf16[16,4,16,768]{3,2,1,0:T(8,128)(2,1)S(1)}, u32[]{:S(2)}, u32[]{:S(2)}) async-start(bf16[16,4,16,768]{3,2,1,0:T(8,128)(2,1)} %bitcast.7), calls=%async_computation.1 | async-start | bytes 3145728 | tf_op jit(solution)/shard_map/all_to_all | solution.py:223
  34.7 0.1 pad_add_fusion.place_ref
  34.7 24.5 %conditional.1 = (bf16[12,256,256]{2,1,0:T(8,128)(2,1)}, bf16[12,256,256]{2,1,0:T(8,128)(2,1)}, bf16[12,256,256]{2,1,0:T(8,128)(2,1)}, f32[384,256]{1,0:T(8,128)S(1)}) conditional(s32[]{:T(128)} %convert_element_type.3, () %tuple.13, (s32[4]{0:T(128)S(1)}, bf16[16,4,16,768]{3,2,1,0:T(8,128)(2,1)}, bf16[768,768]{1,0:T(8,128)(2,1)}, ...), branch_computations={%region_0.1_spmd, %region_1.2_spmd} | conditional | bytes 22020344 | solution.py:267
  34.7 5.6 %branch_1_fun.5 = (bf16[12,256,256]{2,1,0:T(8,128)(2,1)S(1)}, bf16[12,256,256]{2,1,0:T(8,128)(2,1)S(1)}, f32[6,256,256]{2,1,0:T(8,128)S(1)}) custom-call(s32[4]{0:T(128)S(1)} %get-tuple-element.15.refs_0_.place_ref, bf16[16,4,16,768]{3,2,1,0:T(8,128)(2,1)} %get-tuple-element.16.refs_1_.x_ref, bf16[768,768]{1,0:T(8,128)(2,1)} %get-tuple-element.17.refs_2_, ...), custom_call_target="tpu_custom_call" | custom-call | tf_op jit(solution)/shard_map/cond/branch_1_fun/pallas_call | solution.py:173
  40.3 0.1 collective-permute-start
  40.4 2.4 %branch_1_fun.6 = (bf16[12,256,256]{2,1,0:T(8,128)(2,1)}, bf16[12,256,256]{2,1,0:T(8,128)(2,1)}, f32[6,256,256]{2,1,0:T(8,128)S(1)}) custom-call(s32[4]{0:T(128)S(1)} %get-tuple-element.15.refs_0_.place_ref, bf16[12,256,256]{2,1,0:T(8,128)(2,1)S(1)} %get-tuple-element.19.refs_1_, bf16[12,256,256]{2,1,0:T(8,128)(2,1)S(1)} %get-tuple-element.20.refs_2_), custom_call_target="tpu_custom_call" | custom-call | tf_op jit(solution)/shard_map/cond/branch_1_fun/pallas_call | solution.py:173
  42.8 0.9 collective-permute-done
  43.8 0.7 branch_1_fun.8
  44.5 1.6 collective-permute-start.1
  46.1 1.1 collective-permute-start.2
  47.2 2.2 %collective-permute-start.3 = (f32[384,256]{1,0:T(8,128)S(1)}, f32[384,256]{1,0:T(8,128)S(1)}, u32[]{:S(2)}, u32[]{:S(2)}) collective-permute-start(f32[384,256]{1,0:T(8,128)S(1)} %get-tuple-element.29), channel_id=1, source_target_pairs={{0,96},{1,97},{2,98},{3,99},{4,100},{5,101},{6,102},{7,103},{8,104... | collective-permute-start | bytes 1179656 | tf_op jit(solution)/shard_map/cond/branch_1_fun/ppermute | solution.py:226
  49.3 2.6 %branch_1_fun.7 = bf16[12,256,256]{2,1,0:T(8,128)(2,1)} custom-call(bf16[16,4,16,768]{3,2,1,0:T(8,128)(2,1)S(1)} %copy-done.1, bf16[768,768]{1,0:T(8,128)(2,1)S(1)} %copy-done.5), custom_call_target="tpu_custom_call" | custom-call | tf_op jit(solution)/shard_map/cond/branch_1_fun/pallas_call | solution.py:173
  51.9 0.5 collective-permute-done.1.refs_1_
  52.4 3.1 %collective-permute-done.2.refs_2_ = f32[384,256]{1,0:T(8,128)S(1)} collective-permute-done((f32[384,256]{1,0:T(8,128)S(1)}, f32[384,256]{1,0:T(8,128)S(1)}, u32[]{:S(2)}, u32[]{:S(2)}) %collective-permute-start.2) | collective-permute-done | bytes 393248 | tf_op jit(solution)/shard_map/cond/branch_1_fun/ppermute | solution.py:226
  55.5 3.7 %collective-permute-done.3.refs_3_ = f32[384,256]{1,0:T(8,128)S(1)} collective-permute-done((f32[384,256]{1,0:T(8,128)S(1)}, f32[384,256]{1,0:T(8,128)S(1)}, u32[]{:S(2)}, u32[]{:S(2)}) %collective-permute-start.3) | collective-permute-done | bytes 393248 | tf_op jit(solution)/shard_map/cond/branch_1_fun/ppermute | solution.py:226
  59.2 0.1 branch_1_fun.9
  59.3 2.6 %shard_map.64 = (bf16[12,256,256]{2,1,0:T(8,128)(2,1)S(1)}, bf16[12,256,256]{2,1,0:T(8,128)(2,1)S(1)}, bf16[6,256,256]{2,1,0:T(8,128)(2,1)S(1)}) custom-call(s32[4]{0:T(128)S(1)} %pad_add_fusion.place_ref, bf16[16,4,16,768]{3,2,1,0:T(8,128)(2,1)S(1)} %all-to-all-done.1.c_ref, bf16[768,768]{1,0:T(8,128)(2,1)S(1)} %copy-done, ...), custom_call_target="tpu_custom_call" | custom-call | tf_op jit(solution)/shard_map/pallas_call | solution.py:173
  61.9 3.3 %collective-permute-start.4 = (bf16[6,256,256]{2,1,0:T(8,128)(2,1)S(1)}, bf16[6,256,256]{2,1,0:T(8,128)(2,1)S(1)}, u32[]{:S(2)}, u32[]{:S(2)}) collective-permute-start(bf16[6,256,256]{2,1,0:T(8,128)(2,1)S(1)} %get-tuple-element.51), channel_id=1, source_target_pairs={{0,16},{16,0},{1,17},{17,1},{2,18},{18,2},{3,19},{19,3},{4,20},{20... | collective-permute-start | bytes 2359304 | tf_op jit(solution)/shard_map/ppermute | solution.py:189
  65.2 1.0 shard_map.65
  66.2 1.0 collective-permute-done.4
  67.2 0.7 shard_map.66
  67.8 1.5 collective-permute-start.5
  69.4 1.1 collective-permute-start.6
  70.5 2.1 %collective-permute-start.7 = (bf16[384,256]{1,0:T(8,128)(2,1)S(1)}, bf16[384,256]{1,0:T(8,128)(2,1)S(1)}, u32[]{:S(2)}, u32[]{:S(2)}) collective-permute-start(bf16[384,256]{1,0:T(8,128)(2,1)S(1)} %get-tuple-element.55), channel_id=1, source_target_pairs={{0,96},{1,97},{2,98},{3,99},{4,100},{5,101},{6,102},{7,103},{8,104... | collective-permute-start | bytes 589832 | tf_op jit(solution)/shard_map/ppermute | solution.py:226
  72.7 0.9 collective-permute-done.5.refs_1_
  73.6 3.1 %collective-permute-done.6.refs_2_ = bf16[384,256]{1,0:T(8,128)(2,1)S(1)} collective-permute-done((bf16[384,256]{1,0:T(8,128)(2,1)S(1)}, bf16[384,256]{1,0:T(8,128)(2,1)S(1)}, u32[]{:S(2)}, u32[]{:S(2)}) %collective-permute-start.6) | collective-permute-done | bytes 196640 | tf_op jit(solution)/shard_map/ppermute | solution.py:226
  76.7 1.6 %collective-permute-done.7.refs_3_ = bf16[384,256]{1,0:T(8,128)(2,1)S(1)} collective-permute-done((bf16[384,256]{1,0:T(8,128)(2,1)S(1)}, bf16[384,256]{1,0:T(8,128)(2,1)S(1)}, u32[]{:S(2)}, u32[]{:S(2)}) %collective-permute-start.7) | collective-permute-done | bytes 196640 | tf_op jit(solution)/shard_map/ppermute | solution.py:226
  78.3 0.6 shard_map.67
  79.0 2.8 %collective-permute-start.10 = (f32[192,256]{1,0:T(8,128)S(1)}, f32[192,256]{1,0:T(8,128)S(1)}, u32[]{:S(2)}, u32[]{:S(2)}) collective-permute-start(f32[192,256]{1,0:T(8,128)S(1)} %get-tuple-element.59), channel_id=1, source_target_pairs={{0,12},{1,13},{2,14},{3,15},{4,0},{5,1},{6,2},{7,3},{8,4},{9,5},{1... | collective-permute-start | bytes 589832 | tf_op jit(solution)/shard_map/ppermute | solution.py:226
  81.8 0.0 collective-permute-start.8
  81.8 2.3 %collective-permute-start.9 = (f32[192,256]{1,0:T(8,128)S(1)}, f32[192,256]{1,0:T(8,128)S(1)}, u32[]{:S(2)}, u32[]{:S(2)}) collective-permute-start(f32[192,256]{1,0:T(8,128)S(1)} %get-tuple-element.58), channel_id=1, source_target_pairs={{0,8},{1,9},{2,10},{3,11},{4,12},{5,13},{6,14},{7,15},{8,0},{9,1},... | collective-permute-start | bytes 589832 | tf_op jit(solution)/shard_map/ppermute | solution.py:226
  84.1 0.9 collective-permute-done.10.refs_3_
  85.0 6.6 %collective-permute-done.8.refs_1_ = f32[192,256]{1,0:T(8,128)S(1)} collective-permute-done((f32[192,256]{1,0:T(8,128)S(1)}, f32[192,256]{1,0:T(8,128)S(1)}, u32[]{:S(2)}, u32[]{:S(2)}) %collective-permute-start.8) | collective-permute-done | bytes 196640 | tf_op jit(solution)/shard_map/ppermute | solution.py:226
  91.6 0.9 collective-permute-start.11
  92.5 0.2 collective-permute-start.12
  92.7 2.5 %collective-permute-start.13 = (f32[192,256]{1,0:T(8,128)S(1)}, f32[192,256]{1,0:T(8,128)S(1)}, u32[]{:S(2)}, u32[]{:S(2)}) collective-permute-start(f32[192,256]{1,0:T(8,128)S(1)} %shard_map.68.refs_0_), channel_id=1, source_target_pairs={{0,3},{1,0},{2,1},{3,2},{4,7},{5,4},{6,5},{7,6},{8,11},{9,8},{10,9... | collective-permute-start | bytes 589832 | tf_op jit(solution)/shard_map/ppermute | solution.py:226
  95.2 5.4 %collective-permute-done.11.refs_1_ = f32[192,256]{1,0:T(8,128)S(1)} collective-permute-done((f32[192,256]{1,0:T(8,128)S(1)}, f32[192,256]{1,0:T(8,128)S(1)}, u32[]{:S(2)}, u32[]{:S(2)}) %collective-permute-start.11) | collective-permute-done | bytes 196640 | tf_op jit(solution)/shard_map/ppermute | solution.py:226
  100.6 0.0 collective-permute-done.12.refs_2_
  100.6 0.9 collective-permute-done.13.refs_3_
  101.5 0.3 shard_map.69.refs_0_
  101.8 0.1 collective-permute-start.14
  101.9 2.1 %collective-permute-start.15 = (bf16[192,256]{1,0:T(8,128)(2,1)S(1)}, bf16[192,256]{1,0:T(8,128)(2,1)S(1)}, u32[]{:S(2)}, u32[]{:S(2)}) collective-permute-start(bf16[192,256]{1,0:T(8,128)(2,1)S(1)} %shard_map.69.refs_0_), channel_id=1, source_target_pairs={{0,8},{1,9},{2,10},{3,11},{4,12},{5,13},{6,14},{7,15},{8,0},{9,1},... | collective-permute-start | bytes 294920 | tf_op jit(solution)/shard_map/ppermute | solution.py:226
  104.0 1.1 collective-permute-start.16
  105.1 2.0 %shard_map.70 = (bf16[12,256,256]{2,1,0:T(8,128)(2,1)S(1)}, bf16[12,256,256]{2,1,0:T(8,128)(2,1)S(1)}) custom-call(bf16[12,256,256]{2,1,0:T(8,128)(2,1)} %get-tuple-element.60.refs_0_, bf16[12,256,256]{2,1,0:T(8,128)(2,1)} %get-tuple-element.61.refs_1_), custom_call_target="tpu_custom_call" | custom-call | tf_op jit(solution)/shard_map/pallas_call | solution.py:173
  107.1 0.0 copy-start.2
  107.1 0.0 copy-start.3
  107.1 1.6 collective-permute-done.14.refs_1_
  108.8 0.0 collective-permute-done.15.refs_2_
  108.8 0.9 collective-permute-done.16.refs_3_
  109.7 0.6 shard_map.71.refs_0_
  110.2 1.0 collective-permute-start.17
  111.2 0.5 collective-permute-start.18
  111.7 1.9 %collective-permute-start.19 = (bf16[2,384,256]{2,1,0:T(8,128)(2,1)S(1)}, bf16[2,384,256]{2,1,0:T(8,128)(2,1)S(1)}, u32[]{:S(2)}, u32[]{:S(2)}) collective-permute-start(bf16[2,384,256]{2,1,0:T(8,128)(2,1)S(1)} %shard_map.71.refs_0_), channel_id=1, source_target_pairs={{0,96},{1,97},{2,98},{3,99},{4,100},{5,101},{6,102},{7,103},{8,104... | collective-permute-start | bytes 1179656 | tf_op jit(solution)/shard_map/ppermute | solution.py:226
  113.7 0.0 collective-permute-start.20
  113.7 4.4 %collective-permute-done.17.refs_1_ = bf16[2,384,256]{2,1,0:T(8,128)(2,1)S(1)} collective-permute-done((bf16[2,384,256]{2,1,0:T(8,128)(2,1)S(1)}, bf16[2,384,256]{2,1,0:T(8,128)(2,1)S(1)}, u32[]{:S(2)}, u32[]{:S(2)}) %collective-permute-start.17) | collective-permute-done | bytes 393248 | tf_op jit(solution)/shard_map/ppermute | solution.py:226
  118.1 0.0 collective-permute-start.21
  118.1 2.5 %collective-permute-done.18.refs_2_ = bf16[2,384,256]{2,1,0:T(8,128)(2,1)S(1)} collective-permute-done((bf16[2,384,256]{2,1,0:T(8,128)(2,1)S(1)}, bf16[2,384,256]{2,1,0:T(8,128)(2,1)S(1)}, u32[]{:S(2)}, u32[]{:S(2)}) %collective-permute-start.18) | collective-permute-done | bytes 393248 | tf_op jit(solution)/shard_map/ppermute | solution.py:226
  120.6 0.0 collective-permute-start.22
  120.6 3.2 %collective-permute-done.19.refs_3_ = bf16[2,384,256]{2,1,0:T(8,128)(2,1)S(1)} collective-permute-done((bf16[2,384,256]{2,1,0:T(8,128)(2,1)S(1)}, bf16[2,384,256]{2,1,0:T(8,128)(2,1)S(1)}, u32[]{:S(2)}, u32[]{:S(2)}) %collective-permute-start.19) | collective-permute-done | bytes 393248 | tf_op jit(solution)/shard_map/ppermute | solution.py:226
  123.8 1.7 %collective-permute-done.23.refs_7_ = bf16[2,384,256]{2,1,0:T(8,128)(2,1)S(1)} collective-permute-done((bf16[2,384,256]{2,1,0:T(8,128)(2,1)S(1)}, bf16[2,384,256]{2,1,0:T(8,128)(2,1)S(1)}, u32[]{:S(2)}, u32[]{:S(2)}) %collective-permute-start.23) | collective-permute-done | bytes 393248 | tf_op jit(solution)/shard_map/ppermute | solution.py:189
  125.5 6.0 %shard_map.72 = bf16[16,4,16,768]{3,2,1,0:T(8,128)(2,1)S(1)} custom-call(s32[4]{0:T(128)S(1)} %pad_add_fusion.place_ref, bf16[2,384,256]{2,1,0:T(8,128)(2,1)S(1)} %shard_map.71.refs_0_, bf16[2,384,256]{2,1,0:T(8,128)(2,1)S(1)} %collective-permute-done.17.refs_1_, bf16[2,384,256]{2,1,0:T(8,128)(2,1)S(1)} %collective-permute-done.18.refs_2_, ...), custom_call_target="tpu_custom_call" | custom-call | tf_op jit(solution)/shard_map/pallas_call | solution.py:173
  131.5 28.7 %all_to_all.16 = bf16[16,4,16,768]{3,2,1,0:T(8,128)(2,1)S(1)} all-to-all(bf16[16,4,16,768]{3,2,1,0:T(8,128)(2,1)S(1)} %shard_map.72), channel_id=1, replica_groups=mesh['x'=4,'core'=2,'z'=4,'y'=4] {'z','y'}, dimensions={0} | all-to-all | bytes 3145728 | tf_op jit(solution)/shard_map/all_to_all | solution.py:223
  160.2 1.1 copy.16
  (17 shorter events, 0.1 us)
Async XLA Ops:
  30.9 28.3 %all-to-all-start.1 = ((bf16[16,4,16,768]{3,2,1,0:T(8,128)(2,1)}), bf16[16,4,16,768]{3,2,1,0:T(8,128)(2,1)S(1)}, u32[]{:S(2)}, u32[]{:S(2)}) async-start(bf16[16,4,16,768]{3,2,1,0:T(8,128)(2,1)} %bitcast.7), calls=%async_computation.1 | async-start | bytes 3145728 | tf_op jit(solution)/shard_map/all_to_all | solution.py:223
  34.7 24.5 %copy-start = (bf16[768,768]{1,0:T(8,128)(2,1)S(1)}, bf16[768,768]{1,0:T(8,128)(2,1)}, u32[]{:S(2)}) copy-start(bf16[768,768]{1,0:T(8,128)(2,1)} %w_in.1) | copy-start | bytes 3538948
  40.3 3.5 %collective-permute-start = (f32[6,256,256]{2,1,0:T(8,128)S(1)}, f32[6,256,256]{2,1,0:T(8,128)S(1)}, u32[]{:S(2)}, u32[]{:S(2)}) collective-permute-start(f32[6,256,256]{2,1,0:T(8,128)S(1)} %get-tuple-element.25), channel_id=1, source_target_pairs={{0,16},{16,0},{1,17},{17,1},{2,18},{18,2},{3,19},{19,3},{4,20},{20... | collective-permute-start | bytes 4718600 | tf_op jit(solution)/shard_map/cond/branch_1_fun/ppermute | solution.py:189
  43.8 5.5 %copy-start.1 = (bf16[16,4,16,768]{3,2,1,0:T(8,128)(2,1)S(1)}, bf16[16,4,16,768]{3,2,1,0:T(8,128)(2,1)}, u32[]{:S(2)}) copy-start(bf16[16,4,16,768]{3,2,1,0:T(8,128)(2,1)} %get-tuple-element.16.refs_1_.x_ref) | copy-start | bytes 4718596 | tf_op jit(solution)/shard_map/cond
  43.8 5.5 %copy-start.5 = (bf16[768,768]{1,0:T(8,128)(2,1)S(1)}, bf16[768,768]{1,0:T(8,128)(2,1)}, u32[]{:S(2)}) copy-start(bf16[768,768]{1,0:T(8,128)(2,1)} %get-tuple-element.23.w_ref) | copy-start | bytes 3538948 | tf_op jit(solution)/shard_map/cond
  44.5 7.8 %collective-permute-start.1 = (f32[384,256]{1,0:T(8,128)S(1)}, f32[384,256]{1,0:T(8,128)S(1)}, u32[]{:S(2)}, u32[]{:S(2)}) collective-permute-start(f32[384,256]{1,0:T(8,128)S(1)} %get-tuple-element.27), channel_id=1, source_target_pairs={{0,32},{1,33},{2,34},{3,35},{4,36},{5,37},{6,38},{7,39},{8,40},{9,... | collective-permute-start | bytes 1179656 | tf_op jit(solution)/shard_map/cond/branch_1_fun/ppermute | solution.py:226
  46.1 9.4 %collective-permute-start.2 = (f32[384,256]{1,0:T(8,128)S(1)}, f32[384,256]{1,0:T(8,128)S(1)}, u32[]{:S(2)}, u32[]{:S(2)}) collective-permute-start(f32[384,256]{1,0:T(8,128)S(1)} %get-tuple-element.28), channel_id=1, source_target_pairs={{0,64},{1,65},{2,66},{3,67},{4,68},{5,69},{6,70},{7,71},{8,72},{9,... | collective-permute-start | bytes 1179656 | tf_op jit(solution)/shard_map/cond/branch_1_fun/ppermute | solution.py:226
  47.2 12.0 %collective-permute-start.3 = (f32[384,256]{1,0:T(8,128)S(1)}, f32[384,256]{1,0:T(8,128)S(1)}, u32[]{:S(2)}, u32[]{:S(2)}) collective-permute-start(f32[384,256]{1,0:T(8,128)S(1)} %get-tuple-element.29), channel_id=1, source_target_pairs={{0,96},{1,97},{2,98},{3,99},{4,100},{5,101},{6,102},{7,103},{8,104... | collective-permute-start | bytes 1179656 | tf_op jit(solution)/shard_map/cond/branch_1_fun/ppermute | solution.py:226
  61.9 5.2 %collective-permute-start.4 = (bf16[6,256,256]{2,1,0:T(8,128)(2,1)S(1)}, bf16[6,256,256]{2,1,0:T(8,128)(2,1)S(1)}, u32[]{:S(2)}, u32[]{:S(2)}) collective-permute-start(bf16[6,256,256]{2,1,0:T(8,128)(2,1)S(1)} %get-tuple-element.51), channel_id=1, source_target_pairs={{0,16},{16,0},{1,17},{17,1},{2,18},{18,2},{3,19},{19,3},{4,20},{20... | collective-permute-start | bytes 2359304 | tf_op jit(solution)/shard_map/ppermute | solution.py:189
  67.8 5.7 %collective-permute-start.5 = (bf16[384,256]{1,0:T(8,128)(2,1)S(1)}, bf16[384,256]{1,0:T(8,128)(2,1)S(1)}, u32[]{:S(2)}, u32[]{:S(2)}) collective-permute-start(bf16[384,256]{1,0:T(8,128)(2,1)S(1)} %get-tuple-element.53), channel_id=1, source_target_pairs={{0,32},{1,33},{2,34},{3,35},{4,36},{5,37},{6,38},{7,39},{8,40},{9,... | collective-permute-start | bytes 589832 | tf_op jit(solution)/shard_map/ppermute | solution.py:226
  69.4 7.3 %collective-permute-start.6 = (bf16[384,256]{1,0:T(8,128)(2,1)S(1)}, bf16[384,256]{1,0:T(8,128)(2,1)S(1)}, u32[]{:S(2)}, u32[]{:S(2)}) collective-permute-start(bf16[384,256]{1,0:T(8,128)(2,1)S(1)} %get-tuple-element.54), channel_id=1, source_target_pairs={{0,64},{1,65},{2,66},{3,67},{4,68},{5,69},{6,70},{7,71},{8,72},{9,... | collective-permute-start | bytes 589832 | tf_op jit(solution)/shard_map/ppermute | solution.py:226
  70.5 7.8 %collective-permute-start.7 = (bf16[384,256]{1,0:T(8,128)(2,1)S(1)}, bf16[384,256]{1,0:T(8,128)(2,1)S(1)}, u32[]{:S(2)}, u32[]{:S(2)}) collective-permute-start(bf16[384,256]{1,0:T(8,128)(2,1)S(1)} %get-tuple-element.55), channel_id=1, source_target_pairs={{0,96},{1,97},{2,98},{3,99},{4,100},{5,101},{6,102},{7,103},{8,104... | collective-permute-start | bytes 589832 | tf_op jit(solution)/shard_map/ppermute | solution.py:226
  79.0 6.0 %collective-permute-start.10 = (f32[192,256]{1,0:T(8,128)S(1)}, f32[192,256]{1,0:T(8,128)S(1)}, u32[]{:S(2)}, u32[]{:S(2)}) collective-permute-start(f32[192,256]{1,0:T(8,128)S(1)} %get-tuple-element.59), channel_id=1, source_target_pairs={{0,12},{1,13},{2,14},{3,15},{4,0},{5,1},{6,2},{7,3},{8,4},{9,5},{1... | collective-permute-start | bytes 589832 | tf_op jit(solution)/shard_map/ppermute | solution.py:226
  81.8 9.8 %collective-permute-start.8 = (f32[192,256]{1,0:T(8,128)S(1)}, f32[192,256]{1,0:T(8,128)S(1)}, u32[]{:S(2)}, u32[]{:S(2)}) collective-permute-start(f32[192,256]{1,0:T(8,128)S(1)} %get-tuple-element.57), channel_id=1, source_target_pairs={{0,4},{1,5},{2,6},{3,7},{4,8},{5,9},{6,10},{7,11},{8,12},{9,13},{1... | collective-permute-start | bytes 589832 | tf_op jit(solution)/shard_map/ppermute | solution.py:226
  81.8 9.8 %collective-permute-start.9 = (f32[192,256]{1,0:T(8,128)S(1)}, f32[192,256]{1,0:T(8,128)S(1)}, u32[]{:S(2)}, u32[]{:S(2)}) collective-permute-start(f32[192,256]{1,0:T(8,128)S(1)} %get-tuple-element.58), channel_id=1, source_target_pairs={{0,8},{1,9},{2,10},{3,11},{4,12},{5,13},{6,14},{7,15},{8,0},{9,1},... | collective-permute-start | bytes 589832 | tf_op jit(solution)/shard_map/ppermute | solution.py:226
  91.6 9.1 %collective-permute-start.11 = (f32[192,256]{1,0:T(8,128)S(1)}, f32[192,256]{1,0:T(8,128)S(1)}, u32[]{:S(2)}, u32[]{:S(2)}) collective-permute-start(f32[192,256]{1,0:T(8,128)S(1)} %shard_map.68.refs_0_), channel_id=1, source_target_pairs={{0,1},{1,2},{2,3},{3,0},{4,5},{5,6},{6,7},{7,4},{8,9},{9,10},{10,1... | collective-permute-start | bytes 589832 | tf_op jit(solution)/shard_map/ppermute | solution.py:226
  92.5 8.2 %collective-permute-start.12 = (f32[192,256]{1,0:T(8,128)S(1)}, f32[192,256]{1,0:T(8,128)S(1)}, u32[]{:S(2)}, u32[]{:S(2)}) collective-permute-start(f32[192,256]{1,0:T(8,128)S(1)} %shard_map.68.refs_0_), channel_id=1, source_target_pairs={{0,2},{1,3},{2,0},{3,1},{4,6},{5,7},{6,4},{7,5},{8,10},{9,11},{10,... | collective-permute-start | bytes 589832 | tf_op jit(solution)/shard_map/ppermute | solution.py:226
  92.7 8.9 %collective-permute-start.13 = (f32[192,256]{1,0:T(8,128)S(1)}, f32[192,256]{1,0:T(8,128)S(1)}, u32[]{:S(2)}, u32[]{:S(2)}) collective-permute-start(f32[192,256]{1,0:T(8,128)S(1)} %shard_map.68.refs_0_), channel_id=1, source_target_pairs={{0,3},{1,0},{2,1},{3,2},{4,7},{5,4},{6,5},{7,6},{8,11},{9,8},{10,9... | collective-permute-start | bytes 589832 | tf_op jit(solution)/shard_map/ppermute | solution.py:226
  101.8 7.0 %collective-permute-start.14 = (bf16[192,256]{1,0:T(8,128)(2,1)S(1)}, bf16[192,256]{1,0:T(8,128)(2,1)S(1)}, u32[]{:S(2)}, u32[]{:S(2)}) collective-permute-start(bf16[192,256]{1,0:T(8,128)(2,1)S(1)} %shard_map.69.refs_0_), channel_id=1, source_target_pairs={{0,4},{1,5},{2,6},{3,7},{4,8},{5,9},{6,10},{7,11},{8,12},{9,13},{1... | collective-permute-start | bytes 294920 | tf_op jit(solution)/shard_map/ppermute | solution.py:226
  101.9 6.9 %collective-permute-start.15 = (bf16[192,256]{1,0:T(8,128)(2,1)S(1)}, bf16[192,256]{1,0:T(8,128)(2,1)S(1)}, u32[]{:S(2)}, u32[]{:S(2)}) collective-permute-start(bf16[192,256]{1,0:T(8,128)(2,1)S(1)} %shard_map.69.refs_0_), channel_id=1, source_target_pairs={{0,8},{1,9},{2,10},{3,11},{4,12},{5,13},{6,14},{7,15},{8,0},{9,1},... | collective-permute-start | bytes 294920 | tf_op jit(solution)/shard_map/ppermute | solution.py:226
  104.0 5.7 %collective-permute-start.16 = (bf16[192,256]{1,0:T(8,128)(2,1)S(1)}, bf16[192,256]{1,0:T(8,128)(2,1)S(1)}, u32[]{:S(2)}, u32[]{:S(2)}) collective-permute-start(bf16[192,256]{1,0:T(8,128)(2,1)S(1)} %shard_map.69.refs_0_), channel_id=1, source_target_pairs={{0,12},{1,13},{2,14},{3,15},{4,0},{5,1},{6,2},{7,3},{8,4},{9,5},{1... | collective-permute-start | bytes 294920 | tf_op jit(solution)/shard_map/ppermute | solution.py:226
  105.1 20.4 %copy-start.4 = (bf16[768,768]{1,0:T(8,128)(2,1)S(1)}, bf16[768,768]{1,0:T(8,128)(2,1)}, u32[]{:S(2)}) copy-start(bf16[768,768]{1,0:T(8,128)(2,1)} %refs_13_.1) | copy-start | bytes 3538948
  107.1 18.4 %copy-start.2 = (bf16[768,768]{1,0:T(8,128)(2,1)S(1)}, bf16[768,768]{1,0:T(8,128)(2,1)}, u32[]{:S(2)}) copy-start(bf16[768,768]{1,0:T(8,128)(2,1)} %refs_11_.1) | copy-start | bytes 3538948
  107.1 18.4 %copy-start.3 = (bf16[768,768]{1,0:T(8,128)(2,1)S(1)}, bf16[768,768]{1,0:T(8,128)(2,1)}, u32[]{:S(2)}) copy-start(bf16[768,768]{1,0:T(8,128)(2,1)} %refs_12_.1) | copy-start | bytes 3538948
  110.2 7.8 %collective-permute-start.17 = (bf16[2,384,256]{2,1,0:T(8,128)(2,1)S(1)}, bf16[2,384,256]{2,1,0:T(8,128)(2,1)S(1)}, u32[]{:S(2)}, u32[]{:S(2)}) collective-permute-start(bf16[2,384,256]{2,1,0:T(8,128)(2,1)S(1)} %shard_map.71.refs_0_), channel_id=1, source_target_pairs={{0,32},{1,33},{2,34},{3,35},{4,36},{5,37},{6,38},{7,39},{8,40},{9,... | collective-permute-start | bytes 1179656 | tf_op jit(solution)/shard_map/ppermute | solution.py:226
  111.2 9.4 %collective-permute-start.18 = (bf16[2,384,256]{2,1,0:T(8,128)(2,1)S(1)}, bf16[2,384,256]{2,1,0:T(8,128)(2,1)S(1)}, u32[]{:S(2)}, u32[]{:S(2)}) collective-permute-start(bf16[2,384,256]{2,1,0:T(8,128)(2,1)S(1)} %shard_map.71.refs_0_), channel_id=1, source_target_pairs={{0,64},{1,65},{2,66},{3,67},{4,68},{5,69},{6,70},{7,71},{8,72},{9,... | collective-permute-start | bytes 1179656 | tf_op jit(solution)/shard_map/ppermute | solution.py:226
  111.7 12.0 %collective-permute-start.19 = (bf16[2,384,256]{2,1,0:T(8,128)(2,1)S(1)}, bf16[2,384,256]{2,1,0:T(8,128)(2,1)S(1)}, u32[]{:S(2)}, u32[]{:S(2)}) collective-permute-start(bf16[2,384,256]{2,1,0:T(8,128)(2,1)S(1)} %shard_map.71.refs_0_), channel_id=1, source_target_pairs={{0,96},{1,97},{2,98},{3,99},{4,100},{5,101},{6,102},{7,103},{8,104... | collective-permute-start | bytes 1179656 | tf_op jit(solution)/shard_map/ppermute | solution.py:226
  113.7 10.1 %collective-permute-start.20 = (bf16[2,384,256]{2,1,0:T(8,128)(2,1)S(1)}, bf16[2,384,256]{2,1,0:T(8,128)(2,1)S(1)}, u32[]{:S(2)}, u32[]{:S(2)}) collective-permute-start(bf16[2,384,256]{2,1,0:T(8,128)(2,1)S(1)} %shard_map.71.refs_0_), channel_id=1, source_target_pairs={{0,16},{16,0},{1,17},{17,1},{2,18},{18,2},{3,19},{19,3},{4,20},{20... | collective-permute-start | bytes 1179656 | tf_op jit(solution)/shard_map/ppermute | solution.py:189
  118.1 5.7 %collective-permute-start.21 = (bf16[2,384,256]{2,1,0:T(8,128)(2,1)S(1)}, bf16[2,384,256]{2,1,0:T(8,128)(2,1)S(1)}, u32[]{:S(2)}, u32[]{:S(2)}) collective-permute-start(bf16[2,384,256]{2,1,0:T(8,128)(2,1)S(1)} %collective-permute-done.17.refs_1_), channel_id=1, source_target_pairs={{0,16},{16,0},{1,17},{17,1},{2,18},{18,2},{3,19},{19,3},{4,20},{20... | collective-permute-start | bytes 1179656 | tf_op jit(solution)/shard_map/ppermute | solution.py:189
  120.6 3.2 %collective-permute-start.22 = (bf16[2,384,256]{2,1,0:T(8,128)(2,1)S(1)}, bf16[2,384,256]{2,1,0:T(8,128)(2,1)S(1)}, u32[]{:S(2)}, u32[]{:S(2)}) collective-permute-start(bf16[2,384,256]{2,1,0:T(8,128)(2,1)S(1)} %collective-permute-done.18.refs_2_), channel_id=1, source_target_pairs={{0,16},{16,0},{1,17},{17,1},{2,18},{18,2},{3,19},{19,3},{4,20},{20... | collective-permute-start | bytes 1179656 | tf_op jit(solution)/shard_map/ppermute | solution.py:189
  123.8 1.7 %collective-permute-start.23 = (bf16[2,384,256]{2,1,0:T(8,128)(2,1)S(1)}, bf16[2,384,256]{2,1,0:T(8,128)(2,1)S(1)}, u32[]{:S(2)}, u32[]{:S(2)}) collective-permute-start(bf16[2,384,256]{2,1,0:T(8,128)(2,1)S(1)} %collective-permute-done.19.refs_3_), channel_id=1, source_target_pairs={{0,16},{16,0},{1,17},{17,1},{2,18},{18,2},{3,19},{19,3},{4,20},{20... | collective-permute-start | bytes 1179656 | tf_op jit(solution)/shard_map/ppermute | solution.py:189
